TPU v7x, 32 devices: a whole 2x2x4 slice. The times are simulated.
32 devices in a mesh: req: 8 (over z, x), tp: 4 (over y, core).
Axes of the slice: x: 2, y: 2, z: 4, core: 2. Of those that a mesh axis runs over, the one named last changes fastest.
Arguments:
- tokens: bfloat16 [6144, 2048], P('req'), may hold values from -6 to 6
- lengths: int32 [8, 8], P('req'), may hold values from 1 to 384, 768 in all within a row
- request_adapter: int32 [8, 8], P('req'), may hold values from 0 to 15
- w_qkv: bfloat16 [2048, 3, 2048], P('req', None, 'tp'), may hold values from -2 to 2
- w_out: bfloat16 [2048, 2048], P('tp', 'req'), may hold values from -0.125 to 0.125
- w_gate: bfloat16 [2048, 8192], P('req', 'tp'), may hold values from -0.125 to 0.125
- w_up: bfloat16 [2048, 8192], P('req', 'tp'), may hold values from -0.125 to 0.125
- w_down: bfloat16 [8192, 2048], P('tp', 'req'), may hold values from -0.0625 to 0.0625
- a_qkv: bfloat16 [2048, 256], replicated, may hold values from -0.125 to 0.125
- b_qkv: bfloat16 [256, 3, 2048], P(None, None, 'tp'), may hold values from -0.75 to 0.75
- a_out: bfloat16 [2048, 256], P('tp'), may hold values from -0.125 to 0.125
- b_out: bfloat16 [256, 2048], replicated, may hold values from -0.75 to 0.75
- a_gate: bfloat16 [2048, 256], replicated, may hold values from -0.125 to 0.125
- b_gate: bfloat16 [256, 8192], P(None, 'tp'), may hold values from -0.75 to 0.75
- a_up: bfloat16 [2048, 256], replicated, may hold values from -0.125 to 0.125
- b_up: bfloat16 [256, 8192], P(None, 'tp'), may hold values from -0.75 to 0.75
- a_down: bfloat16 [8192, 256], P('tp'), may hold values from -0.0625 to 0.0625
- b_down: bfloat16 [256, 2048], replicated, may hold values from -0.75 to 0.75
Outputs:
- layer_out: bfloat16 [6144, 2048], P('req')
Inputs may be any that keep to these rules, and one draw needn't show every extreme that they name: Each row of lengths sums to 768, so the requests of one index of req fill all its slots; each row's largest length is 384.
All inputs are finite; a program needn't handle non-finite values.
Results may differ from a plain program's by a relative error of at most 0.017.
Values may be sent and summed in bfloat16 or wider, within the bound.
No kernel may reach another device: no remote copies, remote signals or barrier semaphores. Data moves between devices by JAX's collectives and lax.ppermute only.
A program may use at most 128 MiB of HBM per device.

v0:
```python
import math

import jax
import jax.numpy as jnp
from jax import lax
from jax.sharding import PartitionSpec as P

HD = 128
RANK = 16


epsilon = 1e-05
rope_base = 10000.0


def layer_norm(values):
    row_mean = jnp.mean(values, axis=-1, keepdims=True)
    centred = values - row_mean
    spread = jnp.mean(centred * centred, axis=-1, keepdims=True)
    return (centred * lax.rsqrt(spread + epsilon)).astype(jnp.bfloat16)


def slot_layout(lengths_row, adapters_row, slot_count):
    request_ends = jnp.cumsum(lengths_row)
    request_starts = request_ends - lengths_row
    slot_index = jnp.arange(slot_count, dtype=jnp.int32)
    request_of = jnp.sum((slot_index[:, None] >= request_ends[None, :]).astype(jnp.int32), axis=1)
    member = request_of[:, None] == jnp.arange(lengths_row.shape[0], dtype=jnp.int32)[None, :]
    position = slot_index - jnp.sum(jnp.where(member, request_starts[None, :], 0), axis=1)
    adapter = jnp.sum(jnp.where(member, adapters_row[None, :], 0), axis=1)
    return (request_of, position, adapter)


def rotate(values, position):
    half_width = values.shape[-1] // 2
    frequency = jnp.exp(
        -math.log(rope_base) * 2.0 * jnp.arange(half_width, dtype=jnp.float32) / values.shape[-1]
    )
    angles = position.astype(jnp.float32)[:, None] * frequency[None, :]
    cosine = jnp.cos(angles)[:, None, :]
    sine_part = jnp.sin(angles)[:, None, :]
    lower_half = values[..., :half_width]
    upper_half = values[..., half_width:]
    return jnp.concatenate(
        [
            lower_half * cosine - upper_half * sine_part,
            upper_half * cosine + lower_half * sine_part,
        ],
        axis=-1,
    )


def low_rank(inner, b_matrix, select):
    masked = jnp.where(select, inner, jnp.float32(0.0)).astype(jnp.bfloat16)
    return jnp.dot(masked, b_matrix, preferred_element_type=jnp.float32)


def attend(query_rot, key_rot, value_part, request_of):
    slot_index = jnp.arange(query_rot.shape[0], dtype=jnp.int32)
    allowed = (request_of[:, None] == request_of[None, :]) & (
        slot_index[:, None] >= slot_index[None, :]
    )
    scores = jnp.einsum("qhd,khd->hqk", query_rot, key_rot, preferred_element_type=jnp.float32) * (
        1.0 / math.sqrt(HD)
    )
    scores = jnp.where(allowed[None], scores, jnp.float32(-1e30))
    top_score = jnp.max(scores, axis=-1, keepdims=True)
    expo = jnp.exp(scores - top_score)
    weights = (expo / jnp.sum(expo, axis=-1, keepdims=True)).astype(jnp.bfloat16)
    return jnp.einsum(
        "hqk,khd->qhd", weights, value_part, preferred_element_type=jnp.float32
    ).astype(jnp.bfloat16)


def body(
    tokens,
    lengths,
    request_adapter,
    w_qkv,
    w_out,
    w_gate,
    w_up,
    w_down,
    a_qkv,
    b_qkv,
    a_out,
    b_out,
    a_gate,
    b_gate,
    a_up,
    b_up,
    a_down,
    b_down,
):
    slot_count = tokens.shape[0]
    request_of, position, adapter = slot_layout(lengths[0], request_adapter[0], slot_count)
    select = adapter[:, None] == (jnp.arange(a_qkv.shape[1], dtype=jnp.int32) // RANK)[None, :]
    normed = layer_norm(tokens.astype(jnp.float32))
    local_width = w_qkv.shape[2]
    shard_piece = lax.all_gather(w_qkv, "req", axis=0, tiled=True)
    columns = normed
    joined_qkv = jnp.dot(
        columns,
        shard_piece.reshape(shard_piece.shape[0], 3 * local_width),
        preferred_element_type=jnp.float32,
    )
    joined_qkv = joined_qkv + low_rank(
        jnp.dot(normed, a_qkv, preferred_element_type=jnp.float32),
        b_qkv.reshape(b_qkv.shape[0], 3 * local_width),
        select,
    )
    joined_qkv = joined_qkv.reshape(slot_count, 3, local_width // HD, HD)
    query_rot = rotate(joined_qkv[:, 0], position).astype(jnp.bfloat16)
    key_rot = rotate(joined_qkv[:, 1], position).astype(jnp.bfloat16)
    value_part = joined_qkv[:, 2].astype(jnp.bfloat16)
    attn_flat = attend(query_rot, key_rot, value_part, request_of).reshape(slot_count, local_width)
    attn_part = jnp.dot(
        attn_flat,
        lax.all_gather(w_out, "req", axis=1, tiled=True),
        preferred_element_type=jnp.float32,
    )
    low_attn = jnp.dot(attn_flat, a_out, preferred_element_type=jnp.float32)
    attn_sum, low_sum = (
        lax.psum(attn_part.astype(jnp.bfloat16), "tp").astype(jnp.float32),
        lax.psum(low_attn.astype(jnp.bfloat16), "tp").astype(jnp.float32),
    )
    hidden_state = tokens.astype(jnp.float32) + attn_sum + low_rank(low_sum, b_out, select)
    normed2 = layer_norm(hidden_state)
    columns = normed2
    gate_proj = jnp.dot(
        columns,
        lax.all_gather(w_gate, "req", axis=0, tiled=True),
        preferred_element_type=jnp.float32,
    )
    up_proj = jnp.dot(
        columns, lax.all_gather(w_up, "req", axis=0, tiled=True), preferred_element_type=jnp.float32
    )
    gate_proj = gate_proj + low_rank(
        jnp.dot(normed2, a_gate, preferred_element_type=jnp.float32), b_gate, select
    )
    up_proj = up_proj + low_rank(
        jnp.dot(normed2, a_up, preferred_element_type=jnp.float32), b_up, select
    )
    hidden = (jax.nn.silu(gate_proj) * up_proj).astype(jnp.bfloat16)
    down_part = jnp.dot(
        hidden,
        lax.all_gather(w_down, "req", axis=1, tiled=True),
        preferred_element_type=jnp.float32,
    )
    low_down = jnp.dot(hidden, a_down, preferred_element_type=jnp.float32)
    down_sum, low_total = (
        lax.psum(down_part.astype(jnp.bfloat16), "tp").astype(jnp.float32),
        lax.psum(low_down.astype(jnp.bfloat16), "tp").astype(jnp.float32),
    )
    return (hidden_state + down_sum + low_rank(low_total, b_down, select)).astype(jnp.bfloat16)


def solution(mesh):
    in_specs = (
        P("req", None),
        P("req", None),
        P("req", None),
        P("req", None, "tp"),
        P("tp", "req"),
        P("req", "tp"),
        P("req", "tp"),
        P("tp", "req"),
        P(),
        P(None, None, "tp"),
        P("tp", None),
        P(),
        P(),
        P(None, "tp"),
        P(),
        P(None, "tp"),
        P("tp", None),
        P(),
    )
    out_specs = P("req", None)
    return jax.shard_map(body, mesh=mesh, in_specs=in_specs, out_specs=out_specs, check_vma=False)
```

profile of v0, /device:TPU:0, one launch (start us, length us, event | category | flops | bytes accessed | tf_op | source)
XLA Modules:
  0.0 718.2 jit_solution(6395015582493481590)
XLA Ops:
  6.5 2.4 copy.29
  12.8 2.4 convert_reduce_fusion
  18.0 94.1 %all-gather.6.cloned.1.call-done = bf16[2048,3,512]{0,2,1:T(8,128)(2,1)} async-done(((bf16[256,3,512]{0,2,1:T(8,128)(2,1)}), bf16[2048,3,512]{0,2,1:T(8,128)(2,1)}) %all-gather.6.cloned.1.call-update) | async-done | bytes 6291472 | tf_op jit(solution)/shard_map/all_gather | solution.py:100
  112.1 9.7 %fusion.55 = f32[768,1536]{1,0:T(8,128)} fusion(bf16[2048,1536]{0,1:T(8,128)(2,1)} %bitcast.47, bf16[768,2048]{1,0:T(8,128)(2,1)} %param.18, f32[768]{0:T(1024)S(1)} %add_rsqrt_fusion.1, f32[768]{0:T(1024)S(1)} %broadcast_multiply_fusion.1), kind=kOutput, calls=%fused_computation.95 | convolution fusion | flops 4838129664 | bytes 14161920 | tf_op jit(solution)/shard_map/dot_general | solution.py:102
  121.8 8.6 %convolution_add_fusion = f32[768,1536]{1,0:T(8,128)} fusion(f32[768,1536]{1,0:T(8,128)} %fusion.55, bf16[256,1536]{0,1:T(8,128)(2,1)S(1)} %bitcast.44, bf16[2048,256]{1,0:T(8,128)(2,1)} %param.26, s32[256]{0:T(256)S(1)} %and_select_fusion, s32[768]{0:T(1024)S(1)} %get-tuple-element.6, bf16[768,2048]{1,0:T(8,128)(2,1)} %param.18, ...), kind=kOutput, calls=%fused_computation.21 | convolution fusion | flops 1417347072 | bytes 14428160 | tf_op jit(solution)/shard_map/dot_general | solution.py:55
  130.4 6.2 reshape.164
  144.3 9.1 %fusion.58 = (f32[4,768]{1,0:T(4,128)S(1)}, f32[4,768,768]{1,2,0:T(8,128)}) fusion(pred[768,768]{0,1:T(8,128)(4,1)} %fusion.13, bf16[768,4,64]{2,0,1:T(8,128)(2,1)} %get-tuple-element.17, bf16[768,4,64]{2,0,1:T(8,128)(2,1)} %get-tuple-element.18, bf16[768,4,64]{2,0,1:T(8,128)(2,1)S(1)} %get-tuple-element.14, bf16[768,4,64]{2,0,1:T(8,128)(2,1)S(1)} %get-tuple-element.13), kind=kOutput, calls=%fused_computation.97 | convolution fusion | flops 616563456 | bytes 11612160 | tf_op jit(solution)/shard_map/sub | solution.py:68
  153.4 4.6 fusion.14
  159.2 4.2 all-gather.8.cloned.1.call-done
  163.4 5.1 convolution_convert_fusion.1
  170.3 71.6 %all-reduce.7.cloned.1.call-done = (bf16[768,2048]{1,0:T(8,128)(2,1)}, bf16[768,256]{1,0:T(8,128)(2,1)}) async-done(((bf16[768,2048]{1,0:T(8,128)(2,1)}, bf16[768,256]{1,0:T(8,128)(2,1)}), (bf16[768,2048]{1,0:T(8,128)(2,1)}, bf16[768,256]{1,0:T(8,128)(2,1)})) %all-reduce.7.cloned.1.call-update) | async-done | bytes 3538960 | tf_op jit(solution)/shard_map/psum | solution.py:124
  241.9 4.4 fusion.59
  249.0 2.3 multiply_convert_fusion.1
  251.3 8.2 %fusion.17 = f32[768,2048]{1,0:T(8,128)} fusion(bf16[256,2048]{1,0:T(8,128)(2,1)S(1)} %copy-done.4, bf16[768,2048]{1,0:T(8,128)(2,1)} %multiply_convert_fusion.1, bf16[2048,256]{1,0:T(8,128)(2,1)S(1)} %copy-done.5, s32[256]{0:T(256)S(1)} %and_select_fusion, s32[768]{0:T(1024)S(1)} %get-tuple-element.6), kind=kOutput, calls=%fused_computation.41 | convolution fusion | flops 1611202560 | bytes 11538432 | tf_op jit(solution)/shard_map/dot_general | solution.py:55
  259.5 109.4 %all-gather.12.cloned.1.call-done = bf16[2048,2048]{1,0:T(8,128)(2,1)} async-done(((bf16[256,2048]{1,0:T(8,128)(2,1)}), bf16[2048,2048]{1,0:T(8,128)(2,1)}) %all-gather.12.cloned.1.call-update) | async-done | bytes 8388624 | tf_op jit(solution)/shard_map/all_gather | solution.py:136
  368.9 11.9 %fusion.61 = f32[768,2048]{1,0:T(8,128)} fusion(bf16[768,2048]{1,0:T(8,128)(2,1)} %multiply_convert_fusion.1, bf16[2048,2048]{1,0:T(8,128)(2,1)} %all-gather.12.cloned.1.call-done), kind=kOutput, calls=%fused_computation.100 | convolution fusion | flops 6442450944 | bytes 17825792 | tf_op jit(solution)/shard_map/dot_general | solution.py:135
  380.7 113.2 %all-gather.10.cloned.1.call-done = bf16[2048,2048]{1,0:T(8,128)(2,1)} async-done(((bf16[256,2048]{1,0:T(8,128)(2,1)}), bf16[2048,2048]{1,0:T(8,128)(2,1)}) %all-gather.10.cloned.1.call-update) | async-done | bytes 8388624 | tf_op jit(solution)/shard_map/all_gather | solution.py:132
  494.0 11.7 %fusion.60 = f32[768,2048]{1,0:T(8,128)} fusion(bf16[768,2048]{1,0:T(8,128)(2,1)} %multiply_convert_fusion.1, bf16[2048,2048]{1,0:T(8,128)(2,1)} %all-gather.10.cloned.1.call-done), kind=kOutput, calls=%fused_computation.99 | convolution fusion | flops 6442450944 | bytes 17825792 | tf_op jit(solution)/shard_map/dot_general | solution.py:130
  505.7 12.1 %multiply_convert_fusion = bf16[768,2048]{1,0:T(8,128)(2,1)} fusion(f32[768,2048]{1,0:T(8,128)} %fusion.61, f32[768,2048]{1,0:T(8,128)} %fusion.60, f32[768,2048]{1,0:T(8,128)} %fusion.17, bf16[256,2048]{1,0:T(8,128)(2,1)S(1)} %copy-done.10, bf16[768,2048]{1,0:T(8,128)(2,1)} %multiply_convert_fusion.1, bf16[2048,256]{1,0:T(8,128)(2,1)S(1)} %copy-done.11, ...), kind=kOutput, calls=%fused_computation.14 | convolution fusion | flops 1623785472 | bytes 27267072 | tf_op jit(solution)/shard_map/dot_general | solution.py:55
  517.9 3.7 convolution_convert_fusion.2
  521.5 98.0 %all-gather.14.cloned.1.call-done = bf16[2048,2048]{1,0:T(8,128)(2,1)} async-done(((bf16[2048,256]{1,0:T(8,128)(2,1)}), bf16[2048,2048]{1,0:T(8,128)(2,1)}) %all-gather.14.cloned.1.call-update) | async-done | bytes 8388624 | tf_op jit(solution)/shard_map/all_gather | solution.py:147
  619.5 11.8 %convolution_convert_fusion = bf16[768,2048]{1,0:T(8,128)(2,1)} fusion(bf16[768,2048]{1,0:T(8,128)(2,1)} %multiply_convert_fusion, bf16[2048,2048]{1,0:T(8,128)(2,1)} %all-gather.14.cloned.1.call-done), kind=kOutput, calls=%fused_computation.23 | convolution fusion | flops 6444023808 | bytes 14680064 | tf_op jit(solution)/shard_map/dot_general | solution.py:145
  631.4 73.4 %all-reduce.5.cloned.1.call-done = (bf16[768,2048]{1,0:T(8,128)(2,1)}, bf16[768,256]{1,0:T(8,128)(2,1)}) async-done(((bf16[768,2048]{1,0:T(8,128)(2,1)}, bf16[768,256]{1,0:T(8,128)(2,1)}), (bf16[768,2048]{1,0:T(8,128)(2,1)}, bf16[768,256]{1,0:T(8,128)(2,1)})) %all-reduce.5.cloned.1.call-update) | async-done | bytes 3538960 | tf_op jit(solution)/shard_map/psum | solution.py:152
  704.7 6.6 add_convert_fusion
  (64 shorter events, 19.8 us)
Async XLA Ops:
  6.5 235.3 %copy-start = (bf16[256,2048]{1,0:T(8,128)(2,1)S(1)}, bf16[256,2048]{1,0:T(8,128)(2,1)}, u32[]{:S(2)}) copy-start(bf16[256,2048]{1,0:T(8,128)(2,1)} %param.29) | copy-start | bytes 3145732
  6.5 9.6 %copy-start.7 = (bf16[256,3,512]{2,0,1:T(8,128)(2,1)S(1)}, bf16[256,3,512]{2,0,1:T(8,128)(2,1)}, u32[]{:S(2)}) copy-start(bf16[256,3,512]{2,0,1:T(8,128)(2,1)} %param.27) | copy-start | bytes 2359300
  6.5 105.5 %all-gather.6.cloned.1.call-start = ((), (), s32[]{:S(2)}) async-start(), calls=%async_computation | async-start | bytes 7077888 | tf_op jit(solution)/shard_map/all_gather | solution.py:100
  9.0 7.4 %copy-start.9 = (s32[1,8]{1,0:T(1,128)S(1)}, s32[1,8]{1,0:T(1,128)}, u32[]{:S(2)}) copy-start(s32[1,8]{1,0:T(1,128)} %param.20) | copy-start | bytes 100
  9.0 154.4 %all-gather.8.cloned.1.call-start = ((), (), s32[]{:S(2)}) async-start(), calls=%async_computation.1 | async-start | bytes 2359296 | tf_op jit(solution)/shard_map/all_gather | solution.py:119
  9.7 232.1 %all-reduce.7.cloned.1.call-start = ((), (), s32[]{:S(2)}) async-start(), calls=%async_computation.6 | async-start | bytes 7077888 | tf_op jit(solution)/shard_map/psum | solution.py:124
  10.6 4.5 copy-start.3
  144.3 9.2 %copy-start.8 = (bf16[768,1,4,128]{0,3,2,1:T(8,128)(2,1)S(1)}, bf16[768,1,4,128]{0,3,2,1:T(8,128)(2,1)}, u32[]{:S(2)}) copy-start(bf16[768,1,4,128]{0,3,2,1:T(8,128)(2,1)} %copy.38) | copy-start | bytes 2359300
  153.4 4.6 copy-start.13
  168.5 200.3 %all-gather.12.cloned.1.call-start = ((), (), s32[]{:S(2)}) async-start(), calls=%async_computation.3 | async-start | bytes 9437184 | tf_op jit(solution)/shard_map/all_gather | solution.py:136
  169.1 324.9 %all-gather.10.cloned.1.call-start = ((), (), s32[]{:S(2)}) async-start(), calls=%async_computation.2 | async-start | bytes 9437184 | tf_op jit(solution)/shard_map/all_gather | solution.py:132
  169.7 449.8 %all-gather.14.cloned.1.call-start = ((), (), s32[]{:S(2)}) async-start(), calls=%async_computation.4 | async-start | bytes 9437184 | tf_op jit(solution)/shard_map/all_gather | solution.py:147
  170.3 534.5 %all-reduce.5.cloned.1.call-start = ((), (), s32[]{:S(2)}) async-start(), calls=%async_computation.5 | async-start | bytes 7077888 | tf_op jit(solution)/shard_map/psum | solution.py:152
  246.3 2.7 copy-start.2
  249.0 2.3 copy-start.4
  249.0 2.3 copy-start.5
  380.7 125.0 %copy-start.10 = (bf16[256,2048]{1,0:T(8,128)(2,1)S(1)}, bf16[256,2048]{1,0:T(8,128)(2,1)}, u32[]{:S(2)}) copy-start(bf16[256,2048]{1,0:T(8,128)(2,1)} %param.33) | copy-start | bytes 3145732
  380.7 125.0 %copy-start.11 = (bf16[2048,256]{1,0:T(8,128)(2,1)S(1)}, bf16[2048,256]{1,0:T(8,128)(2,1)}, u32[]{:S(2)}) copy-start(bf16[2048,256]{1,0:T(8,128)(2,1)} %param.32) | copy-start | bytes 3145732
  505.7 12.1 %copy-start.12 = (bf16[2048,256]{1,0:T(8,128)(2,1)S(1)}, bf16[2048,256]{1,0:T(8,128)(2,1)}, u32[]{:S(2)}) copy-start(bf16[2048,256]{1,0:T(8,128)(2,1)} %param.34) | copy-start | bytes 3145732
  521.5 183.2 %copy-start.6 = (bf16[256,2048]{1,0:T(8,128)(2,1)S(1)}, bf16[256,2048]{1,0:T(8,128)(2,1)}, u32[]{:S(2)}) copy-start(bf16[256,2048]{1,0:T(8,128)(2,1)} %param.35) | copy-start | bytes 3145732
  704.7 6.6 copy-start.1
Sparse Core Ops, SparseCore 0:
  9.4 102.6 all-gather.5
  114.1 49.2 all-gather.7
  168.6 73.1 all-reduce.6
  243.9 124.9 all-gather.11
  370.8 123.1 all-gather.9
  495.9 123.5 all-gather.13
  631.5 73.2 all-reduce.4
where the time goes:
time: 719 us; the launch traced here: 718 us
  waiting for transfers between devices  566 us (79%)
  matrix products  109 us (15%)
  local copies, waits for them, and re-layouts  16.2 us (2%)
  between operations  13.6 us (2%)
  other arithmetic  13.2 us (2%)
    all_gather x1, waiting for transfers between devices, body(): lax.all_gather(w_gate, 'req', axis=0, tiled=True)  113 us
    all_gather x1, waiting for transfers between devices, body(): lax.all_gather(w_up, 'req', axis=0, tiled=True)  109 us
    all_gather x1, waiting for transfers between devices, body(): lax.all_gather(w_down, 'req', axis=1, tiled=True)  98 us
    all_gather x1, waiting for transfers between devices, body(): shard_piece = lax.all_gather(w_qkv, 'req', axis=0, tiled=True)  94.1 us
    psum x1, waiting for transfers between devices, body(): lax.psum(down_part.astype(jnp.bfloat16), 'tp').astype(jnp.float32)  73.4 us
    psum x1, waiting for transfers between devices, body(): lax.psum(attn_part.astype(jnp.bfloat16), 'tp').astype(jnp.float32)  71.6 us
    dot_general x5, matrix products, low_rank(): return jnp.dot(masked, b_matrix, preferred_element_type=jnp.float32)  40 us
  transfers between devices with their start and end apart: 7, of which 7 were waited for; matrix products, arithmetic and copies ran while one was open for 15% of the time, Pallas kernels for 0%

commit v1 on v0

v1 whole, which is shorter than its diff:
```python
import math

import jax
import jax.numpy as jnp
from jax import lax
from jax.sharding import PartitionSpec as P

HD = 128
RANK = 16
AXES = ("req", "tp")
epsilon = 1e-05
rope_base = 10000.0
F32 = jnp.float32
BF16 = jnp.bfloat16


def layer_norm(values):
    row_mean = jnp.mean(values, axis=-1, keepdims=True)
    centred = values - row_mean
    spread = jnp.mean(centred * centred, axis=-1, keepdims=True)
    return (centred * lax.rsqrt(spread + epsilon)).astype(BF16)


def slot_layout(lengths_row, adapters_row, slot_count):
    request_ends = jnp.cumsum(lengths_row)
    request_starts = request_ends - lengths_row
    slot_index = jnp.arange(slot_count, dtype=jnp.int32)
    request_of = jnp.sum((slot_index[:, None] >= request_ends[None, :]).astype(jnp.int32), axis=1)
    member = request_of[:, None] == jnp.arange(lengths_row.shape[0], dtype=jnp.int32)[None, :]
    position = slot_index - jnp.sum(jnp.where(member, request_starts[None, :], 0), axis=1)
    adapter = jnp.sum(jnp.where(member, adapters_row[None, :], 0), axis=1)
    return (request_of, position, adapter)


def rotate(values, position):
    half_width = values.shape[-1] // 2
    frequency = jnp.exp(
        -math.log(rope_base) * 2.0 * jnp.arange(half_width, dtype=F32) / values.shape[-1]
    )
    angles = position.astype(F32)[:, None] * frequency[None, :]
    cosine = jnp.cos(angles)[:, None, :]
    sine_part = jnp.sin(angles)[:, None, :]
    lower_half = values[..., :half_width]
    upper_half = values[..., half_width:]
    return jnp.concatenate(
        [
            lower_half * cosine - upper_half * sine_part,
            upper_half * cosine + lower_half * sine_part,
        ],
        axis=-1,
    )


def dot(a, b):
    return jnp.dot(a, b, preferred_element_type=F32)


def attend(query_rot, key_rot, value_part, request_of):
    slot_index = jnp.arange(query_rot.shape[0], dtype=jnp.int32)
    allowed = (request_of[:, None] == request_of[None, :]) & (
        slot_index[:, None] >= slot_index[None, :]
    )
    scores = jnp.einsum("qhd,khd->hqk", query_rot, key_rot, preferred_element_type=F32) * (
        1.0 / math.sqrt(HD)
    )
    scores = jnp.where(allowed[None], scores, F32(-1e30))
    top_score = jnp.max(scores, axis=-1, keepdims=True)
    expo = jnp.exp(scores - top_score)
    weights = (expo / jnp.sum(expo, axis=-1, keepdims=True)).astype(BF16)
    return jnp.einsum("hqk,khd->qhd", weights, value_part, preferred_element_type=F32).astype(BF16)


def make_body(R, T):
    Z, ZH, Y = R // 2, R // 4, T // 2

    def move(f):
        pairs = []
        for r in range(R):
            for t in range(T):
                z, x, y, c = f(r // 2, r % 2, t // 2, t % 2)
                pairs.append((r * T + t, (z * 2 + x) * T + y * 2 + c))
        return pairs

    def send(value, pairs):
        return lax.ppermute(value, AXES, pairs)

    to_core = move(lambda z, x, y, c: (z, x, y, 1 - c))
    to_x = move(lambda z, x, y, c: (z, 1 - x, y, c))
    to_xz = {
        (i, j): move(lambda z, x, y, c: (z ^ j, x ^ i, y, c)) for i in (0, 1) for j in (0, 1)
    }
    z_up = move(lambda z, x, y, c: ((z + 1) % Z, x, y, c))
    z_down = move(lambda z, x, y, c: ((z - 1) % Z, x, y, c))
    from_y = {k: move(lambda z, x, y, c: (z, x, (y - k) % Y, c)) for k in range(1, Y)}
    from_zh = {
        k: move(lambda z, x, y, c: ((z - 2 * k) % Z, x, y, c)) for k in range(1, ZH)
    }

    def ring(halves):
        got = {0: halves}
        left, right = halves, halves
        for k in range(1, Z // 2):
            left = [send(h, z_up) for h in left]
            right = [send(h, z_down) for h in right]
            got[Z - k], got[k] = left, right
        got[Z // 2] = [send(left[0], z_up), send(right[1], z_down)]
        return got

    def body(
        tokens, lengths, request_adapter, w_qkv, w_out, w_gate, w_up, w_down,
        a_qkv, b_qkv, a_out, b_out, a_gate, b_gate, a_up, b_up, a_down, b_down,
    ):
        r, t = lax.axis_index("req"), lax.axis_index("tp")
        z, x, y, c = r // 2, r % 2, t // 2, t % 2
        zh, zl = z // 2, z % 2
        slots, width = tokens.shape
        piece = slots // T
        block = width // R
        local = w_qkv.shape[2]
        rank_all = a_qkv.shape[1]
        quarter = w_gate.shape[1] // 4
        span = width // ZH

        def cut(array, start, size, axis):
            return lax.dynamic_slice_in_dim(array, start, size, axis)

        own_qkv = w_qkv.reshape(block, 3 * local)
        got = ring([own_qkv[: block // 2], own_qkv[block // 2 :]])
        qkv_blocks = []
        for k in range(Z):
            here = jnp.concatenate(got[k], axis=0)
            qkv_blocks += [here, send(here, to_x)]
        w_qkv_all = jnp.concatenate(qkv_blocks, axis=0)
        got = ring([w_out[: local // 2], w_out[local // 2 :]])
        out_blocks = []
        for k in range(Z):
            here = jnp.concatenate(got[k], axis=0)
            out_blocks += [here, send(here, to_x)]
        w_out_all = jnp.concatenate(out_blocks, axis=1)
        order = [((z + k) % Z) * 2 + (x ^ i) for k in range(Z) for i in (0, 1)]

        def scatter(parts, axis, join):
            pieces = {}
            for i in (0, 1):
                for j in (0, 1):
                    at = ((zl ^ j) * 2 + (x ^ i)) * quarter
                    p = jnp.concatenate([cut(w, at, quarter, axis) for w in parts], axis=axis)
                    pieces[(i, j)] = p if i == j == 0 else send(p, to_xz[(i, j)])
            stacked = jnp.stack([pieces[(i, j)] for j in (0, 1) for i in (0, 1)])
            me = zl * 2 + x
            return jnp.concatenate(
                [lax.dynamic_index_in_dim(stacked, me ^ b, 0, keepdims=False) for b in range(4)],
                axis=join,
            )

        mine = (zl * 2 + x) * quarter
        gu_own = scatter([w_gate, w_up], 1, 0)
        down_own = scatter([w_down], 0, 1)
        b_own = jnp.concatenate(
            [cut(b_gate, mine, quarter, 1), cut(b_up, mine, quarter, 1)], axis=1
        )
        a_down_own = cut(a_down, mine, quarter, 0)
        gu, down, b_gu, a_dn = {(0, 0): gu_own}, {(0, 0): down_own}, [b_own], [a_down_own]
        for k in range(1, ZH):
            gu[(k, 0)] = send(gu_own, from_zh[k])
            down[(k, 0)] = send(down_own, from_zh[k])
        for k in range(1, Y):
            both = send(jnp.concatenate([gu_own, b_own], axis=0), from_y[k])
            gu[(0, k)] = both[: gu_own.shape[0]]
            b_gu.append(both[gu_own.shape[0] :])
            both = send(jnp.concatenate([down_own, a_down_own], axis=1), from_y[k])
            down[(0, k)] = both[:, : down_own.shape[1]]
            a_dn.append(both[:, down_own.shape[1] :])
            for h in range(1, ZH):
                gu[(h, k)] = send(gu[(h, 0)], from_y[k])
                down[(h, k)] = send(down[(h, 0)], from_y[k])

        request_of, position, adapter = slot_layout(lengths[0], request_adapter[0], slots)
        column_adapter = jnp.arange(rank_all, dtype=jnp.int32) // RANK

        def masked(inner, adapter_rows):
            chosen = adapter_rows[:, None] == column_adapter[None, :]
            return jnp.where(chosen, inner, F32(0.0)).astype(BF16)

        normed = layer_norm(tokens.astype(F32))
        normed_rel = jnp.concatenate([cut(normed, b * block, block, 1) for b in order], axis=1)
        low = masked(dot(normed, a_qkv), adapter)
        joined = dot(normed_rel, w_qkv_all) + dot(low, b_qkv.reshape(rank_all, 3 * local))
        joined = joined.reshape(slots, 3, local // HD, HD)
        query_rot = rotate(joined[:, 0], position).astype(BF16)
        key_rot = rotate(joined[:, 1], position).astype(BF16)
        attn = attend(query_rot, key_rot, joined[:, 2].astype(BF16), request_of)
        attn = attn.reshape(slots, local)
        low = masked(dot(attn, a_out), adapter)
        b_out_rel = jnp.concatenate([cut(b_out, b * block, block, 1) for b in order], axis=1)
        part = (dot(attn, w_out_all) + dot(low, b_out_rel)).astype(BF16)
        part = part.reshape(Y, 2, piece, width)
        keep = lax.dynamic_index_in_dim(part, c, 1, keepdims=False)
        give = lax.dynamic_index_in_dim(part, 1 - c, 1, keepdims=False)
        pair = (keep.astype(F32) + send(give, to_core).astype(F32)).astype(BF16)
        total = lax.dynamic_index_in_dim(pair, y, 0, keepdims=False).astype(F32)
        for k in range(1, Y):
            p = lax.dynamic_index_in_dim(pair, (y - k) % Y, 0, keepdims=False)
            total = total + send(p, from_y[k]).astype(F32)
        back = [((b // 2 - z) % Z) * 2 + ((b % 2) ^ x) for b in range(R)]
        total = jnp.concatenate([cut(total, b * block, block, 1) for b in back], axis=1)
        hidden_state = cut(tokens, t * piece, piece, 0).astype(F32) + total
        normed2 = layer_norm(hidden_state)

        others = [(1, 0), (0, 1), (1, 1)]
        rows = jnp.concatenate([normed2] + [send(normed2, to_xz[o]) for o in others], axis=0)
        rows = jnp.concatenate([rows, send(rows, to_core)], axis=0)
        adapters = jnp.stack([adapter] + [send(adapter, to_xz[o]) for o in others])
        adapters = jnp.concatenate(
            [cut(adapters, (y * 2 + (c ^ s)) * piece, piece, 1).reshape(-1) for s in (0, 1)]
        )
        low_gate = masked(dot(rows, a_gate), adapters)
        low_up = masked(dot(rows, a_up), adapters)
        hidden = []
        columns = [cut(rows, ((zh + k) % ZH) * span, span, 1) for k in range(ZH)]
        for k in range(Y):
            gate_proj = dot(low_gate, b_gu[k][:, :quarter])
            up_proj = dot(low_up, b_gu[k][:, quarter:])
            for h in range(ZH):
                gate_proj = gate_proj + dot(columns[h], gu[(h, k)][:, :quarter])
                up_proj = up_proj + dot(columns[h], gu[(h, k)][:, quarter:])
            hidden.append((jax.nn.silu(gate_proj) * up_proj).astype(BF16))
        low_down = dot(hidden[0], a_dn[0])
        for k in range(1, Y):
            low_down = low_down + dot(hidden[k], a_dn[k])
        low_down = masked(low_down, adapters)
        out = jnp.zeros((slots, width), BF16)
        for h in range(ZH):
            at = ((zh + h) % ZH) * span
            part = dot(low_down, cut(b_down, at, span, 1))
            for k in range(Y):
                part = part + dot(hidden[k], down[(h, k)])
            part = part.astype(BF16)
            half = part.shape[0] // 2
            pair = part[:half].astype(F32) + send(part[half:], to_core).astype(F32)
            total = cut(hidden_state, at, span, 1) + pair[:piece]
            pair = pair.astype(BF16)
            for n, o in enumerate(others):
                total = total + send(pair[(n + 1) * piece : (n + 2) * piece], to_xz[o]).astype(F32)
            done = total.astype(BF16)
            held = {0: done}
            for k in range(1, Y):
                held[k] = send(done, from_y[k])
            for k in range(Y):
                there = send(held[k], to_core)
                row = ((y + k) % Y) * 2 * piece
                out = lax.dynamic_update_slice(out, held[k], (row + c * piece, at))
                out = lax.dynamic_update_slice(out, there, (row + (1 - c) * piece, at))
        return out

    return body


def solution(mesh):
    in_specs = (
        P("req", None),
        P("req", None),
        P("req", None),
        P("req", None, "tp"),
        P("tp", "req"),
        P("req", "tp"),
        P("req", "tp"),
        P("tp", "req"),
        P(),
        P(None, None, "tp"),
        P("tp", None),
        P(),
        P(),
        P(None, "tp"),
        P(),
        P(None, "tp"),
        P("tp", None),
        P(),
    )
    return jax.shard_map(
        make_body(mesh.shape["req"], mesh.shape["tp"]),
        mesh=mesh, in_specs=in_specs, out_specs=P("req", None), check_vma=False,
    )
```

time: 719 us -> 672 us (0.935); the launches traced: 718 us -> 663 us
  waiting for transfers between devices: 566 us -> 329 us
  local copies, waits for them, and re-layouts: 16.2 us -> 126 us
  starting transfers between devices: 0.24 us -> 65.9 us
  other arithmetic: 13.2 us -> 49.4 us
  matrix products: 109 us -> 90.9 us
  between operations: 13.6 us -> 1.11 us
    all_gather x5 -> x0, waiting for transfers between devices: 419 us -> none  [the longest x1 113 us: body(): lax.all_gather(w_gate, 'req', axis=0, tiled=True)]
    ppermute x0 -> x55, waiting for transfers between devices: none -> 329 us  [send(): return lax.ppermute(value, AXES, pairs)]
    psum x2 -> x0, waiting for transfers between devices: 145 us -> none  [the longest x1 73.4 us: body(): lax.psum(down_part.astype(jnp.bfloat16), 'tp').astype(jnp.float32)]
    ppermute x0 -> x55, starting transfers between devices: none -> 65.9 us  [send(): return lax.ppermute(value, AXES, pairs)]
    unnamed x31 -> x117, local copies, waits for them, and re-layouts: 5.94 us -> 60.6 us
    dynamic_update_slice x0 -> x6, local copies, waits for them, and re-layouts: none -> 30.3 us  [the longest x4 19.7 us: body(): out = lax.dynamic_update_slice(out, there, (row + (1 - c) * piece, at))]
    dot_general x13 -> x27, matrix products: 99.6 us -> 82 us  [the longest x26 77.2 us: dot(): return jnp.dot(a, b, preferred_element_type=F32)]
    concatenate x0 -> x15, other arithmetic: none -> 12.4 us  [the longest x1 3.04 us: body(): jnp.concatenate([normed2] + [send(normed2, to_xz[o]) for o in others], ax...]
  transfers between devices with their start and end apart: 7 -> 55, of which waited for: 7 -> 24; matrix products, arithmetic and copies ran while one was open for 15% -> 30% of each run, Pallas kernels for 0% -> 0%
where the time goes in v1:
time: 672 us; the launch traced here: 663 us
  waiting for transfers between devices  329 us (49%)
  local copies, waits for them, and re-layouts  126 us (19%)
  matrix products  90.9 us (14%)
  starting transfers between devices  65.9 us (10%)
  other arithmetic  49.4 us (7%)
    ppermute x55, waiting for transfers between devices, send(): return lax.ppermute(value, AXES, pairs)  329 us
    dot_general x26, matrix products, dot(): return jnp.dot(a, b, preferred_element_type=F32)  77.2 us
    ppermute x55, starting transfers between devices, send(): return lax.ppermute(value, AXES, pairs)  65.9 us
    unnamed x117, local copies, waits for them, and re-layouts  60.6 us
    dynamic_update_slice x4, local copies, waits for them, and re-layouts, body(): out = lax.dynamic_update_slice(out, there, (row + (1 - c) * piece, at))  19.7 us
  transfers between devices with their start and end apart: 55, of which 24 were waited for; matrix products, arithmetic and copies ran while one was open for 30% of the time, Pallas kernels for 0%

profile of v1, /device:TPU:0, one launch (start us, length us, event | category | flops | bytes accessed | tf_op | source)
XLA Modules:
  0.0 662.6 jit_solution(17766375804953624093)
XLA Ops:
  56.5 7.0 %fusion.34 = f32[768,1536]{1,0:T(8,128)} fusion(bf16[256,1536]{0,1:T(8,128)(2,1)S(1)} %bitcast.109, bf16[768,2048]{1,0:T(8,128)(2,1)} %fusion.5, bf16[2048,256]{1,0:T(8,128)(2,1)} %param.26, s32[256]{0:T(256)S(1)} %and_select_fusion, s32[768]{0:T(1024)S(1)} %get-tuple-element.6), kind=kOutput, calls=%fused_computation.72 | convolution fusion | flops 1409875968 | bytes 9703424 | tf_op jit(solution)/shard_map/dot_general | solution.py:55
  80.3 10.6 %collective-permute-done.15 = bf16[256,256]{1,0:T(8,128)(2,1)S(1)} collective-permute-done((bf16[256,256]{1,0:T(8,128)(2,1)S(1)}, bf16[256,256]{1,0:T(8,128)(2,1)S(1)}, u32[]{:S(2)}, u32[]{:S(2)}) %collective-permute-start.15) | collective-permute-done | bytes 131104 | tf_op jit(solution)/shard_map/ppermute | solution.py:85
  105.2 6.1 collective-permute-done.8
  111.4 16.0 %collective-permute-done.17 = bf16[512,256]{1,0:T(8,128)(2,1)S(1)} collective-permute-done((bf16[512,256]{1,0:T(8,128)(2,1)S(1)}, bf16[512,256]{1,0:T(8,128)(2,1)S(1)}, u32[]{:S(2)}, u32[]{:S(2)}) %collective-permute-start.17) | collective-permute-done | bytes 262176 | tf_op jit(solution)/shard_map/ppermute | solution.py:85
  139.0 5.3 collective-permute-done.3
  147.0 29.4 %collective-permute-done.7 = bf16[256,1536]{0,1:T(8,128)(2,1)S(1)} collective-permute-done((bf16[256,1536]{0,1:T(8,128)(2,1)S(1)}, bf16[256,1536]{0,1:T(8,128)(2,1)S(1)}, u32[]{:S(2)}, u32[]{:S(2)}) %collective-permute-start.7) | collective-permute-done | bytes 786464 | tf_op jit(solution)/shard_map/ppermute | solution.py:85
  180.0 9.7 %convolution_add_fusion = f32[768,1536]{1,0:T(8,128)} fusion(f32[768,1536]{1,0:T(8,128)S(1)} %bitcast.100, bf16[768,2048]{1,0:T(8,128)(2,1)S(1)} %copy-done.24, bf16[2048,1536]{0,1:T(8,128)(2,1)} %constant_dynamic-update-slice_fusion), kind=kOutput, calls=%fused_computation.18 | convolution fusion | flops 4833017856 | bytes 18874368 | tf_op jit(solution)/shard_map/dot_general | solution.py:55
  189.8 6.2 reshape.177
  205.9 8.9 %fusion.107 = (f32[4,768]{1,0:T(4,128)S(1)}, f32[4,768,768]{1,2,0:T(8,128)}) fusion(pred[768,768]{0,1:T(8,128)(4,1)} %fusion.19, bf16[768,4,64]{2,0,1:T(8,128)(2,1)S(1)} %get-tuple-element.59, bf16[768,4,64]{2,0,1:T(8,128)(2,1)} %get-tuple-element.60, bf16[768,4,64]{2,0,1:T(8,128)(2,1)S(1)} %get-tuple-element.38, bf16[768,4,64]{2,0,1:T(8,128)(2,1)S(1)} %get-tuple-element.37), kind=kOutput, calls=%fused_computation.265 | convolution fusion | flops 616563456 | bytes 11612160 | tf_op jit(solution)/shard_map/sub | solution.py:68
  223.8 5.3 add_convert_fusion.2
  247.1 9.7 %collective-permute-done.21 = bf16[192,2048]{1,0:T(8,128)(2,1)} collective-permute-done((bf16[192,2048]{1,0:T(8,128)(2,1)S(1)}, bf16[192,2048]{1,0:T(8,128)(2,1)}, u32[]{:S(2)}, u32[]{:S(2)}) %collective-permute-start.21) | collective-permute-done | bytes 786464 | tf_op jit(solution)/shard_map/ppermute | solution.py:85
  270.2 15.6 %collective-permute-done.25 = bf16[192,2048]{1,0:T(8,128)(2,1)S(1)} collective-permute-done((bf16[192,2048]{1,0:T(8,128)(2,1)}, bf16[192,2048]{1,0:T(8,128)(2,1)S(1)}, u32[]{:S(2)}, u32[]{:S(2)}) %collective-permute-start.25) | collective-permute-done | bytes 786464 | tf_op jit(solution)/shard_map/ppermute | solution.py:85
  285.9 15.9 %collective-permute-done.27 = bf16[192,2048]{1,0:T(8,128)(2,1)} collective-permute-done((bf16[192,2048]{1,0:T(8,128)(2,1)}, bf16[192,2048]{1,0:T(8,128)(2,1)}, u32[]{:S(2)}, u32[]{:S(2)}) %collective-permute-start.27) | collective-permute-done | bytes 786464 | tf_op jit(solution)/shard_map/ppermute | solution.py:85
  312.0 48.2 %collective-permute-done.37 = bf16[512,256]{1,0:T(8,128)(2,1)S(1)} collective-permute-done((bf16[512,256]{1,0:T(8,128)(2,1)S(1)}, bf16[512,256]{1,0:T(8,128)(2,1)S(1)}, u32[]{:S(2)}, u32[]{:S(2)}) %collective-permute-start.37) | collective-permute-done | bytes 262176 | tf_op jit(solution)/shard_map/ppermute | solution.py:85
  360.2 5.2 collective-permute-done.36
  374.5 19.9 %collective-permute-done.24 = s32[768]{0:T(1024)S(1)} collective-permute-done((s32[768]{0:T(1024)S(1)}, s32[768]{0:T(1024)S(1)}, u32[]{:S(2)}, u32[]{:S(2)}) %collective-permute-start.24) | collective-permute-done | bytes 3104 | tf_op jit(solution)/shard_map/ppermute | solution.py:85
  404.0 43.1 %collective-permute-done.46 = bf16[512,1024]{1,0:T(8,128)(2,1)} collective-permute-done((bf16[512,1024]{1,0:T(8,128)(2,1)}, bf16[512,1024]{1,0:T(8,128)(2,1)}, u32[]{:S(2)}, u32[]{:S(2)}) %collective-permute-start.46) | collective-permute-done | bytes 1048608 | tf_op jit(solution)/shard_map/ppermute | solution.py:85
  473.2 15.0 %collective-permute-done.33 = bf16[1280,1024]{1,0:T(8,128)(2,1)S(1)} collective-permute-done((bf16[1280,1024]{1,0:T(8,128)(2,1)}, bf16[1280,1024]{1,0:T(8,128)(2,1)S(1)}, u32[]{:S(2)}, u32[]{:S(2)}) %collective-permute-start.33) | collective-permute-done | bytes 2621472 | tf_op jit(solution)/shard_map/ppermute | solution.py:85
  504.1 48.6 %collective-permute-done.34 = bf16[1024,1024]{1,0:T(8,128)(2,1)S(1)} collective-permute-done((bf16[1024,1024]{1,0:T(8,128)(2,1)}, bf16[1024,1024]{1,0:T(8,128)(2,1)S(1)}, u32[]{:S(2)}, u32[]{:S(2)}) %collective-permute-start.34) | collective-permute-done | bytes 2097184 | tf_op jit(solution)/shard_map/ppermute | solution.py:85
  583.6 9.5 %collective-permute-done.42 = bf16[192,1024]{1,0:T(8,128)(2,1)} collective-permute-done((bf16[192,1024]{1,0:T(8,128)(2,1)}, bf16[192,1024]{1,0:T(8,128)(2,1)}, u32[]{:S(2)}, u32[]{:S(2)}) %collective-permute-start.42) | collective-permute-done | bytes 393248 | tf_op jit(solution)/shard_map/ppermute | solution.py:85
  593.0 7.2 %collective-permute-done.41 = bf16[192,1024]{1,0:T(8,128)(2,1)} collective-permute-done((bf16[192,1024]{1,0:T(8,128)(2,1)S(1)}, bf16[192,1024]{1,0:T(8,128)(2,1)}, u32[]{:S(2)}, u32[]{:S(2)}) %collective-permute-start.41) | collective-permute-done | bytes 393248 | tf_op jit(solution)/shard_map/ppermute | solution.py:85
  618.5 5.8 dynamic_update_slice.25
  624.3 5.8 dynamic_update_slice.26
  638.5 9.9 %collective-permute-done.53 = bf16[192,1024]{1,0:T(8,128)(2,1)S(1)} collective-permute-done((bf16[192,1024]{1,0:T(8,128)(2,1)S(1)}, bf16[192,1024]{1,0:T(8,128)(2,1)S(1)}, u32[]{:S(2)}, u32[]{:S(2)}) %collective-permute-start.53) | collective-permute-done | bytes 393248 | tf_op jit(solution)/shard_map/ppermute | solution.py:85
  (313 shorter events, 297.6 us)
Async XLA Ops:
  0.0 75.0 %collective-permute-start.10 = (bf16[512,256]{1,0:T(8,128)(2,1)}, bf16[512,256]{1,0:T(8,128)(2,1)}, u32[]{:S(2)}, u32[]{:S(2)}) collective-permute-start(bf16[512,256]{1,0:T(8,128)(2,1)} %param.22), channel_id=1, source_target_pairs={{0,4},{1,5},{2,6},{3,7},{4,0},{5,1},{6,2},{7,3},{8,12},{9,13},{10,... | collective-permute-start | bytes 786440 | tf_op jit(solution)/shard_map/ppermute | solution.py:85
  4.6 62.0 %collective-permute-start.11 = (bf16[256,256]{1,0:T(8,128)(2,1)}, bf16[256,256]{1,0:T(8,128)(2,1)}, u32[]{:S(2)}, u32[]{:S(2)}) collective-permute-start(bf16[256,256]{1,0:T(8,128)(2,1)} %get-tuple-element.64), channel_id=1, source_target_pairs={{0,24},{1,25},{2,26},{3,27},{4,28},{5,29},{6,30},{7,31},{8,0},{9,1... | collective-permute-start | bytes 393224 | tf_op jit(solution)/shard_map/ppermute | solution.py:85
  8.2 63.3 %collective-permute-start.14 = (bf16[256,256]{1,0:T(8,128)(2,1)}, bf16[256,256]{1,0:T(8,128)(2,1)S(1)}, u32[]{:S(2)}, u32[]{:S(2)}) collective-permute-start(bf16[256,256]{1,0:T(8,128)(2,1)} %get-tuple-element.64), channel_id=1, source_target_pairs={{0,8},{1,9},{2,10},{3,11},{4,12},{5,13},{6,14},{7,15},{8,16},{9,17... | collective-permute-start | bytes 393224 | tf_op jit(solution)/shard_map/ppermute | solution.py:85
  8.2 62.3 %collective-permute-start.12 = (bf16[256,256]{1,0:T(8,128)(2,1)}, bf16[256,256]{1,0:T(8,128)(2,1)}, u32[]{:S(2)}, u32[]{:S(2)}) collective-permute-start(bf16[256,256]{1,0:T(8,128)(2,1)} %get-tuple-element.63), channel_id=1, source_target_pairs={{0,24},{1,25},{2,26},{3,27},{4,28},{5,29},{6,30},{7,31},{8,0},{9,1... | collective-permute-start | bytes 393224 | tf_op jit(solution)/shard_map/ppermute | solution.py:85
  12.1 60.1 %collective-permute-start.18 = (bf16[256,256]{1,0:T(8,128)(2,1)}, bf16[256,256]{1,0:T(8,128)(2,1)}, u32[]{:S(2)}, u32[]{:S(2)}) collective-permute-start(bf16[256,256]{1,0:T(8,128)(2,1)} %get-tuple-element.63), channel_id=1, source_target_pairs={{0,8},{1,9},{2,10},{3,11},{4,12},{5,13},{6,14},{7,15},{8,16},{9,17... | collective-permute-start | bytes 393224 | tf_op jit(solution)/shard_map/ppermute | solution.py:85
  66.7 31.7 %collective-permute-start.1 = (bf16[128,1536]{0,1:T(8,128)(2,1)S(1)}, bf16[128,1536]{0,1:T(8,128)(2,1)S(1)}, u32[]{:S(2)}, u32[]{:S(2)}) collective-permute-start(bf16[128,1536]{0,1:T(8,128)(2,1)S(1)} %bitcast.107), channel_id=1, source_target_pairs={{0,24},{1,25},{2,26},{3,27},{4,28},{5,29},{6,30},{7,31},{8,0},{9,1... | collective-permute-start | bytes 1179656 | tf_op jit(solution)/shard_map/ppermute | solution.py:85
  70.5 29.4 %collective-permute-start.2 = (bf16[128,1536]{0,1:T(8,128)(2,1)S(1)}, bf16[128,1536]{0,1:T(8,128)(2,1)S(1)}, u32[]{:S(2)}, u32[]{:S(2)}) collective-permute-start(bf16[128,1536]{0,1:T(8,128)(2,1)S(1)} %bitcast.103), channel_id=1, source_target_pairs={{0,24},{1,25},{2,26},{3,27},{4,28},{5,29},{6,30},{7,31},{8,0},{9,1... | collective-permute-start | bytes 1179656 | tf_op jit(solution)/shard_map/ppermute | solution.py:85
  95.7 40.6 %collective-permute-start = (bf16[256,1536]{0,1:T(8,128)(2,1)S(1)}, bf16[256,1536]{0,1:T(8,128)(2,1)S(1)}, u32[]{:S(2)}, u32[]{:S(2)}) collective-permute-start(bf16[256,1536]{0,1:T(8,128)(2,1)S(1)} %pad_maximum_fusion.5), channel_id=1, source_target_pairs={{0,4},{1,5},{2,6},{3,7},{4,0},{5,1},{6,2},{7,3},{8,12},{9,13},{10,... | collective-permute-start | bytes 2359304 | tf_op jit(solution)/shard_map/ppermute | solution.py:85
  98.4 34.6 %collective-permute-start.19 = (bf16[512,256]{1,0:T(8,128)(2,1)S(1)}, bf16[512,256]{1,0:T(8,128)(2,1)S(1)}, u32[]{:S(2)}, u32[]{:S(2)}) collective-permute-start(bf16[512,256]{1,0:T(8,128)(2,1)S(1)} %pad_maximum_fusion.16), channel_id=1, source_target_pairs={{0,4},{1,5},{2,6},{3,7},{4,0},{5,1},{6,2},{7,3},{8,12},{9,13},{10,... | collective-permute-start | bytes 786440 | tf_op jit(solution)/shard_map/ppermute | solution.py:85
  104.7 39.6 %collective-permute-start.3 = (bf16[256,1536]{0,1:T(8,128)(2,1)S(1)}, bf16[256,1536]{0,1:T(8,128)(2,1)S(1)}, u32[]{:S(2)}, u32[]{:S(2)}) collective-permute-start(bf16[256,1536]{0,1:T(8,128)(2,1)S(1)} %pad_maximum_fusion.6), channel_id=1, source_target_pairs={{0,4},{1,5},{2,6},{3,7},{4,0},{5,1},{6,2},{7,3},{8,12},{9,13},{10,... | collective-permute-start | bytes 2359304 | tf_op jit(solution)/shard_map/ppermute | solution.py:85
  133.0 46.1 %collective-permute-start.9 = (bf16[256,1536]{0,1:T(8,128)(2,1)S(1)}, bf16[256,1536]{0,1:T(8,128)(2,1)S(1)}, u32[]{:S(2)}, u32[]{:S(2)}) collective-permute-start(bf16[256,1536]{0,1:T(8,128)(2,1)S(1)} %pad_maximum_fusion.8), channel_id=1, source_target_pairs={{0,4},{1,5},{2,6},{3,7},{4,0},{5,1},{6,2},{7,3},{8,12},{9,13},{10,... | collective-permute-start | bytes 2359304 | tf_op jit(solution)/shard_map/ppermute | solution.py:85
  135.6 40.8 %collective-permute-start.7 = (bf16[256,1536]{0,1:T(8,128)(2,1)S(1)}, bf16[256,1536]{0,1:T(8,128)(2,1)S(1)}, u32[]{:S(2)}, u32[]{:S(2)}) collective-permute-start(bf16[256,1536]{0,1:T(8,128)(2,1)S(1)} %pad_maximum_fusion.7), channel_id=1, source_target_pairs={{0,4},{1,5},{2,6},{3,7},{4,0},{5,1},{6,2},{7,3},{8,12},{9,13},{10,... | collective-permute-start | bytes 2359304 | tf_op jit(solution)/shard_map/ppermute | solution.py:85
  263.6 38.3 %collective-permute-start.27 = (bf16[192,2048]{1,0:T(8,128)(2,1)}, bf16[192,2048]{1,0:T(8,128)(2,1)}, u32[]{:S(2)}, u32[]{:S(2)}) collective-permute-start(bf16[192,2048]{1,0:T(8,128)(2,1)} %get-tuple-element.28), channel_id=1, source_target_pairs={{0,12},{1,13},{2,14},{3,15},{4,8},{5,9},{6,10},{7,11},{8,4},{9,5},... | collective-permute-start | bytes 2359304 | tf_op jit(solution)/shard_map/ppermute | solution.py:85
  304.9 149.4 %collective-permute-start.28 = (bf16[768,2048]{1,0:T(8,128)(2,1)}, bf16[768,2048]{1,0:T(8,128)(2,1)}, u32[]{:S(2)}, u32[]{:S(2)}) collective-permute-start(bf16[768,2048]{1,0:T(8,128)(2,1)} %pad_maximum_fusion), channel_id=1, source_target_pairs={{0,1},{1,0},{2,3},{3,2},{4,5},{5,4},{6,7},{7,6},{8,9},{9,8},{10,11... | collective-permute-start | bytes 9437192 | tf_op jit(solution)/shard_map/ppermute | solution.py:85
  308.0 139.6 %collective-permute-start.32 = (bf16[1024,1024]{1,0:T(8,128)(2,1)}, bf16[1024,1024]{1,0:T(8,128)(2,1)}, u32[]{:S(2)}, u32[]{:S(2)}) collective-permute-start(bf16[1024,1024]{1,0:T(8,128)(2,1)} %pad_maximum_fusion.2), channel_id=1, source_target_pairs={{0,16},{1,17},{2,18},{3,19},{4,20},{5,21},{6,22},{7,23},{8,24},{9,... | collective-permute-start | bytes 6291464 | tf_op jit(solution)/shard_map/ppermute | solution.py:85
  308.4 51.7 %collective-permute-start.37 = (bf16[512,256]{1,0:T(8,128)(2,1)S(1)}, bf16[512,256]{1,0:T(8,128)(2,1)S(1)}, u32[]{:S(2)}, u32[]{:S(2)}) collective-permute-start(bf16[512,256]{1,0:T(8,128)(2,1)S(1)} %get-tuple-element.49), channel_id=1, source_target_pairs={{0,12},{1,13},{2,14},{3,15},{4,8},{5,9},{6,10},{7,11},{8,4},{9,5},... | collective-permute-start | bytes 786440 | tf_op jit(solution)/shard_map/ppermute | solution.py:85
  310.1 55.3 %collective-permute-start.36 = (bf16[512,256]{1,0:T(8,128)(2,1)S(1)}, bf16[512,256]{1,0:T(8,128)(2,1)S(1)}, u32[]{:S(2)}, u32[]{:S(2)}) collective-permute-start(bf16[512,256]{1,0:T(8,128)(2,1)S(1)} %get-tuple-element.50), channel_id=1, source_target_pairs={{0,8},{1,9},{2,10},{3,11},{4,12},{5,13},{6,14},{7,15},{8,0},{9,1},... | collective-permute-start | bytes 786440 | tf_op jit(solution)/shard_map/ppermute | solution.py:85
  311.3 54.1 %collective-permute-start.35 = (bf16[512,256]{1,0:T(8,128)(2,1)S(1)}, bf16[512,256]{1,0:T(8,128)(2,1)S(1)}, u32[]{:S(2)}, u32[]{:S(2)}) collective-permute-start(bf16[512,256]{1,0:T(8,128)(2,1)S(1)} %get-tuple-element.48), channel_id=1, source_target_pairs={{0,4},{1,5},{2,6},{3,7},{4,0},{5,1},{6,2},{7,3},{8,12},{9,13},{10,... | collective-permute-start | bytes 786440 | tf_op jit(solution)/shard_map/ppermute | solution.py:85
  368.1 79.1 %collective-permute-start.46 = (bf16[512,1024]{1,0:T(8,128)(2,1)}, bf16[512,1024]{1,0:T(8,128)(2,1)}, u32[]{:S(2)}, u32[]{:S(2)}) collective-permute-start(bf16[512,1024]{1,0:T(8,128)(2,1)} %pad_maximum_fusion.4), channel_id=1, source_target_pairs={{0,16},{1,17},{2,18},{3,19},{4,20},{5,21},{6,22},{7,23},{8,24},{9,... | collective-permute-start | bytes 3145736 | tf_op jit(solution)/shard_map/ppermute | solution.py:85
  400.1 162.7 %collective-permute-start.38 = (bf16[512,1280]{1,0:T(8,128)(2,1)}, bf16[512,1280]{1,0:T(8,128)(2,1)S(1)}, u32[]{:S(2)}, u32[]{:S(2)}) collective-permute-start(bf16[512,1280]{1,0:T(8,128)(2,1)} %dynamic-slice_dynamic-update-slice_fusion.8), channel_id=1, source_target_pairs={{0,2},{1,3},{2,0},{3,1},{4,6},{5,7},{6,4},{7,5},{8,10},{9,11},{10,... | collective-permute-start | bytes 3932168 | tf_op jit(solution)/shard_map/ppermute | solution.py:85
  402.5 85.7 %collective-permute-start.33 = (bf16[1280,1024]{1,0:T(8,128)(2,1)}, bf16[1280,1024]{1,0:T(8,128)(2,1)S(1)}, u32[]{:S(2)}, u32[]{:S(2)}) collective-permute-start(bf16[1280,1024]{1,0:T(8,128)(2,1)} %maximum_dynamic-update-slice_fusion), channel_id=1, source_target_pairs={{0,2},{1,3},{2,0},{3,1},{4,6},{5,7},{6,4},{7,5},{8,10},{9,11},{10,... | collective-permute-start | bytes 7864328 | tf_op jit(solution)/shard_map/ppermute | solution.py:85
  447.1 123.7 %collective-permute-start.47 = (bf16[512,1024]{1,0:T(8,128)(2,1)}, bf16[512,1024]{1,0:T(8,128)(2,1)}, u32[]{:S(2)}, u32[]{:S(2)}) collective-permute-start(bf16[512,1024]{1,0:T(8,128)(2,1)} %collective-permute-done.46), channel_id=1, source_target_pairs={{0,2},{1,3},{2,0},{3,1},{4,6},{5,7},{6,4},{7,5},{8,10},{9,11},{10,... | collective-permute-start | bytes 3145736 | tf_op jit(solution)/shard_map/ppermute | solution.py:85
  447.6 105.1 %collective-permute-start.34 = (bf16[1024,1024]{1,0:T(8,128)(2,1)}, bf16[1024,1024]{1,0:T(8,128)(2,1)S(1)}, u32[]{:S(2)}, u32[]{:S(2)}) collective-permute-start(bf16[1024,1024]{1,0:T(8,128)(2,1)} %collective-permute-done.32), channel_id=1, source_target_pairs={{0,2},{1,3},{2,0},{3,1},{4,6},{5,7},{6,4},{7,5},{8,10},{9,11},{10,... | collective-permute-start | bytes 6291464 | tf_op jit(solution)/shard_map/ppermute | solution.py:85
  575.5 30.1 %collective-permute-start.48 = (bf16[768,1024]{1,0:T(8,128)(2,1)}, bf16[768,1024]{1,0:T(8,128)(2,1)}, u32[]{:S(2)}, u32[]{:S(2)}) collective-permute-start(bf16[768,1024]{1,0:T(8,128)(2,1)} %slice.182), channel_id=1, source_target_pairs={{0,1},{1,0},{2,3},{3,2},{4,5},{5,4},{6,7},{7,6},{8,9},{9,8},{10,11... | collective-permute-start | bytes 4718600 | tf_op jit(solution)/shard_map/ppermute | solution.py:85
  (61 other events, 1302.5 us)

commit v2 on v1

v2 whole, which is shorter than its diff:
```python
import functools
import math

import jax
import jax.numpy as jnp
from jax import lax
from jax.experimental import pallas as pl
from jax.experimental.pallas import tpu as pltpu
from jax.sharding import PartitionSpec as P

HD = 128
RANK = 16
AXES = ("req", "tp")
epsilon = 1e-05
rope_base = 10000.0
F32 = jnp.float32
BF16 = jnp.bfloat16
VM = pltpu.VMEM
PARAMS = pltpu.CompilerParams(vmem_limit_bytes=56 * 2**20)
COST = pl.CostEstimate(flops=1000, bytes_accessed=1000, transcendentals=0)


def dot(a, b):
    return jnp.dot(a, b, preferred_element_type=F32)


def layer_norm(values):
    row_mean = jnp.mean(values, axis=-1, keepdims=True)
    centred = values - row_mean
    spread = jnp.mean(centred * centred, axis=-1, keepdims=True)
    return (centred * lax.rsqrt(spread + epsilon)).astype(BF16)


def slot_layout(lengths_row, adapters_row, slot_count):
    request_ends = jnp.cumsum(lengths_row)
    request_starts = request_ends - lengths_row
    slot_index = jnp.arange(slot_count, dtype=jnp.int32)
    request_of = jnp.sum((slot_index[:, None] >= request_ends[None, :]).astype(jnp.int32), axis=1)
    member = request_of[:, None] == jnp.arange(lengths_row.shape[0], dtype=jnp.int32)[None, :]
    position = slot_index - jnp.sum(jnp.where(member, request_starts[None, :], 0), axis=1)
    adapter = jnp.sum(jnp.where(member, adapters_row[None, :], 0), axis=1)
    return (request_of, position, adapter)


def rope_tables(position):
    half = HD // 2
    frequency = jnp.exp(-math.log(rope_base) * 2.0 * jnp.arange(half, dtype=F32) / HD)
    angles = position.astype(F32)[:, None] * frequency[None, :]
    cosine, sine = jnp.cos(angles), jnp.sin(angles)
    return jnp.concatenate([cosine, cosine], 1), jnp.concatenate([-sine, sine], 1)


def masked(inner, adapter_column):
    rank = lax.broadcasted_iota(jnp.int32, inner.shape, 1) // RANK
    return jnp.where(adapter_column == rank, inner, F32(0.0)).astype(BF16)


def whole(array):
    return pl.BlockSpec(array.shape, lambda *_: (0,) * array.ndim, pipeline_mode=pl.Buffered(1))


def mm(start, size):
    return pl.ds(pl.multiple_of(start * size, size), size)


def qkv_kernel(blocks, half_tiles, rotated, order, x, low, b, cosine, sine, *refs):
    weights, out = refs[:-1], refs[-1]
    n = pl.program_id(0)
    size = x.shape[1] // blocks
    total = dot(low[...], b[...])
    for at in range(blocks):
        w = weights[2 * at][...]
        if weights[2 * at + 1] is not None:
            w = jnp.where(n < half_tiles, w, weights[2 * at + 1][...])
        total = total + dot(x[:, mm(order[at], size)], w)

    @pl.when(n < rotated)
    def _():
        for h in range(total.shape[1] // HD):
            v = total[:, h * HD : (h + 1) * HD]
            turned = v * cosine[...] + pltpu.roll(v, HD // 2, 1) * sine[...]
            out[:, h * HD : (h + 1) * HD] = turned.astype(BF16)

    @pl.when(n >= rotated)
    def _():
        out[...] = total.astype(BF16)


def project_qkv(x, low, b, cosine, sine, weights, order):
    slots, columns = x.shape[0], b.shape[1]
    tile = 256 if columns % 512 == 0 and columns % 768 == 0 else HD
    half = columns // 2 // tile
    specs, flat, kept = [], [], []
    for w in weights:
        size = w[0].shape[0]
        if len(w) == 1:
            specs.append(pl.BlockSpec((size, tile), lambda n, o: (0, n)))
            flat.append(w[0])
            kept += [True, False]
        else:
            specs.append(pl.BlockSpec((size, tile), lambda n, o: (0, jnp.minimum(n, half - 1))))
            specs.append(pl.BlockSpec((size, tile), lambda n, o: (0, jnp.maximum(n - half, 0))))
            flat += list(w)
            kept += [True, True]

    def kernel(order_ref, x_ref, low_ref, b_ref, cos_ref, sin_ref, *refs):
        it = iter(refs[:-1])
        spread = [next(it) if k else None for k in kept]
        qkv_kernel(
            len(weights), half, columns // 3 * 2 // tile,
            order_ref, x_ref, low_ref, b_ref, cos_ref, sin_ref, *spread, refs[-1],
        )

    return pl.pallas_call(
        kernel,
        grid_spec=pltpu.PrefetchScalarGridSpec(
            num_scalar_prefetch=1,
            grid=(columns // tile,),
            in_specs=[
                whole(x),
                whole(low),
                pl.BlockSpec((b.shape[0], tile), lambda n, o: (0, n)),
                whole(cosine),
                whole(sine),
                *specs,
            ],
            out_specs=pl.BlockSpec((slots, tile), lambda n, o: (0, n)),
        ),
        out_shape=jax.ShapeDtypeStruct((slots, columns), BF16),
        compiler_params=PARAMS,
        cost_estimate=COST,
        name="project_qkv",
    )(order, x, low, b, cosine, sine, *flat)


def attend(qkv, request_of):
    slots, heads = qkv.shape[0], qkv.shape[1] // 3 // HD
    rows = 256 if slots % 256 == 0 else slots
    column, line = request_of[:, None], request_of[None, :]

    def kernel(q, k, v, column_ref, line_ref, out):
        for at in range(0, slots, rows):
            seen = at + rows
            s = lax.dot_general(
                q[at:seen], k[:seen], (((1,), (1,)), ((), ())), preferred_element_type=F32
            )
            s = s * (1.0 / math.sqrt(HD))
            here = at + lax.broadcasted_iota(jnp.int32, s.shape, 0)
            there = lax.broadcasted_iota(jnp.int32, s.shape, 1)
            allowed = (column_ref[at:seen] == line_ref[:, :seen]) & (here >= there)
            s = jnp.where(allowed, s, F32(-1e30))
            e = jnp.exp(s - jnp.max(s, axis=1, keepdims=True))
            weights = (e * (1.0 / jnp.sum(e, axis=1, keepdims=True))).astype(BF16)
            out[at:seen] = dot(weights, v[:seen]).astype(BF16)

    return pl.pallas_call(
        kernel,
        grid=(heads,),
        in_specs=[
            pl.BlockSpec((slots, HD), lambda h: (0, h)),
            pl.BlockSpec((slots, HD), lambda h: (0, heads + h)),
            pl.BlockSpec((slots, HD), lambda h: (0, 2 * heads + h)),
            whole(column),
            whole(line),
        ],
        out_specs=pl.BlockSpec((slots, HD), lambda h: (0, h)),
        out_shape=jax.ShapeDtypeStruct((slots, heads * HD), BF16),
        compiler_params=PARAMS,
        cost_estimate=COST,
        name="attend",
    )(qkv, qkv, qkv, column, line)


def project_out(attn, adapter, a, b, weights, order, row_order, chunks):
    slots, width = attn.shape[0], b.shape[1]
    size, n = width // len(weights), len(weights)
    piece = slots // row_order.shape[0]
    flat = [p for w in weights for p in w]
    column = adapter[:, None]
    shape = jax.ShapeDtypeStruct((slots // 2, width // chunks), BF16)

    def kernel(order_ref, rows_ref, attn_ref, adapter_ref, a_ref, b_ref, *refs):
        ws, outs, rows, low = refs[: len(flat)], refs[len(flat) : -2], refs[-2], refs[-1]
        for q in range(row_order.shape[0]):
            here = mm(rows_ref[q], piece)
            part = attn_ref[here, :]
            rows[q * piece : (q + 1) * piece] = part
            low[q * piece : (q + 1) * piece] = masked(dot(part, a_ref[...]), adapter_ref[here, :])
        it = iter(ws)
        for at, w in enumerate(weights):
            total = dot(low[...], b_ref[:, mm(order_ref[at], size)])
            start = 0
            for p in w:
                total = total + dot(rows[:, start : start + p.shape[0]], next(it)[...])
                start += p.shape[0]
            total = total.astype(BF16)
            chunk, place = divmod(at, n // chunks)
            to = slice(place * size, (place + 1) * size)
            outs[2 * chunk][:, to] = total[: slots // 2]
            outs[2 * chunk + 1][:, to] = total[slots // 2 :]

    smem = pl.BlockSpec(memory_space=pltpu.SMEM)
    out = pl.pallas_call(
        kernel,
        in_specs=[smem, smem] + [pl.BlockSpec(memory_space=VM)] * (4 + len(flat)),
        out_specs=[pl.BlockSpec(memory_space=VM)] * (2 * chunks),
        out_shape=[shape] * (2 * chunks),
        scratch_shapes=[VM(attn.shape, BF16), VM((slots, a.shape[1]), BF16)],
        compiler_params=PARAMS,
        cost_estimate=COST,
        name="project_out",
    )(order, row_order, attn, column, a, b, *flat)
    return [(out[2 * i], out[2 * i + 1]) for i in range(chunks)]


def residual_norm(tokens, row, order, chunks):
    width, n = tokens.shape[1], order.shape[0]
    piece, size = chunks[0][-1].shape[0], width // n
    flat = [p for c in chunks for p in c]
    per = n // len(chunks)

    def kernel(row_ref, order_ref, tok_ref, *refs):
        parts, hidden, normed = refs[: len(flat)], refs[-2], refs[-1]
        it = iter(parts)
        for c, group in enumerate(chunks):
            total = None
            for _ in group:
                p = next(it)[...].astype(F32)
                total = p if total is None else total + p
            for place in range(per):
                to = mm(order_ref[c * per + place], size)
                hidden[:, to] = tok_ref[:, to].astype(F32) + total[:, place * size : (place + 1) * size]
        normed[...] = layer_norm(hidden[...])

    return pl.pallas_call(
        kernel,
        grid_spec=pltpu.PrefetchScalarGridSpec(
            num_scalar_prefetch=2,
            grid=(1,),
            in_specs=[
                pl.BlockSpec((piece, width), lambda n, r, o: (r[0], 0)),
                *[pl.BlockSpec((piece, p.shape[1]), lambda n, r, o: (0, 0)) for p in flat],
            ],
            out_specs=[pl.BlockSpec((piece, width), lambda n, r, o: (0, 0))] * 2,
        ),
        out_shape=[
            jax.ShapeDtypeStruct((piece, width), F32),
            jax.ShapeDtypeStruct((piece, width), BF16),
        ],
        compiler_params=PARAMS,
        cost_estimate=COST,
        name="residual_norm",
    )(row, order, tokens, *flat)


def gated(rows, adapters, a_gate, a_up, sets, order):
    piece, width = rows[0].shape
    total_rows = piece * len(rows)
    n_blocks = len(sets[0][0])
    size = width // n_blocks
    units = sets[0][1].shape[1] // 2
    tile = min(256, units)
    tiles = units // tile
    rank = a_gate.shape[1]
    column = adapters[:, None]
    flat = [w for s in sets for w in s[0]]
    bs = [s[1] for s in sets]
    downs = [s[2] for s in sets]
    n_rows, n_sets = len(rows), len(sets)
    steps = n_sets * tiles
    chunk = total_rows // 4 if total_rows % 64 == 0 else total_rows

    def kernel(order_ref, adapter_ref, ag_ref, au_ref, *refs):
        it = iter(refs)
        take = lambda k: [next(it) for _ in range(k)]
        x_in, w_in, b_in, d_in = take(n_rows), take(len(flat)), take(n_sets), take(n_sets)
        hidden, low_out, x, w, bb, lg, lu, ld, x_sem, w_sem, b_sem = take(11)

        def weight_copies(step, slot):
            s, t = divmod(step, tiles)
            for at in range(n_blocks):
                for g in range(2):
                    yield pltpu.make_async_copy(
                        w_in[s * n_blocks + at].at[:, pl.ds(g * units + t * tile, tile)],
                        w.at[slot, g, mm(order_ref[at], size), :],
                        w_sem.at[slot, g, at],
                    )
            for g in range(2):
                yield pltpu.make_async_copy(
                    b_in[s].at[:, pl.ds(g * units + t * tile, tile)],
                    bb.at[slot, g],
                    b_sem.at[slot, g],
                )

        x_copies = [
            pltpu.make_async_copy(x_in[i], x.at[pl.ds(i * piece, piece), :], x_sem.at[i])
            for i in range(n_rows)
        ]
        for copy in weight_copies(0, 0):
            copy.start()
        for copy in x_copies:
            copy.start()
        for copy in x_copies:
            copy.wait()
        for step in range(steps):
            slot = step % 2
            if step + 1 < steps:
                for copy in weight_copies(step + 1, 1 - slot):
                    copy.start()
            for copy in weight_copies(step, slot):
                copy.wait()
            s, t = divmod(step, tiles)

            @pl.loop(0, total_rows // chunk)
            def _(m):
                at = mm(m, chunk)
                xs = x[at, :]
                if step == 0:
                    lg[at, :] = masked(dot(xs, ag_ref[...]), adapter_ref[at, :])
                    lu[at, :] = masked(dot(xs, au_ref[...]), adapter_ref[at, :])
                gate = dot(xs, w[slot, 0]) + dot(lg[at, :], bb[slot, 0])
                up = dot(xs, w[slot, 1]) + dot(lu[at, :], bb[slot, 1])
                h = (gate / (1.0 + jnp.exp(-gate)) * up).astype(BF16)
                hidden[at, step * tile : (step + 1) * tile] = h
                more = dot(h, d_in[s][t * tile : (t + 1) * tile, :])
                if step == 0:
                    ld[at, :] = more
                else:
                    ld[at, :] = ld[at, :] + more
                if step == steps - 1:
                    low_out[at, :] = masked(ld[at, :], adapter_ref[at, :])

    smem = pl.BlockSpec(memory_space=pltpu.SMEM)
    vmem = pl.BlockSpec(memory_space=VM)
    hbm = pl.BlockSpec(memory_space=pl.ANY)
    return pl.pallas_call(
        kernel,
        in_specs=[smem, vmem, vmem, vmem]
        + [hbm] * (n_rows + len(flat) + n_sets)
        + [vmem] * n_sets,
        out_specs=[vmem, vmem],
        out_shape=[
            jax.ShapeDtypeStruct((total_rows, n_sets * units), BF16),
            jax.ShapeDtypeStruct((total_rows, rank), BF16),
        ],
        scratch_shapes=[
            VM((total_rows, width), BF16),
            VM((2, 2, width, tile), BF16),
            VM((2, 2, rank, tile), BF16),
            VM((total_rows, rank), BF16),
            VM((total_rows, rank), BF16),
            VM((total_rows, rank), F32),
            pltpu.SemaphoreType.DMA((n_rows,)),
            pltpu.SemaphoreType.DMA((2, 2, n_blocks)),
            pltpu.SemaphoreType.DMA((2, 2)),
        ],
        compiler_params=PARAMS,
        cost_estimate=COST,
        name="gated",
    )(order, column, a_gate, a_up, *rows, *flat, *bs, *downs)


def project_down(hidden, low, b, blocks, order):
    total_rows = hidden.shape[0]
    flat = [w for block in blocks for w in block]
    units, size = flat[0].shape
    half = total_rows // 2
    chunk = half // 2 if half % 32 == 0 else half

    def kernel(order_ref, h_ref, low_ref, b_ref, *refs):
        ws, outs = refs[: len(flat)], refs[len(flat) :]
        for at, block in enumerate(blocks):
            to = mm(order_ref[at], size)
            for o in range(2):

                @pl.loop(0, half // chunk)
                def _(m):
                    here = mm(m + o * (half // chunk), chunk)
                    total = dot(low_ref[here, :], b_ref[:, to])
                    for k in range(len(block)):
                        w = ws[at * len(block) + k][...]
                        total = total + dot(h_ref[here, k * units : (k + 1) * units], w)
                    outs[o][mm(m, chunk), to] = total.astype(BF16)

    smem = pl.BlockSpec(memory_space=pltpu.SMEM)
    vmem = pl.BlockSpec(memory_space=VM)
    return pl.pallas_call(
        kernel,
        in_specs=[smem] + [vmem] * (3 + len(flat)),
        out_specs=[vmem, vmem],
        out_shape=[jax.ShapeDtypeStruct((half, b.shape[1]), BF16)] * 2,
        compiler_params=PARAMS,
        cost_estimate=COST,
        name="project_down",
    )(order, hidden, low, b, *flat)


def assemble(pieces, places, shape):
    rows, columns = pieces[0].shape

    def kernel(places_ref, *refs):
        parts, out, sems = refs[: len(pieces)], refs[-2], refs[-1]
        copies = [
            pltpu.make_async_copy(
                parts[i],
                out.at[mm(places_ref[2 * i], rows), mm(places_ref[2 * i + 1], columns)],
                sems.at[i],
            )
            for i in range(len(pieces))
        ]
        for copy in copies:
            copy.start()
        for copy in copies:
            copy.wait()

    hbm = pl.BlockSpec(memory_space=pl.ANY)
    return pl.pallas_call(
        kernel,
        in_specs=[pl.BlockSpec(memory_space=pltpu.SMEM)] + [hbm] * len(pieces),
        out_specs=hbm,
        out_shape=jax.ShapeDtypeStruct(shape, BF16),
        scratch_shapes=[pltpu.SemaphoreType.DMA((len(pieces),))],
        compiler_params=PARAMS,
        cost_estimate=COST,
        name="assemble",
    )(places, *pieces)


def make_body(R, T):
    Z, ZH, Y = R // 2, R // 4, T // 2

    def move(f):
        pairs = []
        for r in range(R):
            for t in range(T):
                z, x, y, c = f(r // 2, r % 2, t // 2, t % 2)
                pairs.append((r * T + t, (z * 2 + x) * T + y * 2 + c))
        return pairs

    def send(value, pairs, after=()):
        if after:
            value = lax.optimization_barrier((value, *after))[0]
        return lax.ppermute(value, AXES, pairs)

    to_core = move(lambda z, x, y, c: (z, x, y, 1 - c))
    to_x = move(lambda z, x, y, c: (z, 1 - x, y, c))
    to_xz = {}
    for i in (0, 1):
        for j in (0, 1):
            to_xz[(i, j)] = move(lambda z, x, y, c, i=i, j=j: (z ^ j, x ^ i, y, c))
    z_up = move(lambda z, x, y, c: ((z + 1) % Z, x, y, c))
    z_down = move(lambda z, x, y, c: ((z - 1) % Z, x, y, c))
    from_y = {k: move(lambda z, x, y, c, k=k: (z, x, (y - k) % Y, c)) for k in range(1, Y)}
    from_zh = {
        k: move(lambda z, x, y, c, k=k: ((z - 2 * k) % Z, x, y, c)) for k in range(1, ZH)
    }
    near = [(0, 0), (1, 0), (0, 1), (1, 1)]
    others = near[1:]

    def ring(own, halve, after=()):
        got, left, right = {0: (own,)}, own, own
        if after:
            left = right = lax.optimization_barrier((own, *after))[0]
        for k in range(1, Z // 2):
            left, right = send(left, z_up), send(right, z_down)
            got[Z - k], got[k] = (left,), (right,)
        first, second = halve(left)[0], halve(right)[1]
        got[Z // 2] = (send(first, z_up), send(second, z_down))
        return got

    def body(
        tokens, lengths, request_adapter, w_qkv, w_out, w_gate, w_up, w_down,
        a_qkv, b_qkv, a_out, b_out, a_gate, b_gate, a_up, b_up, a_down, b_down,
    ):
        r, t = lax.axis_index("req"), lax.axis_index("tp")
        z, x, y, c = r // 2, r % 2, t // 2, t % 2
        zh, zl = z // 2, z % 2
        slots, width = tokens.shape
        piece = slots // T
        block = width // R
        local = w_qkv.shape[2]
        rank_all = a_qkv.shape[1]
        quarter = w_gate.shape[1] // 4
        span = width // ZH

        def cut(array, start, size, axis):
            return lax.dynamic_slice_in_dim(array, start, size, axis)

        def ints(values):
            return jnp.stack([jnp.asarray(v, jnp.int32) for v in values])

        def columns_halved(w):
            return w[:, : w.shape[1] // 2], w[:, w.shape[1] // 2 :]

        def rows_halved(w):
            return w[: w.shape[0] // 2], w[w.shape[0] // 2 :]

        qkv_got = ring(w_qkv.reshape(block, 3 * local), columns_halved)
        qkv_swapped = {}
        for k in [0, *[k for k in range(1, Z) if k != Z // 2], Z // 2]:
            qkv_swapped[k] = tuple(send(w, to_x) for w in qkv_got[k])
        qkv_weights = [w for k in range(Z) for w in (qkv_got[k], qkv_swapped[k])]
        order = ints([((z + k) % Z) * 2 + (x ^ i) for k in range(Z) for i in (0, 1)])

        out_got = ring(w_out, rows_halved, after=[qkv_got[1][0], qkv_got[Z - 1][0]])
        out_swapped = {k: tuple(send(w, to_x) for w in out_got[k]) for k in range(Z)}
        out_weights = [w for k in range(Z) for w in (out_got[k], out_swapped[k])]

        mine = (zl * 2 + x) * quarter
        gu, down = {}, {}
        for i, j in near:
            at = ((zl ^ j) * 2 + (x ^ i)) * quarter
            pair = [cut(w, at, quarter, 1) for w in (w_gate, w_up)]
            gu[(i, j, 0, 0)] = jnp.concatenate(pair, axis=1)
            down[(i, j, 0, 0)] = cut(w_down, at, quarter, 0)
        b_own = jnp.concatenate(
            [cut(b_gate, mine, quarter, 1), cut(b_up, mine, quarter, 1)], axis=1
        )
        a_down_own = cut(a_down, mine, quarter, 0)
        for o in others:
            gu[(*o, 0, 0)] = send(gu[(*o, 0, 0)], to_xz[o])
        for o in others:
            down[(*o, 0, 0)] = send(down[(*o, 0, 0)], to_xz[o])
        b_gu, a_dn = [b_own], [a_down_own]
        for k in range(1, Y):
            b_gu.append(send(b_own, from_y[k]))
            a_dn.append(send(a_down_own, from_y[k]))
        for held in (gu, down):
            for k in range(1, Y):
                for o in near:
                    held[(*o, 0, k)] = send(held[(*o, 0, 0)], from_y[k])
            for h in range(1, ZH):
                for o in near:
                    held[(*o, h, 0)] = send(held[(*o, 0, 0)], from_zh[h])
                    for k in range(1, Y):
                        held[(*o, h, k)] = send(held[(*o, h, 0)], from_y[k])

        request_of, position, adapter = slot_layout(lengths[0], request_adapter[0], slots)
        near_adapters = [adapter] + [send(adapter, to_xz[o]) for o in others]
        cosine, sine = rope_tables(position)
        normed = layer_norm(tokens.astype(F32))
        column_adapter = jnp.arange(rank_all, dtype=jnp.int32) // RANK
        chosen = adapter[:, None] == column_adapter[None, :]
        low = jnp.where(chosen, dot(normed, a_qkv), F32(0.0)).astype(BF16)
        qkv = project_qkv(
            normed, low, b_qkv.reshape(rank_all, 3 * local), cosine, sine, qkv_weights, order
        )
        attn = attend(qkv, request_of)
        row_order = ints([((y - k) % Y) * 2 + s for s in (c, 1 - c) for k in range(Y)])
        sums = []
        for keep, give in project_out(
            attn, adapter, a_out, b_out, out_weights, order, row_order, 2
        ):
            came = send(give, to_core)
            parts = [keep, came]
            for k in range(1, Y):
                rows = slice(k * piece, (k + 1) * piece)
                pair = (keep[rows].astype(F32) + came[rows].astype(F32)).astype(BF16)
                parts.append(send(pair, from_y[k]))
            sums.append(parts)
        hidden_state, normed2 = residual_norm(tokens, ints([t]), order, sums)

        rows = [normed2] + [send(normed2, to_xz[o]) for o in others]
        rows = rows + [send(row, to_core) for row in rows]
        adapters = jnp.stack(near_adapters)
        adapters = jnp.concatenate(
            [cut(adapters, (y * 2 + (c ^ s)) * piece, piece, 1).reshape(-1) for s in (0, 1)]
        )
        keys = [(*o, h) for h in range(ZH) for o in near]
        gu_order = ints([((zh + h) % ZH) * 4 + (zl ^ j) * 2 + (x ^ i) for i, j, h in keys])
        sets = [([gu[(*key, k)] for key in keys], b_gu[k], a_dn[k]) for k in range(Y)]
        hidden, low_down = gated(rows, adapters, a_gate, a_up, sets, gu_order)
        down_order = ints([(zl ^ j) * 2 + (x ^ i) for i, j in near])
        pieces, places = [], []
        for h in range(ZH):
            at = ((zh + h) % ZH) * span
            blocks = [[down[(*o, h, k)] for k in range(Y)] for o in near]
            keep, give = project_down(hidden, low_down, cut(b_down, at, span, 1), blocks, down_order)
            came = send(give, to_core)
            total = cut(hidden_state, at, span, 1)
            total = total + keep[:piece].astype(F32) + came[:piece].astype(F32)
            for n, o in enumerate(others):
                part = slice((n + 1) * piece, (n + 2) * piece)
                pair = (keep[part].astype(F32) + came[part].astype(F32)).astype(BF16)
                total = total + send(pair, to_xz[o]).astype(F32)
            done = total.astype(BF16)
            for k in range(Y):
                here = done if k == 0 else send(done, from_y[k])
                for s, got in ((0, here), (1, send(here, to_core))):
                    pieces.append(got)
                    places += [((y + k) % Y) * 2 + (c ^ s), (zh + h) % ZH]
        return assemble(pieces, ints(places), tokens.shape)

    return body


def solution(mesh):
    in_specs = (
        P("req", None),
        P("req", None),
        P("req", None),
        P("req", None, "tp"),
        P("tp", "req"),
        P("req", "tp"),
        P("req", "tp"),
        P("tp", "req"),
        P(),
        P(None, None, "tp"),
        P("tp", None),
        P(),
        P(),
        P(None, "tp"),
        P(),
        P(None, "tp"),
        P("tp", None),
        P(),
    )
    return jax.shard_map(
        make_body(mesh.shape["req"], mesh.shape["tp"]),
        mesh=mesh, in_specs=in_specs, out_specs=P("req", None), check_vma=False,
    )
```

time: 672 us -> 622 us (0.926); the launches traced: 663 us -> 622 us
  Pallas kernels: 0 us -> 183 us
  local copies, waits for them, and re-layouts: 126 us -> 19.9 us
  matrix products: 90.9 us -> 1.76 us
  other arithmetic: 49.4 us -> 18.2 us
  starting transfers between devices: 65.9 us -> 76.7 us
  waiting for transfers between devices: 329 us -> 321 us
    pallas_call x0 -> x8, Pallas kernels: none -> 183 us  [the longest x1 97.1 us: assemble(): pl.pallas_call(kernel, in_specs=[pl.BlockSpec(memory_space=pltpu.SMEM)] +...]
    dot_general x26 -> x1, matrix products: 77.2 us -> 1.76 us  [dot(): return jnp.dot(a, b, preferred_element_type=F32)]
    unnamed x117 -> x148, local copies, waits for them, and re-layouts: 60.6 us -> 5.12 us
    dynamic_update_slice x6 -> x0, local copies, waits for them, and re-layouts: 30.3 us -> none  [the longest x4 19.7 us: body(): out = lax.dynamic_update_slice(out, there, (row + (1 - c) * piece, at))]
    concatenate x7 -> x0, local copies, waits for them, and re-layouts: 11 us -> none  [the longest x1 4.09 us: body(): rows = jnp.concatenate([rows, send(rows, to_core)], axis=0)]
    ppermute x55 -> x78, starting transfers between devices: 65.9 us -> 76.7 us  [send(): return lax.ppermute(value, AXES, pairs)]
    slice x8 -> x4, local copies, waits for them, and re-layouts: 11 us -> 1.35 us  [the longest x2 1.33 us: columns_halved(): return (w[:, :w.shape[1] // 2], w[:, w.shape[1] // 2:])]
    sub x1 -> x0, matrix products: 8.89 us -> none  [attend(): expo = jnp.exp(scores - top_score)]
  transfers between devices with their start and end apart: 55 -> 78, of which waited for: 24 -> 36; matrix products, arithmetic and copies ran while one was open for 30% -> 5% of each run, Pallas kernels for 0% -> 12%
where the time goes in v2:
time: 622 us
  waiting for transfers between devices  321 us (52%)
  Pallas kernels  183 us (29%)
  starting transfers between devices  76.7 us (12%)
  local copies, waits for them, and re-layouts  19.9 us (3%)
  other arithmetic  18.2 us (3%)
    ppermute x78, waiting for transfers between devices, send(): return lax.ppermute(value, AXES, pairs)  321 us
    pallas_call x1, Pallas kernels, assemble(): pl.pallas_call(kernel, in_specs=[pl.BlockSpec(memory_space=pltpu.SMEM)] +...  97.1 us
    ppermute x78, starting transfers between devices, send(): return lax.ppermute(value, AXES, pairs)  76.7 us
    pallas_call x1, Pallas kernels, gated(): pl.pallas_call(kernel, in_specs=[smem, vmem, vmem, vmem] + [hbm] * (n_row...  31.6 us
    pallas_call x2, Pallas kernels, project_down(): pl.pallas_call(kernel, in_specs=[smem] + [vmem] * (3 + len(flat)), out_sp...  22.2 us
    pallas_call x1, Pallas kernels, project_qkv(): pl.pallas_call(kernel, grid_spec=pltpu.PrefetchScalarGridSpec(num_scalar_...  12.8 us
  transfers between devices with their start and end apart: 78, of which 36 were waited for; matrix products, arithmetic and copies ran while one was open for 5% of the time, Pallas kernels for 12%

profile of v2, /device:TPU:0, one launch (start us, length us, event | category | flops | bytes accessed | tf_op | source)
XLA Modules:
  0.0 621.8 jit_solution(9813457280604554985)
XLA Ops:
  21.2 9.5 %collective-permute-done.1.refs_2_ = bf16[256,1536]{1,0:T(8,128)(2,1)S(1)} collective-permute-done((bf16[256,1536]{1,0:T(8,128)(2,1)S(1)}, bf16[256,1536]{1,0:T(8,128)(2,1)S(1)}, u32[]{:S(2)}, u32[]{:S(2)}) %collective-permute-start.1) | collective-permute-done | bytes 786464 | tf_op jit(solution)/shard_map/ppermute | solution.py:443
  32.3 14.3 %collective-permute-done.3.refs_8_ = bf16[256,1536]{1,0:T(8,128)(2,1)} collective-permute-done((bf16[256,1536]{1,0:T(8,128)(2,1)S(1)}, bf16[256,1536]{1,0:T(8,128)(2,1)}, u32[]{:S(2)}, u32[]{:S(2)}) %collective-permute-start.3) | collective-permute-done | bytes 786464 | tf_op jit(solution)/shard_map/ppermute | solution.py:443
  56.7 11.4 %collective-permute-done.63.refs_0_ = bf16[512,256]{1,0:T(8,128)(2,1)S(1)} collective-permute-done((bf16[512,256]{1,0:T(8,128)(2,1)S(1)}, bf16[512,256]{1,0:T(8,128)(2,1)S(1)}, u32[]{:S(2)}, u32[]{:S(2)}) %collective-permute-start.63) | collective-permute-done | bytes 262176 | tf_op jit(solution)/shard_map/ppermute | solution.py:443
  73.9 12.1 %collective-permute-done.10.refs_2_ = bf16[512,256]{1,0:T(8,128)(2,1)S(1)} collective-permute-done((bf16[512,256]{1,0:T(8,128)(2,1)}, bf16[512,256]{1,0:T(8,128)(2,1)S(1)}, u32[]{:S(2)}, u32[]{:S(2)}) %collective-permute-start.10) | collective-permute-done | bytes 262176 | tf_op jit(solution)/shard_map/ppermute | solution.py:443
  116.7 19.0 %collective-permute-done.17.refs_9_ = bf16[512,256]{1,0:T(8,128)(2,1)S(1)} collective-permute-done((bf16[512,256]{1,0:T(8,128)(2,1)S(1)}, bf16[512,256]{1,0:T(8,128)(2,1)S(1)}, u32[]{:S(2)}, u32[]{:S(2)}) %collective-permute-start.17) | collective-permute-done | bytes 262176 | tf_op jit(solution)/shard_map/ppermute | solution.py:443
  137.1 12.6 %collective-permute-done.6.refs_6_ = bf16[256,768]{1,0:T(8,128)(2,1)S(1)} collective-permute-done((bf16[256,768]{1,0:T(8,128)(2,1)S(1)}, bf16[256,768]{1,0:T(8,128)(2,1)S(1)}, u32[]{:S(2)}, u32[]{:S(2)}) %collective-permute-start.6) | collective-permute-done | bytes 393248 | tf_op jit(solution)/shard_map/ppermute | solution.py:443
  149.7 12.0 %collective-permute-done.7.refs_7_ = bf16[256,768]{1,0:T(8,128)(2,1)S(1)} collective-permute-done((bf16[256,768]{1,0:T(8,128)(2,1)S(1)}, bf16[256,768]{1,0:T(8,128)(2,1)S(1)}, u32[]{:S(2)}, u32[]{:S(2)}) %collective-permute-start.7) | collective-permute-done | bytes 393248 | tf_op jit(solution)/shard_map/ppermute | solution.py:443
  165.0 9.0 %collective-permute-start.35 = (bf16[256,1024]{1,0:T(8,128)(2,1)S(1)}, bf16[256,1024]{1,0:T(8,128)(2,1)S(1)}, u32[]{:S(2)}, u32[]{:S(2)}) collective-permute-start(bf16[256,1024]{1,0:T(8,128)(2,1)S(1)} %pad_maximum_fusion.refs_8_), channel_id=1, source_target_pairs={{0,16},{1,17},{2,18},{3,19},{4,20},{5,21},{6,22},{7,23},{8,24},{9,... | collective-permute-start | bytes 1572872 | tf_op jit(solution)/shard_map/ppermute | solution.py:443
  179.3 12.8 %project_qkv.1.q.k.v = bf16[768,1536]{1,0:T(8,128)(2,1)} custom-call(s32[8]{0:T(128)} %stack.147.order_ref, bf16[768,2048]{1,0:T(8,128)(2,1)} %copy-done.3, bf16[768,256]{1,0:T(8,128)(2,1)} %fusion.4.low_ref, bf16[256,1536]{1,0:T(8,128)(2,1)} %copy.36.b_ref, f32[768,128]{1,0:T(8,128)} %get-tuple-element.60.cos_ref, f32[768,128]{1,0:T(8,128)} %get-tuple-element.61.sin_ref, ...), custom_call_target="tpu_custom_call" | custom-call | flops 1000 | bytes 1000 | tf_op jit(solution)/shard_map/project_qkv/pallas_call | solution.py:114
  193.0 8.5 %attend.1.attn_ref = bf16[768,512]{1,0:T(8,128)(2,1)} custom-call(bf16[768,1536]{1,0:T(8,128)(2,1)} %project_qkv.1.q.k.v, bf16[768,1536]{1,0:T(8,128)(2,1)} %project_qkv.1.q.k.v, bf16[768,1536]{1,0:T(8,128)(2,1)} %project_qkv.1.q.k.v, s32[768,1]{1,0:T(8,128)} %broadcast_in_dim.59.column_ref, s32[1,768]{1,0:T(1,128)} %broadcast_in_dim.56.line_ref), custom_call_target="tpu_custom_call" | custom-call | flops 1000 | bytes 1000 | tf_op jit(solution)/shard_map/attend/pallas_call | solution.py:156
  211.5 12.4 %collective-permute-done.39.refs_16_ = bf16[256,1024]{1,0:T(8,128)(2,1)S(1)} collective-permute-done((bf16[256,1024]{1,0:T(8,128)(2,1)S(1)}, bf16[256,1024]{1,0:T(8,128)(2,1)S(1)}, u32[]{:S(2)}, u32[]{:S(2)}) %collective-permute-start.39) | collective-permute-done | bytes 524320 | tf_op jit(solution)/shard_map/ppermute | solution.py:443
  224.0 10.8 %collective-permute-done.47.refs_25_ = bf16[256,1024]{1,0:T(8,128)(2,1)S(1)} collective-permute-done((bf16[256,1024]{1,0:T(8,128)(2,1)S(1)}, bf16[256,1024]{1,0:T(8,128)(2,1)S(1)}, u32[]{:S(2)}, u32[]{:S(2)}) %collective-permute-start.47) | collective-permute-done | bytes 524320 | tf_op jit(solution)/shard_map/ppermute | solution.py:443
  239.5 38.0 %collective-permute-done.67.refs_4_ = bf16[512,256]{1,0:T(8,128)(2,1)S(1)} collective-permute-done((bf16[512,256]{1,0:T(8,128)(2,1)S(1)}, bf16[512,256]{1,0:T(8,128)(2,1)S(1)}, u32[]{:S(2)}, u32[]{:S(2)}) %collective-permute-start.67) | collective-permute-done | bytes 262176 | tf_op jit(solution)/shard_map/ppermute | solution.py:443
  285.5 20.1 %collective-permute-done.37.refs_14_ = bf16[256,1024]{1,0:T(8,128)(2,1)S(1)} collective-permute-done((bf16[256,1024]{1,0:T(8,128)(2,1)}, bf16[256,1024]{1,0:T(8,128)(2,1)S(1)}, u32[]{:S(2)}, u32[]{:S(2)}) %collective-permute-start.37) | collective-permute-done | bytes 524320 | tf_op jit(solution)/shard_map/ppermute | solution.py:443
  321.2 10.8 %collective-permute-done.42.refs_19_ = bf16[256,1024]{1,0:T(8,128)(2,1)} collective-permute-done((bf16[256,1024]{1,0:T(8,128)(2,1)}, bf16[256,1024]{1,0:T(8,128)(2,1)}, u32[]{:S(2)}, u32[]{:S(2)}) %collective-permute-start.42) | collective-permute-done | bytes 524320 | tf_op jit(solution)/shard_map/ppermute | solution.py:443
  332.0 11.2 %collective-permute-done.43.refs_20_ = bf16[256,1024]{1,0:T(8,128)(2,1)} collective-permute-done((bf16[256,1024]{1,0:T(8,128)(2,1)S(1)}, bf16[256,1024]{1,0:T(8,128)(2,1)}, u32[]{:S(2)}, u32[]{:S(2)}) %collective-permute-start.43) | collective-permute-done | bytes 524320 | tf_op jit(solution)/shard_map/ppermute | solution.py:443
  343.7 10.6 %collective-permute-done.44.refs_21_ = bf16[256,1024]{1,0:T(8,128)(2,1)S(1)} collective-permute-done((bf16[256,1024]{1,0:T(8,128)(2,1)S(1)}, bf16[256,1024]{1,0:T(8,128)(2,1)S(1)}, u32[]{:S(2)}, u32[]{:S(2)}) %collective-permute-start.44) | collective-permute-done | bytes 524320 | tf_op jit(solution)/shard_map/ppermute | solution.py:443
  355.0 9.2 %collective-permute-done.45.refs_22_ = bf16[256,1024]{1,0:T(8,128)(2,1)S(1)} collective-permute-done((bf16[256,1024]{1,0:T(8,128)(2,1)S(1)}, bf16[256,1024]{1,0:T(8,128)(2,1)S(1)}, u32[]{:S(2)}, u32[]{:S(2)}) %collective-permute-start.45) | collective-permute-done | bytes 524320 | tf_op jit(solution)/shard_map/ppermute | solution.py:443
  368.1 9.1 %collective-permute-done.46.refs_23_ = bf16[256,1024]{1,0:T(8,128)(2,1)} collective-permute-done((bf16[256,1024]{1,0:T(8,128)(2,1)}, bf16[256,1024]{1,0:T(8,128)(2,1)}, u32[]{:S(2)}, u32[]{:S(2)}) %collective-permute-start.46) | collective-permute-done | bytes 524320 | tf_op jit(solution)/shard_map/ppermute | solution.py:443
  382.7 31.6 %gated.1 = (bf16[1536,1024]{1,0:T(8,128)(2,1)}, bf16[1536,256]{1,0:T(8,128)(2,1)}) custom-call(s32[8]{0:T(128)} %stack.165.order_ref, s32[1536,1]{1,0:T(8,128)} %broadcast_in_dim.61.adapter_ref, bf16[2048,256]{1,0:T(8,128)(2,1)} %ag_ref.1, bf16[2048,256]{1,0:T(8,128)(2,1)} %au_ref.1, bf16[192,2048]{1,0:T(8,128)(2,1)} %get-tuple-element.24.refs_0_, ...), custom_call_target="tpu_custom_call" | custom-call | flops 1000 | bytes 1000 | tf_op jit(solution)/shard_map/gated/pallas_call | solution.py:336
  415.3 11.1 %project_down.3 = (bf16[768,1024]{1,0:T(8,128)(2,1)}, bf16[768,1024]{1,0:T(8,128)(2,1)}) custom-call(s32[4]{0:T(128)} %pad_add_fusion.3.order_ref, bf16[1536,1024]{1,0:T(8,128)(2,1)} %get-tuple-element.25.h_ref, bf16[1536,256]{1,0:T(8,128)(2,1)} %get-tuple-element.26.low_ref, bf16[256,1024]{1,0:T(8,128)(2,1)} %get-tuple-element.41.b_ref, ...), custom_call_target="tpu_custom_call" | custom-call | flops 1000 | bytes 1000 | tf_op jit(solution)/shard_map/project_down/pallas_call | solution.py:387
  452.6 11.2 %project_down.2 = (bf16[768,1024]{1,0:T(8,128)(2,1)}, bf16[768,1024]{1,0:T(8,128)(2,1)}) custom-call(s32[4]{0:T(128)} %pad_add_fusion.3.order_ref, bf16[1536,1024]{1,0:T(8,128)(2,1)} %get-tuple-element.25.h_ref, bf16[1536,256]{1,0:T(8,128)(2,1)} %get-tuple-element.26.low_ref, bf16[256,1024]{1,0:T(8,128)(2,1)} %get-tuple-element.42.b_ref, ...), custom_call_target="tpu_custom_call" | custom-call | flops 1000 | bytes 1000 | tf_op jit(solution)/shard_map/project_down/pallas_call | solution.py:387
  505.6 9.4 %collective-permute-done.61.refs_2_ = bf16[192,1024]{1,0:T(8,128)(2,1)S(1)} collective-permute-done((bf16[192,1024]{1,0:T(8,128)(2,1)S(1)}, bf16[192,1024]{1,0:T(8,128)(2,1)S(1)}, u32[]{:S(2)}, u32[]{:S(2)}) %collective-permute-start.61) | collective-permute-done | bytes 393248 | tf_op jit(solution)/shard_map/ppermute | solution.py:443
  524.4 97.1 %assemble.1 = bf16[768,2048]{1,0:T(8,128)(2,1)} custom-call(s32[16]{0:T(128)} %stack.137.places_ref, bf16[192,1024]{1,0:T(8,128)(2,1)} %copy-done.15, bf16[192,1024]{1,0:T(8,128)(2,1)} %copy-done.42, bf16[192,1024]{1,0:T(8,128)(2,1)} %copy-done.40, bf16[192,1024]{1,0:T(8,128)(2,1)} %collective-permute-done.62.refs_3_, bf16[192,1024]{1,0:T(8,128)(2,1)} %copy-done.14, ...), custom_call_target="tpu_custom_call" | custom-call | flops 1000 | bytes 1000 | tf_op jit(solution)/shard_map/assemble/pallas_call | solution.py:417
  (342 shorter events, 206.8 us)
Async XLA Ops:
  2.4 45.7 %collective-permute-start.24 = (s32[768]{0:T(1024)S(1)}, s32[768]{0:T(1024)S(1)}, u32[]{:S(2)}, u32[]{:S(2)}) collective-permute-start(s32[768]{0:T(1024)S(1)} %get-tuple-element.32), channel_id=1, source_target_pairs={{0,12},{1,13},{2,14},{3,15},{4,8},{5,9},{6,10},{7,11},{8,4},{9,5},... | collective-permute-start | bytes 9224 | tf_op jit(solution)/shard_map/ppermute | solution.py:443
  6.4 43.2 %collective-permute-start.23 = (s32[768]{0:T(1024)S(1)}, s32[768]{0:T(1024)S(1)}, u32[]{:S(2)}, u32[]{:S(2)}) collective-permute-start(s32[768]{0:T(1024)S(1)} %get-tuple-element.32), channel_id=1, source_target_pairs={{0,8},{1,9},{2,10},{3,11},{4,12},{5,13},{6,14},{7,15},{8,0},{9,1},... | collective-permute-start | bytes 9224 | tf_op jit(solution)/shard_map/ppermute | solution.py:443
  6.9 43.5 %collective-permute-start.22 = (s32[768]{0:T(1024)S(1)}, s32[768]{0:T(1024)}, u32[]{:S(2)}, u32[]{:S(2)}) collective-permute-start(s32[768]{0:T(1024)S(1)} %get-tuple-element.32), channel_id=1, source_target_pairs={{0,4},{1,5},{2,6},{3,7},{4,0},{5,1},{6,2},{7,3},{8,12},{9,13},{10,... | collective-permute-start | bytes 9224 | tf_op jit(solution)/shard_map/ppermute | solution.py:443
  30.8 55.9 %collective-permute-start = (bf16[256,1536]{1,0:T(8,128)(2,1)S(1)}, bf16[256,1536]{1,0:T(8,128)(2,1)S(1)}, u32[]{:S(2)}, u32[]{:S(2)}) collective-permute-start(bf16[256,1536]{1,0:T(8,128)(2,1)S(1)} %copy.37.refs_0_), channel_id=1, source_target_pairs={{0,4},{1,5},{2,6},{3,7},{4,0},{5,1},{6,2},{7,3},{8,12},{9,13},{10,... | collective-permute-start | bytes 2359304 | tf_op jit(solution)/shard_map/ppermute | solution.py:443
  86.0 51.0 %collective-permute-start.2 = (bf16[256,1536]{1,0:T(8,128)(2,1)S(1)}, bf16[256,1536]{1,0:T(8,128)(2,1)S(1)}, u32[]{:S(2)}, u32[]{:S(2)}) collective-permute-start(bf16[256,1536]{1,0:T(8,128)(2,1)S(1)} %collective-permute-done.1.refs_2_), channel_id=1, source_target_pairs={{0,4},{1,5},{2,6},{3,7},{4,0},{5,1},{6,2},{7,3},{8,12},{9,13},{10,... | collective-permute-start | bytes 2359304 | tf_op jit(solution)/shard_map/ppermute | solution.py:443
  100.9 64.1 %collective-permute-start.8 = (bf16[256,1536]{1,0:T(8,128)(2,1)}, bf16[256,1536]{1,0:T(8,128)(2,1)}, u32[]{:S(2)}, u32[]{:S(2)}) collective-permute-start(bf16[256,1536]{1,0:T(8,128)(2,1)} %collective-permute-done.3.refs_8_), channel_id=1, source_target_pairs={{0,4},{1,5},{2,6},{3,7},{4,0},{5,1},{6,2},{7,3},{8,12},{9,13},{10,... | collective-permute-start | bytes 2359304 | tf_op jit(solution)/shard_map/ppermute | solution.py:443
  113.2 36.5 %collective-permute-start.6 = (bf16[256,768]{1,0:T(8,128)(2,1)S(1)}, bf16[256,768]{1,0:T(8,128)(2,1)S(1)}, u32[]{:S(2)}, u32[]{:S(2)}) collective-permute-start(bf16[256,768]{1,0:T(8,128)(2,1)S(1)} %collective-permute-done.4.refs_4_), channel_id=1, source_target_pairs={{0,4},{1,5},{2,6},{3,7},{4,0},{5,1},{6,2},{7,3},{8,12},{9,13},{10,... | collective-permute-start | bytes 1179656 | tf_op jit(solution)/shard_map/ppermute | solution.py:443
  113.8 47.9 %collective-permute-start.7 = (bf16[256,768]{1,0:T(8,128)(2,1)S(1)}, bf16[256,768]{1,0:T(8,128)(2,1)S(1)}, u32[]{:S(2)}, u32[]{:S(2)}) collective-permute-start(bf16[256,768]{1,0:T(8,128)(2,1)S(1)} %collective-permute-done.5.refs_5_), channel_id=1, source_target_pairs={{0,4},{1,5},{2,6},{3,7},{4,0},{5,1},{6,2},{7,3},{8,12},{9,13},{10,... | collective-permute-start | bytes 1179656 | tf_op jit(solution)/shard_map/ppermute | solution.py:443
  135.7 73.5 %collective-permute-start.32 = (bf16[256,1024]{1,0:T(8,128)(2,1)}, bf16[256,1024]{1,0:T(8,128)(2,1)S(1)}, u32[]{:S(2)}, u32[]{:S(2)}) collective-permute-start(bf16[256,1024]{1,0:T(8,128)(2,1)} %pad_maximum_fusion.1), channel_id=1, source_target_pairs={{0,4},{1,5},{2,6},{3,7},{4,0},{5,1},{6,2},{7,3},{8,12},{9,13},{10,... | collective-permute-start | bytes 1572872 | tf_op jit(solution)/shard_map/ppermute | solution.py:443
  137.1 72.8 %collective-permute-start.33 = (bf16[256,1024]{1,0:T(8,128)(2,1)}, bf16[256,1024]{1,0:T(8,128)(2,1)}, u32[]{:S(2)}, u32[]{:S(2)}) collective-permute-start(bf16[256,1024]{1,0:T(8,128)(2,1)} %pad_maximum_fusion.2), channel_id=1, source_target_pairs={{0,8},{1,9},{2,10},{3,11},{4,12},{5,13},{6,14},{7,15},{8,0},{9,1},... | collective-permute-start | bytes 1572872 | tf_op jit(solution)/shard_map/ppermute | solution.py:443
  149.7 61.7 %collective-permute-start.34 = (bf16[256,1024]{1,0:T(8,128)(2,1)}, bf16[256,1024]{1,0:T(8,128)(2,1)}, u32[]{:S(2)}, u32[]{:S(2)}) collective-permute-start(bf16[256,1024]{1,0:T(8,128)(2,1)} %pad_maximum_fusion.3), channel_id=1, source_target_pairs={{0,12},{1,13},{2,14},{3,15},{4,8},{5,9},{6,10},{7,11},{8,4},{9,5},... | collective-permute-start | bytes 1572872 | tf_op jit(solution)/shard_map/ppermute | solution.py:443
  161.7 46.3 %collective-permute-start.54 = (bf16[512,256]{1,0:T(8,128)(2,1)}, bf16[512,256]{1,0:T(8,128)(2,1)}, u32[]{:S(2)}, u32[]{:S(2)}) collective-permute-start(bf16[512,256]{1,0:T(8,128)(2,1)} %get-tuple-element.43), channel_id=1, source_target_pairs={{0,12},{1,13},{2,14},{3,15},{4,8},{5,9},{6,10},{7,11},{8,4},{9,5},... | collective-permute-start | bytes 786440 | tf_op jit(solution)/shard_map/ppermute | solution.py:443
  165.0 46.4 %collective-permute-start.35 = (bf16[256,1024]{1,0:T(8,128)(2,1)S(1)}, bf16[256,1024]{1,0:T(8,128)(2,1)S(1)}, u32[]{:S(2)}, u32[]{:S(2)}) collective-permute-start(bf16[256,1024]{1,0:T(8,128)(2,1)S(1)} %pad_maximum_fusion.refs_8_), channel_id=1, source_target_pairs={{0,16},{1,17},{2,18},{3,19},{4,20},{5,21},{6,22},{7,23},{8,24},{9,... | collective-permute-start | bytes 1572872 | tf_op jit(solution)/shard_map/ppermute | solution.py:443
  211.4 71.7 %collective-permute-start.20 = (bf16[384,1024]{1,0:T(8,128)(2,1)}, bf16[384,1024]{1,0:T(8,128)(2,1)S(1)}, u32[]{:S(2)}, u32[]{:S(2)}) collective-permute-start(bf16[384,1024]{1,0:T(8,128)(2,1)} %get-tuple-element.22), channel_id=1, source_target_pairs={{0,1},{1,0},{2,3},{3,2},{4,5},{5,4},{6,7},{7,6},{8,9},{9,8},{10,11... | collective-permute-start | bytes 2359304 | tf_op jit(solution)/shard_map/ppermute | solution.py:443
  224.0 59.9 %collective-permute-start.36 = (bf16[256,1024]{1,0:T(8,128)(2,1)S(1)}, bf16[256,1024]{1,0:T(8,128)(2,1)S(1)}, u32[]{:S(2)}, u32[]{:S(2)}) collective-permute-start(bf16[256,1024]{1,0:T(8,128)(2,1)S(1)} %collective-permute-done.32.refs_9_), channel_id=1, source_target_pairs={{0,16},{1,17},{2,18},{3,19},{4,20},{5,21},{6,22},{7,23},{8,24},{9,... | collective-permute-start | bytes 1572872 | tf_op jit(solution)/shard_map/ppermute | solution.py:443
  234.8 42.8 %collective-permute-start.67 = (bf16[512,256]{1,0:T(8,128)(2,1)S(1)}, bf16[512,256]{1,0:T(8,128)(2,1)S(1)}, u32[]{:S(2)}, u32[]{:S(2)}) collective-permute-start(bf16[512,256]{1,0:T(8,128)(2,1)S(1)} %copy-done.53), channel_id=1, source_target_pairs={{0,16},{1,17},{2,18},{3,19},{4,20},{5,21},{6,22},{7,23},{8,24},{9,... | collective-permute-start | bytes 786440 | tf_op jit(solution)/shard_map/ppermute | solution.py:443
  234.8 48.4 %collective-permute-start.69 = (bf16[512,256]{1,0:T(8,128)(2,1)}, bf16[512,256]{1,0:T(8,128)(2,1)S(1)}, u32[]{:S(2)}, u32[]{:S(2)}) collective-permute-start(bf16[512,256]{1,0:T(8,128)(2,1)} %collective-permute-done.54.refs_6_), channel_id=1, source_target_pairs={{0,16},{1,17},{2,18},{3,19},{4,20},{5,21},{6,22},{7,23},{8,24},{9,... | collective-permute-start | bytes 786440 | tf_op jit(solution)/shard_map/ppermute | solution.py:443
  237.7 67.9 %collective-permute-start.37 = (bf16[256,1024]{1,0:T(8,128)(2,1)}, bf16[256,1024]{1,0:T(8,128)(2,1)S(1)}, u32[]{:S(2)}, u32[]{:S(2)}) collective-permute-start(bf16[256,1024]{1,0:T(8,128)(2,1)} %collective-permute-done.33.refs_10_), channel_id=1, source_target_pairs={{0,16},{1,17},{2,18},{3,19},{4,20},{5,21},{6,22},{7,23},{8,24},{9,... | collective-permute-start | bytes 1572872 | tf_op jit(solution)/shard_map/ppermute | solution.py:443
  277.5 39.9 %collective-permute-start.40 = (bf16[256,1024]{1,0:T(8,128)(2,1)S(1)}, bf16[256,1024]{1,0:T(8,128)(2,1)S(1)}, u32[]{:S(2)}, u32[]{:S(2)}) collective-permute-start(bf16[256,1024]{1,0:T(8,128)(2,1)S(1)} %collective-permute-done.32.refs_9_), channel_id=1, source_target_pairs={{0,2},{1,3},{2,0},{3,1},{4,6},{5,7},{6,4},{7,5},{8,10},{9,11},{10,... | collective-permute-start | bytes 1572872 | tf_op jit(solution)/shard_map/ppermute | solution.py:443
  316.7 37.6 %collective-permute-start.25 = (bf16[192,2048]{1,0:T(8,128)(2,1)}, bf16[192,2048]{1,0:T(8,128)(2,1)S(1)}, u32[]{:S(2)}, u32[]{:S(2)}) collective-permute-start(bf16[192,2048]{1,0:T(8,128)(2,1)} %get-tuple-element.24.refs_0_), channel_id=1, source_target_pairs={{0,4},{1,5},{2,6},{3,7},{4,0},{5,1},{6,2},{7,3},{8,12},{9,13},{10,... | collective-permute-start | bytes 2359304 | tf_op jit(solution)/shard_map/ppermute | solution.py:443
  317.5 37.5 %collective-permute-start.26 = (bf16[192,2048]{1,0:T(8,128)(2,1)}, bf16[192,2048]{1,0:T(8,128)(2,1)}, u32[]{:S(2)}, u32[]{:S(2)}) collective-permute-start(bf16[192,2048]{1,0:T(8,128)(2,1)} %get-tuple-element.24.refs_0_), channel_id=1, source_target_pairs={{0,8},{1,9},{2,10},{3,11},{4,12},{5,13},{6,14},{7,15},{8,0},{9,1},... | collective-permute-start | bytes 2359304 | tf_op jit(solution)/shard_map/ppermute | solution.py:443
  377.2 37.2 %collective-permute-start.64 = (bf16[512,256]{1,0:T(8,128)(2,1)}, bf16[512,256]{1,0:T(8,128)(2,1)S(1)}, u32[]{:S(2)}, u32[]{:S(2)}) collective-permute-start(bf16[512,256]{1,0:T(8,128)(2,1)} %copy-done.55), channel_id=1, source_target_pairs={{0,2},{1,3},{2,0},{3,1},{4,6},{5,7},{6,4},{7,5},{8,10},{9,11},{10,... | collective-permute-start | bytes 786440 | tf_op jit(solution)/shard_map/ppermute | solution.py:443
  377.7 36.6 %collective-permute-start.66 = (bf16[512,256]{1,0:T(8,128)(2,1)}, bf16[512,256]{1,0:T(8,128)(2,1)S(1)}, u32[]{:S(2)}, u32[]{:S(2)}) collective-permute-start(bf16[512,256]{1,0:T(8,128)(2,1)} %copy-done.56), channel_id=1, source_target_pairs={{0,2},{1,3},{2,0},{3,1},{4,6},{5,7},{6,4},{7,5},{8,10},{9,11},{10,... | collective-permute-start | bytes 786440 | tf_op jit(solution)/shard_map/ppermute | solution.py:443
  426.4 37.5 %collective-permute-start.71 = (bf16[768,1024]{1,0:T(8,128)(2,1)}, bf16[768,1024]{1,0:T(8,128)(2,1)S(1)}, u32[]{:S(2)}, u32[]{:S(2)}) collective-permute-start(bf16[768,1024]{1,0:T(8,128)(2,1)} %get-tuple-element.30), channel_id=1, source_target_pairs={{0,1},{1,0},{2,3},{3,2},{4,5},{5,4},{6,7},{7,6},{8,9},{9,8},{10,11... | collective-permute-start | bytes 4718600 | tf_op jit(solution)/shard_map/ppermute | solution.py:443
  (127 other events, 3873.2 us)

commit v3 on v2

v3 whole, which is shorter than its diff:
```python
import functools
import math

import jax
import jax.numpy as jnp
from jax import lax
from jax.experimental import pallas as pl
from jax.experimental.pallas import tpu as pltpu
from jax.sharding import PartitionSpec as P

HD = 128
RANK = 16
AXES = ("req", "tp")
epsilon = 1e-05
rope_base = 10000.0
F32 = jnp.float32
BF16 = jnp.bfloat16
VM = pltpu.VMEM
PARAMS = pltpu.CompilerParams(vmem_limit_bytes=56 * 2**20)
COST = pl.CostEstimate(flops=1000, bytes_accessed=1000, transcendentals=0)


def dot(a, b):
    return jnp.dot(a, b, preferred_element_type=F32)


def layer_norm(values):
    row_mean = jnp.mean(values, axis=-1, keepdims=True)
    centred = values - row_mean
    spread = jnp.mean(centred * centred, axis=-1, keepdims=True)
    return (centred * lax.rsqrt(spread + epsilon)).astype(BF16)


def slot_layout(lengths_row, adapters_row, slot_count):
    request_ends = jnp.cumsum(lengths_row)
    request_starts = request_ends - lengths_row
    slot_index = jnp.arange(slot_count, dtype=jnp.int32)
    request_of = jnp.sum((slot_index[:, None] >= request_ends[None, :]).astype(jnp.int32), axis=1)
    member = request_of[:, None] == jnp.arange(lengths_row.shape[0], dtype=jnp.int32)[None, :]
    position = slot_index - jnp.sum(jnp.where(member, request_starts[None, :], 0), axis=1)
    adapter = jnp.sum(jnp.where(member, adapters_row[None, :], 0), axis=1)
    return (request_of, position, adapter)


def rope_tables(position):
    half = HD // 2
    frequency = jnp.exp(-math.log(rope_base) * 2.0 * jnp.arange(half, dtype=F32) / HD)
    angles = position.astype(F32)[:, None] * frequency[None, :]
    cosine, sine = jnp.cos(angles), jnp.sin(angles)
    return jnp.concatenate([cosine, cosine], 1), jnp.concatenate([-sine, sine], 1)


def masked(inner, adapter_column):
    rank = lax.broadcasted_iota(jnp.int32, inner.shape, 1) // RANK
    return jnp.where(adapter_column == rank, inner, F32(0.0)).astype(BF16)


def whole(array):
    return pl.BlockSpec(array.shape, lambda *_: (0,) * array.ndim, pipeline_mode=pl.Buffered(1))


def mm(start, size):
    return pl.ds(pl.multiple_of(start * size, size), size)


def dma(source, target, semaphore):
    return pltpu.make_async_copy(source, target, semaphore)


def run_all(copies):
    for copy in copies:
        copy.start()
    for copy in copies:
        copy.wait()


SMEM_SPEC = pl.BlockSpec(memory_space=pltpu.SMEM)
VMEM_SPEC = pl.BlockSpec(memory_space=VM)
HBM_SPEC = pl.BlockSpec(memory_space=pl.ANY)


def project_qkv(own, pieces, adapter, a, b, cosine, sine, weights, places):
    slots, width = own.shape
    total_rows, columns, rank = 2 * slots, b.shape[1], b.shape[0]
    piece, size, tile = pieces[0].shape[0], width // len(weights), columns // 3
    n_pieces, n_weights = len(pieces), len(weights)
    chunk = total_rows // 4
    column = adapter[:, None]

    def kernel(at_ref, adapter_ref, a_ref, cos_ref, sin_ref, own_ref, b_ref, *refs):
        p_in, w_in, rest = refs[:n_pieces], refs[n_pieces : n_pieces + n_weights], refs[-7:]
        out, x, w, bb, low, x_sem, w_sem = rest

        def weight_copies(step, slot):
            to = pl.ds(step * tile, tile)
            for i in range(n_weights):
                yield dma(
                    w_in[i].at[:, to],
                    w.at[slot, mm(at_ref[1 + n_pieces + i], size), :],
                    w_sem.at[slot, i],
                )
            yield dma(b_ref.at[:, to], bb.at[slot], w_sem.at[slot, n_weights])

        x_copies = [dma(own_ref, x.at[mm(at_ref[0], slots), :], x_sem.at[n_pieces])]
        for i in range(n_pieces):
            x_copies.append(dma(p_in[i], x.at[mm(at_ref[1 + i], piece), :], x_sem.at[i]))
        for copy in x_copies:
            copy.start()
        for copy in weight_copies(0, 0):
            copy.start()
        for copy in x_copies:
            copy.wait()
        for step in range(3):
            slot = step % 2
            if step < 2:
                for copy in weight_copies(step + 1, 1 - slot):
                    copy.start()
            for copy in weight_copies(step, slot):
                copy.wait()

            @pl.loop(0, total_rows // chunk)
            def _(m):
                at = mm(m, chunk)
                xs = x[at, :]
                if step == 0:
                    low[at, :] = masked(dot(xs, a_ref[...]), adapter_ref[at, :])
                total = dot(xs, w[slot]) + dot(low[at, :], bb[slot])
                for h in range(tile // HD):
                    v = total[:, h * HD : (h + 1) * HD]
                    if step < 2:
                        v = v * cos_ref[at, :] + pltpu.roll(v, HD // 2, 1) * sin_ref[at, :]
                    start = step * tile + h * HD
                    out[at, start : start + HD] = v.astype(BF16)

    return pl.pallas_call(
        kernel,
        in_specs=[SMEM_SPEC] + [VMEM_SPEC] * 4 + [HBM_SPEC] * (2 + n_pieces + n_weights),
        out_specs=VMEM_SPEC,
        out_shape=jax.ShapeDtypeStruct((total_rows, columns), BF16),
        scratch_shapes=[
            VM((total_rows, width), BF16),
            VM((2, width, tile), BF16),
            VM((2, rank, tile), BF16),
            VM((total_rows, rank), BF16),
            pltpu.SemaphoreType.DMA((n_pieces + 1,)),
            pltpu.SemaphoreType.DMA((2, n_weights + 1)),
        ],
        compiler_params=PARAMS,
        cost_estimate=COST,
        name="project_qkv",
    )(places, column, a, cosine, sine, own, b, *pieces, *weights)


def attend(qkv, request_of):
    indices, slots = request_of.shape
    heads = qkv.shape[1] // 3 // HD
    rows = 256 if slots % 256 == 0 else slots
    column, line = request_of[:, :, None], request_of[:, None, :]

    def kernel(q, k, v, column_ref, line_ref, out):
        for at in range(0, slots, rows):
            seen = at + rows
            s = lax.dot_general(
                q[at:seen], k[:seen], (((1,), (1,)), ((), ())), preferred_element_type=F32
            )
            s = s * (1.0 / math.sqrt(HD))
            here = at + lax.broadcasted_iota(jnp.int32, s.shape, 0)
            there = lax.broadcasted_iota(jnp.int32, s.shape, 1)
            allowed = (column_ref[0, at:seen] == line_ref[0, :, :seen]) & (here >= there)
            s = jnp.where(allowed, s, F32(-1e30))
            e = jnp.exp(s - jnp.max(s, axis=1, keepdims=True))
            weights = (e * (1.0 / jnp.sum(e, axis=1, keepdims=True))).astype(BF16)
            out[at:seen] = dot(weights, v[:seen]).astype(BF16)

    return pl.pallas_call(
        kernel,
        grid=(indices, heads),
        in_specs=[
            pl.BlockSpec((slots, HD), lambda i, h: (i, h)),
            pl.BlockSpec((slots, HD), lambda i, h: (i, heads + h)),
            pl.BlockSpec((slots, HD), lambda i, h: (i, 2 * heads + h)),
            pl.BlockSpec((1, slots, 1), lambda i, h: (i, 0, 0)),
            pl.BlockSpec((1, 1, slots), lambda i, h: (i, 0, 0)),
        ],
        out_specs=pl.BlockSpec((slots, HD), lambda i, h: (i, h)),
        out_shape=jax.ShapeDtypeStruct((indices * slots, heads * HD), BF16),
        compiler_params=PARAMS,
        cost_estimate=COST,
        name="attend",
    )(qkv, qkv, qkv, column, line)


def project_out(attn, adapter, a, b, weights, order, scalars, T, chunks):
    total_rows, depth = attn.shape
    width = b.shape[1]
    n, slots, piece = len(weights), total_rows // 2, total_rows // 2 // T
    size = width // n // 2
    flat = [p for w in weights for p in w]
    column = adapter[:, None]
    half = total_rows // 2
    shape = jax.ShapeDtypeStruct((half, width // chunks), BF16)

    def kernel(order_ref, at_ref, attn_ref, adapter_ref, a_ref, b_ref, *refs):
        ws, outs = refs[: len(flat)], refs[len(flat) : -2]
        rows, low = refs[-2:]
        x, c = at_ref[0], at_ref[1]
        mine = a_ref[mm(x, depth), :]
        for s in range(2):
            side = c if s == 0 else 1 - c
            for xa in range(2):
                for ya in range(T // 2):
                    here = mm(xa * T + ya * 2 + side, piece)
                    to = s * half + (xa * (T // 2) + ya) * piece
                    part = attn_ref[here, :]
                    rows[to : to + piece] = part
                    low[to : to + piece] = masked(dot(part, mine), adapter_ref[here, :])
        it = iter(ws)
        for k, w in enumerate(weights):
            blocks = []
            for p in w:
                ref = next(it)
                for start in range(0, p.shape[1], size):
                    blocks.append((ref, start))
            chunk, place = divmod(k, n // chunks)
            for i, (ref, start) in enumerate(blocks):
                there = mm(order_ref[2 * k + i], size)
                to = mm(place * 2 + (x ^ i), size)
                for s in range(2):
                    these = slice(s * half, (s + 1) * half)
                    total = dot(rows[these], ref[:, start : start + size])
                    total = total + dot(low[these], b_ref[:, there])
                    outs[2 * chunk + s][:, to] = total.astype(BF16)

    out = pl.pallas_call(
        kernel,
        in_specs=[SMEM_SPEC, SMEM_SPEC] + [VMEM_SPEC] * (4 + len(flat)),
        out_specs=[VMEM_SPEC] * (2 * chunks),
        out_shape=[shape] * (2 * chunks),
        scratch_shapes=[VM(attn.shape, BF16), VM((total_rows, a.shape[1]), BF16)],
        compiler_params=PARAMS,
        cost_estimate=COST,
        name="project_out",
    )(order, scalars, attn, column, a, b, *flat)
    return [(out[2 * i], out[2 * i + 1]) for i in range(chunks)]


def residual_norm(tokens, row, order, chunks, T):
    slots, width = tokens.shape
    n = order.shape[0]
    piece, size, per = slots // T, width // n, n // len(chunks)

    def kernel(row_ref, order_ref, tok_ref, *refs):
        parts, hidden, normed = refs[:-2], refs[-2], refs[-1]
        for c, part in enumerate(parts):
            total = part[:piece].astype(F32)
            for k in range(1, part.shape[0] // piece):
                total = total + part[k * piece : (k + 1) * piece].astype(F32)
            for place in range(per):
                to = mm(order_ref[c * per + place], size)
                more = total[:, place * size : (place + 1) * size]
                hidden[:, to] = tok_ref[:, to].astype(F32) + more
        normed[...] = layer_norm(hidden[...])

    return pl.pallas_call(
        kernel,
        grid_spec=pltpu.PrefetchScalarGridSpec(
            num_scalar_prefetch=2,
            grid=(1,),
            in_specs=[
                pl.BlockSpec((piece, width), lambda n, r, o: (r[0], 0)),
                *[pl.BlockSpec(p.shape, lambda n, r, o: (0, 0)) for p in chunks],
            ],
            out_specs=[pl.BlockSpec((piece, width), lambda n, r, o: (0, 0))] * 2,
        ),
        out_shape=[
            jax.ShapeDtypeStruct((piece, width), F32),
            jax.ShapeDtypeStruct((piece, width), BF16),
        ],
        compiler_params=PARAMS,
        cost_estimate=COST,
        name="residual_norm",
    )(row, order, tokens, *chunks)


def gated(rows, adapters, a_gate, a_up, sets, places):
    width = rows[0].shape[1]
    half = rows[0].shape[0]
    total_rows = half * len(rows)
    units = sets[0][1].shape[1] // 2
    tile = min(256, units)
    tiles = units // tile
    rank = a_gate.shape[1]
    column = adapters[:, None]
    flat = [w for s in sets for w in s[0]]
    first = [sum(len(s[0]) for s in sets[:k]) for k in range(len(sets) + 1)]
    bs = [s[1] for s in sets]
    downs = [s[2] for s in sets]
    n_rows, n_sets = len(rows), len(sets)
    most = max(len(s[0]) for s in sets)
    steps = n_sets * tiles
    chunk = total_rows // 4
    hidden_width = n_sets * units

    def kernel(place_ref, adapter_ref, ag_ref, au_ref, *refs):
        it = iter(refs)
        take = lambda k: [next(it) for _ in range(k)]
        x_in, w_in, b_in, d_in = take(n_rows), take(len(flat)), take(n_sets), take(n_sets)
        hidden, x, w, bb, lg, lu, ld, x_sem, w_sem, b_sem = take(10)

        def weight_copies(step, slot):
            s, t = divmod(step, tiles)
            for g in range(2):
                for i in range(first[s], first[s + 1]):
                    yield dma(
                        w_in[i].at[:, pl.ds(g * units + t * tile, tile)],
                        w.at[slot, g, mm(place_ref[i], flat[i].shape[0]), :],
                        w_sem.at[slot, g, i - first[s]],
                    )
                yield dma(
                    b_in[s].at[:, pl.ds(g * units + t * tile, tile)],
                    bb.at[slot, g],
                    b_sem.at[slot, g],
                )

        x_copies = [dma(x_in[i], x.at[pl.ds(i * half, half), :], x_sem.at[i]) for i in range(n_rows)]
        for copy in x_copies:
            copy.start()
        for copy in weight_copies(0, 0):
            copy.start()
        for copy in x_copies:
            copy.wait()
        for step in range(steps):
            slot = step % 2
            if step + 1 < steps:
                for copy in weight_copies(step + 1, 1 - slot):
                    copy.start()
            for copy in weight_copies(step, slot):
                copy.wait()
            s, t = divmod(step, tiles)

            @pl.loop(0, total_rows // chunk)
            def _(m):
                at = mm(m, chunk)
                xs = x[at, :]
                if step == 0:
                    lg[at, :] = masked(dot(xs, ag_ref[...]), adapter_ref[at, :])
                    lu[at, :] = masked(dot(xs, au_ref[...]), adapter_ref[at, :])
                gate = dot(xs, w[slot, 0]) + dot(lg[at, :], bb[slot, 0])
                up = dot(xs, w[slot, 1]) + dot(lu[at, :], bb[slot, 1])
                h = (gate / (1.0 + jnp.exp(-gate)) * up).astype(BF16)
                hidden[at, step * tile : (step + 1) * tile] = h
                more = dot(h, d_in[s][t * tile : (t + 1) * tile, :])
                if step > 0:
                    more = more + ld[at, :]
                if step < steps - 1:
                    ld[at, :] = more
                else:
                    hidden[at, hidden_width:] = masked(more, adapter_ref[at, :])

    return pl.pallas_call(
        kernel,
        in_specs=[SMEM_SPEC] + [VMEM_SPEC] * 3
        + [HBM_SPEC] * (n_rows + len(flat) + n_sets)
        + [VMEM_SPEC] * n_sets,
        out_specs=VMEM_SPEC,
        out_shape=jax.ShapeDtypeStruct((total_rows, hidden_width + rank), BF16),
        scratch_shapes=[
            VM((total_rows, width), BF16),
            VM((2, 2, width, tile), BF16),
            VM((2, 2, rank, tile), BF16),
            VM((total_rows, rank), BF16),
            VM((total_rows, rank), BF16),
            VM((total_rows, rank), F32),
            pltpu.SemaphoreType.DMA((n_rows,)),
            pltpu.SemaphoreType.DMA((2, 2, most)),
            pltpu.SemaphoreType.DMA((2, 2)),
        ],
        compiler_params=PARAMS,
        cost_estimate=COST,
        name="gated",
    )(places, column, a_gate, a_up, *rows, *flat, *bs, *downs)


def project_down(hidden, b, sets, units, scalars):
    total_rows, depth = hidden.shape
    half = total_rows // 2
    rank = b.shape[0]
    size = sets[0].shape[1]
    n = 4
    n_sets = len(sets)
    chunk = half // 2

    def kernel(at_ref, h_ref, b_ref, *refs):
        w_in, outs, w, sems = refs[:n_sets], refs[n_sets : n_sets + 2], refs[-2], refs[-1]
        copies = [
            dma(
                b_ref.at[:, mm(at_ref[0], n * size)],
                w.at[n_sets * units : n_sets * units + rank, :],
                sems.at[n_sets * n],
            )
        ]
        for at in range(n):
            for k in range(n_sets):
                copies.append(
                    dma(
                        w_in[k].at[mm(at_ref[1 + k] * n + at, units), :],
                        w.at[k * units : (k + 1) * units, at * size : (at + 1) * size],
                        sems.at[k * n + at],
                    )
                )
        run_all(copies)
        for o in range(2):

            @pl.loop(0, half // chunk)
            def _(m):
                hs = h_ref[mm(m + o * (half // chunk), chunk), :]
                for at in range(n):
                    to = slice(at * size, (at + 1) * size)
                    outs[o][mm(m, chunk), to] = dot(hs, w[:, to]).astype(BF16)

    return pl.pallas_call(
        kernel,
        in_specs=[SMEM_SPEC, VMEM_SPEC] + [HBM_SPEC] * (1 + n_sets),
        out_specs=[VMEM_SPEC] * 2,
        out_shape=[jax.ShapeDtypeStruct((half, n * size), BF16)] * 2,
        scratch_shapes=[
            VM((depth, n * size), BF16),
            pltpu.SemaphoreType.DMA((n_sets * n + 1,)),
        ],
        compiler_params=PARAMS,
        cost_estimate=COST,
        name="project_down",
    )(scalars, hidden, b, *sets)


def assemble(pieces, places, shape):
    rows, columns = pieces[0].shape

    def kernel(places_ref, *refs):
        out = refs[-1]
        for i in range(len(pieces)):
            to = mm(places_ref[2 * i], rows), mm(places_ref[2 * i + 1], columns)
            out[to] = refs[i][...]

    return pl.pallas_call(
        kernel,
        in_specs=[SMEM_SPEC] + [VMEM_SPEC] * len(pieces),
        out_specs=VMEM_SPEC,
        out_shape=jax.ShapeDtypeStruct(shape, BF16),
        compiler_params=PARAMS,
        cost_estimate=COST,
        name="assemble",
    )(places, *pieces)


def make_body(R, T):
    Z, ZH, Y = R // 2, R // 4, T // 2

    def flat(z, x, y, c):
        return (z * 2 + x) * T + y * 2 + c

    def move(f):
        every = [(r // 2, r % 2, t // 2, t % 2) for r in range(R) for t in range(T)]
        return [(flat(*d), flat(*f(*d))) for d in every]

    def wait_for(value, after):
        return lax.optimization_barrier((value, *after))[0] if after else value

    def send(value, pairs, after=()):
        return lax.ppermute(wait_for(value, after), AXES, pairs)

    to_core = move(lambda z, x, y, c: (z, x, y, 1 - c))
    to_x = move(lambda z, x, y, c: (z, 1 - x, y, c))
    z_up = move(lambda z, x, y, c: ((z + 1) % Z, x, y, c))
    z_down = move(lambda z, x, y, c: ((z - 1) % Z, x, y, c))
    from_y = {k: move(lambda z, x, y, c, k=k: (z, x, (y - k) % Y, c)) for k in range(1, Y)}
    same_xzl = [[zh * 4 + b for b in range(4)] for zh in range(ZH)]
    same_zh = [[zh * 4 + b for zh in range(ZH)] for b in range(4)]
    same_xy = [
        [flat(z, x, y, c) for x in (0, 1) for y in range(Y)] for z in range(Z) for c in (0, 1)
    ]

    def spread(value, axes, groups, after=()):
        return lax.all_to_all(
            wait_for(value, after), axes, 0, 0, axis_index_groups=groups, tiled=True
        )

    def gather_zh(value, after=()):
        return lax.all_gather(
            wait_for(value, after), "req", axis=0, axis_index_groups=same_zh, tiled=True
        )

    def body(
        tokens, lengths, request_adapter, w_qkv, w_out, w_gate, w_up, w_down,
        a_qkv, b_qkv, a_out, b_out, a_gate, b_gate, a_up, b_up, a_down, b_down,
    ):
        r, t = lax.axis_index("req"), lax.axis_index("tp")
        z, x, y, c = r // 2, r % 2, t // 2, t % 2
        zh, zl = z // 2, z % 2
        slots, width = tokens.shape
        piece = slots // T
        block = width // R
        local = w_qkv.shape[2] // 2
        rank = a_qkv.shape[1]
        quarter = w_gate.shape[1] // 4
        span = width // ZH

        def cut(array, start, size, axis):
            return lax.dynamic_slice_in_dim(array, start, size, axis)

        def ints(values):
            return jnp.stack([jnp.asarray(v, jnp.int32) for v in values])

        both = jnp.concatenate([lengths, request_adapter], axis=1)
        both = lax.all_gather(both, "req", axis=0, axis_index_groups=same_xzl, tiled=True)
        count = lengths.shape[1]
        request_of, position, adapter = jax.vmap(lambda l, a: slot_layout(l, a, slots))(
            both[:, :count], both[:, count:]
        )
        here = lambda v: cut(v, zl * 2, 2, 0)
        cosine, sine = rope_tables(here(position).reshape(-1))

        def heads_of(w, which):
            return cut(w, which * local, local, 2).reshape(w.shape[0], 3 * local)

        qkv = {(0, 0): heads_of(w_qkv, x)}
        qkv[(0, 1)] = send(heads_of(w_qkv, 1 - x), to_x)
        normed = layer_norm(tokens.astype(F32))
        quarter_x = send(cut(normed, t * piece, piece, 0), to_x)
        for i in (0, 1):
            left = right = qkv[(0, i)]
            for k in range(1, Z // 2):
                left, right = send(left, z_up), send(right, z_down)
                qkv[(Z - k, i)], qkv[(k, i)] = left, right
        gu = jnp.concatenate([w_gate.reshape(block, 4, quarter), w_up.reshape(block, 4, quarter)], 2)
        gu = gu.transpose(1, 0, 2).reshape(4 * block, 2 * quarter)
        gu = spread(gu, "req", same_xzl, [qkv[(0, 1)]])
        qkv[(Z // 2, 0)] = send(qkv[(Z // 2 + 1, 0)], z_up)
        qkv[(Z // 2, 1)] = send(qkv[(Z // 2 - 1, 1)], z_down)
        keys = [(k, i) for k in range(Z) for i in (0, 1)]
        order = [((z + k) % Z) * 2 + (x ^ i) for k, i in keys]
        quarters, at = [], []
        for k in range(Y):
            came = quarter_x if k == 0 else send(quarter_x, from_y[k])
            quarters += [came, send(came, to_core)]
            at += [(1 - x) * T + ((y + k) % Y) * 2 + s for s in (c, 1 - c)]

        own = cut(w_out, x * local, local, 0)
        other = send(cut(w_out, (1 - x) * local, local, 0), to_x, [quarter_x])
        left = right = jnp.concatenate([own, other], axis=1)
        late = [qkv[(Z // 2, 0)], qkv[(Z // 2, 1)]]
        out = {0: (left,)}
        for k in range(1, Z // 2):
            left, right = send(left, z_up, late), send(right, z_down, late)
            out[Z - k], out[k] = (left,), (right,)
        out[Z // 2] = (send(left[:, :block], z_up), send(right[:, block:], z_down))

        gu_all = gather_zh(gu, [qkv[(1, 1)], qkv[(Z - 1, 1)]])
        down = spread(w_down, "req", same_xzl, [quarter_x, gu])
        down_all = gather_zh(down)
        mine = (zl * 2 + x) * quarter
        b_own = jnp.concatenate(
            [cut(b_gate, mine, quarter, 1), cut(b_up, mine, quarter, 1)], axis=1
        )
        a_down_own = cut(a_down, mine, quarter, 0)
        sets = [([gu_all], b_own, a_down_own)]
        places = [0]
        down_sets = [[(down, 0)]] + [[(down_all, (zh + h) % ZH)] for h in range(1, ZH)]
        for k in range(1, Y):
            first = send(gu, from_y[k])
            ends = send(b_own, from_y[k]), send(a_down_own, from_y[k])
            down_sets[0].append((send(down, from_y[k]), 0))
            relayed = [first]
            places.append(zh)
            for h in range(1, ZH):
                there = (zh + h) % ZH
                relayed.append(send(cut(gu_all, there * gu.shape[0], gu.shape[0], 0), from_y[k]))
                places.append(there)
                part = cut(down_all, there * down.shape[0], down.shape[0], 0)
                down_sets[h].append((send(part, from_y[k]), 0))
            sets.append((relayed, *ends))

        two = here(adapter).reshape(-1)
        b_heads = heads_of(b_qkv, x)
        joined = project_qkv(
            normed, quarters, two, a_qkv, b_heads, cosine, sine,
            [qkv[key] for key in keys], ints([x, *at, *order]),
        )
        attn = attend(joined, here(request_of))
        terms = []
        for keep, give in project_out(
            attn, two, a_out, b_out, [out[k] for k in range(Z)], ints(order), ints([x, c]), T, 2
        ):
            pair = keep.astype(F32) + send(give, to_core).astype(F32)
            terms.append(spread(pair.astype(BF16), AXES, same_xy))
        z_order = ints([(z + k) % Z for k in range(Z)])
        hidden_state, normed2 = residual_norm(tokens, ints([t]), z_order, terms, T)

        rows = spread(jnp.concatenate([normed2] * 4, axis=0), "req", same_xzl)
        rows = [rows, send(rows, to_core)]
        adapters = jnp.concatenate(
            [cut(adapter, (y * 2 + (c ^ s)) * piece, piece, 1).reshape(-1) for s in (0, 1)]
        )
        hidden = gated(rows, adapters, a_gate, a_up, sets, ints(places))
        pieces, places = [], []
        for h in range(ZH):
            there = (zh + h) % ZH
            keep, give = project_down(
                hidden, b_down, [w for w, _ in down_sets[h]], quarter,
                ints([there] + [p for _, p in down_sets[h]]),
            )
            pair = keep.astype(F32) + send(give, to_core).astype(F32)
            came = spread(pair.astype(BF16), "req", same_xzl).astype(F32)
            total = cut(hidden_state, there * span, span, 1)
            for b in range(4):
                total = total + came[b * piece : (b + 1) * piece]
            done = total.astype(BF16)
            for k in range(Y):
                there_y = done if k == 0 else send(done, from_y[k])
                for s, got in ((0, there_y), (1, send(there_y, to_core))):
                    pieces.append(got)
                    places += [((y + k) % Y) * 2 + (c ^ s), there]
        return assemble(pieces, ints(places), tokens.shape)

    return body


def solution(mesh):
    in_specs = (
        P("req", None),
        P("req", None),
        P("req", None),
        P("req", None, "tp"),
        P("tp", "req"),
        P("req", "tp"),
        P("req", "tp"),
        P("tp", "req"),
        P(),
        P(None, None, "tp"),
        P("tp", None),
        P(),
        P(),
        P(None, "tp"),
        P(),
        P(None, "tp"),
        P("tp", None),
        P(),
    )
    return jax.shard_map(
        make_body(mesh.shape["req"], mesh.shape["tp"]),
        mesh=mesh, in_specs=in_specs, out_specs=P("req", None), check_vma=False,
    )
```

time: 622 us -> 606 us (0.974)
  Pallas kernels: 183 us -> 96 us
  blocking collectives: 0 us -> 23 us
  other arithmetic: 18.2 us -> 41 us
  local copies, waits for them, and re-layouts: 19.9 us -> 40.5 us
  starting transfers between devices: 76.7 us -> 63.4 us
  between operations: 1.04 us -> 14 us
    ppermute x78 -> x33, waiting for transfers between devices: 321 us -> 114 us  [send(): return lax.ppermute(wait_for(value, after), AXES, pairs)]
    all_to_all x0 -> x7, waiting for transfers between devices: none -> 114 us  [spread(): lax.all_to_all(wait_for(value, after), axes, 0, 0, axis_index_groups=grou...]
    all_gather x0 -> x2, waiting for transfers between devices: none -> 97.5 us  [gather_zh(): lax.all_gather(wait_for(value, after), 'req', axis=0, axis_index_groups=s...]
    pallas_call x7, Pallas kernels: 179 us -> 91.1 us  [the longest x1 30.9 us: gated(): pl.pallas_call(kernel, in_specs=[SMEM_SPEC] + [VMEM_SPEC] * 3 + [HBM_SPEC...]
    ppermute x78 -> x33, starting transfers between devices: 76.7 us -> 35.5 us  [send(): return lax.ppermute(wait_for(value, after), AXES, pairs)]
    all_to_all x0 -> x7, starting transfers between devices: none -> 27.6 us  [spread(): lax.all_to_all(wait_for(value, after), axes, 0, 0, axis_index_groups=grou...]
    all_gather x0 -> x1, blocking collectives: none -> 23 us  [body(): lax.all_gather(both, 'req', axis=0, axis_index_groups=same_xzl, tiled=True)]
    convert_element_type x4 -> x6, other arithmetic: 2.13 us -> 17.4 us  [the longest x4 10.4 us: body(): came = spread(pair.astype(BF16), 'req', same_xzl).astype(F32)]
  transfers between devices with their start and end apart: 78 -> 42, of which waited for: 36 -> 20; matrix products, arithmetic and copies ran while one was open for 5% -> 11% of each run, Pallas kernels for 12% -> 14%
where the time goes in v3:
time: 606 us; the launch traced here: 604 us
  waiting for transfers between devices  326 us (54%)
  Pallas kernels  96 us (16%)
  starting transfers between devices  63.4 us (10%)
  other arithmetic  41 us (7%)
  local copies, waits for them, and re-layouts  40.5 us (7%)
  blocking collectives  23 us (4%)
  between operations  14 us (2%)
    ppermute x33, waiting for transfers between devices, send(): return lax.ppermute(wait_for(value, after), AXES, pairs)  114 us
    all_to_all x7, waiting for transfers between devices, spread(): lax.all_to_all(wait_for(value, after), axes, 0, 0, axis_index_groups=grou...  114 us
    all_gather x2, waiting for transfers between devices, gather_zh(): lax.all_gather(wait_for(value, after), 'req', axis=0, axis_index_groups=s...  97.5 us
    ppermute x33, starting transfers between devices, send(): return lax.ppermute(wait_for(value, after), AXES, pairs)  35.5 us
    pallas_call x1, Pallas kernels, gated(): pl.pallas_call(kernel, in_specs=[SMEM_SPEC] + [VMEM_SPEC] * 3 + [HBM_SPEC...  30.9 us
    all_to_all x7, starting transfers between devices, spread(): lax.all_to_all(wait_for(value, after), axes, 0, 0, axis_index_groups=grou...  27.6 us
    all_gather x1, blocking collectives, body(): lax.all_gather(both, 'req', axis=0, axis_index_groups=same_xzl, tiled=True)  23 us
    pallas_call x1, Pallas kernels, project_qkv(): pl.pallas_call(kernel, in_specs=[SMEM_SPEC] + [VMEM_SPEC] * 4 + [HBM_SPEC...  20.1 us
  transfers between devices with their start and end apart: 42, of which 20 were waited for; matrix products, arithmetic and copies ran while one was open for 11% of the time, Pallas kernels for 14%

profile of v3, /device:TPU:0, one launch (start us, length us, event | category | flops | bytes accessed | tf_op | source)
XLA Modules:
  0.0 604.2 jit_solution(13037807839916458476)
XLA Ops:
  25.5 23.0 %all-gather = s32[4,1,16]{2,1,0:T(1,128)S(1)} all-gather(s32[1,1,16]{2,1,0:T(1,128)S(1)} %add_bitcast_fusion), channel_id=1, replica_groups={{0,4,8,12},{16,20,24,28},{1,5,9,13},{17,21,25,29},{2,6,10,14},{18,22,26..., dimensions={0}, use_global_device_ids=true | all-gather | bytes 320 | tf_op jit(solution)/shard_map/all_gather | solution.py:515
  79.6 16.2 %collective-permute-done.11 = bf16[256,256]{1,0:T(8,128)(2,1)S(1)} collective-permute-done((bf16[256,256]{1,0:T(8,128)(2,1)}, bf16[256,256]{1,0:T(8,128)(2,1)S(1)}, u32[]{:S(2)}, u32[]{:S(2)}) %collective-permute-start.11) | collective-permute-done | bytes 131104 | tf_op jit(solution)/shard_map/ppermute | solution.py:470
  97.3 7.2 %collective-permute-done.8.refs_8_ = bf16[256,768]{1,0:T(8,128)(2,1)S(1)} collective-permute-done((bf16[256,768]{1,0:T(8,128)(2,1)}, bf16[256,768]{1,0:T(8,128)(2,1)S(1)}, u32[]{:S(2)}, u32[]{:S(2)}) %collective-permute-start.8) | collective-permute-done | bytes 393248 | tf_op jit(solution)/shard_map/ppermute | solution.py:470
  104.6 6.1 %collective-permute-done.9.refs_9_ = bf16[256,768]{1,0:T(8,128)(2,1)S(1)} collective-permute-done((bf16[256,768]{1,0:T(8,128)(2,1)}, bf16[256,768]{1,0:T(8,128)(2,1)S(1)}, u32[]{:S(2)}, u32[]{:S(2)}) %collective-permute-start.9) | collective-permute-done | bytes 393248 | tf_op jit(solution)/shard_map/ppermute | solution.py:470
  114.3 7.3 %collective-permute-done.13.refs_4_ = bf16[256,512]{1,0:T(8,128)(2,1)S(1)} collective-permute-done((bf16[256,512]{1,0:T(8,128)(2,1)S(1)}, bf16[256,512]{1,0:T(8,128)(2,1)S(1)}, u32[]{:S(2)}, u32[]{:S(2)}) %collective-permute-start.13) | collective-permute-done | bytes 262176 | tf_op jit(solution)/shard_map/ppermute | solution.py:470
  137.7 20.1 %project_qkv.1.q.k.v = bf16[1536,768]{1,0:T(8,128)(2,1)} custom-call(s32[13]{0:T(128)} %stack.154.at_ref, s32[1536,1]{1,0:T(8,128)} %bitcast.111, bf16[2048,256]{1,0:T(8,128)(2,1)} %a_ref.2, f32[1536,128]{1,0:T(8,128)} %get-tuple-element.50.cos_ref, f32[1536,128]{1,0:T(8,128)} %get-tuple-element.51.sin_ref, bf16[768,2048]{1,0:T(8,128)(2,1)} %fusion.3.own_ref, ...), custom_call_target="tpu_custom_call" | custom-call | flops 1000 | bytes 1000 | tf_op jit(solution)/shard_map/project_qkv/pallas_call | solution.py:135
  158.3 8.4 %attend.1.attn_ref = bf16[1536,256]{1,0:T(8,128)(2,1)} custom-call(bf16[1536,768]{1,0:T(8,128)(2,1)} %project_qkv.1.q.k.v, bf16[1536,768]{1,0:T(8,128)(2,1)} %project_qkv.1.q.k.v, bf16[1536,768]{1,0:T(8,128)(2,1)} %project_qkv.1.q.k.v, s32[2,768,1]{2,1,0:T(8,128)} %copy.73.column_ref, s32[2,1,768]{2,1,0:T(1,128)} %broadcast_in_dim.42.line_ref), custom_call_target="tpu_custom_call" | custom-call | flops 1000 | bytes 1000 | tf_op jit(solution)/shard_map/attend/pallas_call | solution.py:175
  166.8 8.4 %project_out.1 = (bf16[768,1024]{1,0:T(8,128)(2,1)}, bf16[768,1024]{1,0:T(8,128)(2,1)}, bf16[768,1024]{1,0:T(8,128)(2,1)}, bf16[768,1024]{1,0:T(8,128)(2,1)}) custom-call(s32[8]{0:T(128)} %stack.146.order_ref, s32[2]{0:T(128)} %pad_add_fusion.2.at_ref, bf16[1536,256]{1,0:T(8,128)(2,1)} %attend.1.attn_ref, s32[1536,1]{1,0:T(8,128)} %bitcast.112, ...), custom_call_target="tpu_custom_call" | custom-call | flops 1000 | bytes 1000 | tf_op jit(solution)/shard_map/project_out/pallas_call | solution.py:234
  175.7 4.7 collective-permute-done.16
  191.8 16.2 %all-to-all-done = bf16[4,192,1024]{2,1,0:T(8,128)(2,1)} async-done(((bf16[4,192,1024]{2,1,0:T(8,128)(2,1)}), bf16[4,192,1024]{2,1,0:T(8,128)(2,1)}, u32[]{:S(2)}, u32[]{:S(2)}) %all-to-all-start) | async-done | bytes 1572896 | tf_op jit(solution)/shard_map/all_to_all | solution.py:484
  211.6 19.3 %all-to-all-done.1 = bf16[4,192,1024]{2,1,0:T(8,128)(2,1)S(1)} async-done(((bf16[4,192,1024]{2,1,0:T(8,128)(2,1)}), bf16[4,192,1024]{2,1,0:T(8,128)(2,1)S(1)}, u32[]{:S(2)}, u32[]{:S(2)}) %all-to-all-start.1) | async-done | bytes 1572896 | tf_op jit(solution)/shard_map/all_to_all | solution.py:484
  236.2 5.0 residual_norm.1
  256.2 57.2 %all-to-all-done.2 = bf16[4,192,2048]{2,1,0:T(8,128)(2,1)} async-done(((bf16[4,192,2048]{2,1,0:T(8,128)(2,1)}), bf16[4,192,2048]{2,1,0:T(8,128)(2,1)}, u32[]{:S(2)}, u32[]{:S(2)}) %all-to-all-start.2) | async-done | bytes 3145760 | tf_op jit(solution)/shard_map/all_to_all | solution.py:484
  313.4 45.0 %all-gather.4.cloned.1.call-done.refs_2_ = bf16[2048,1024]{1,0:T(8,128)(2,1)} async-done(((bf16[1024,1024]{1,0:T(8,128)(2,1)}), bf16[2048,1024]{1,0:T(8,128)(2,1)}) %all-gather.4.cloned.1.call-update) | async-done | bytes 4194320 | tf_op jit(solution)/shard_map/all_gather | solution.py:489
  362.9 52.5 %all-gather.6.cloned.1.call-done.refs_0_ = bf16[4096,256]{1,0:T(8,128)(2,1)} async-done(((bf16[2048,256]{1,0:T(8,128)(2,1)}), bf16[4096,256]{1,0:T(8,128)(2,1)}) %all-gather.6.cloned.1.call-update) | async-done | bytes 2097168 | tf_op jit(solution)/shard_map/all_gather | solution.py:489
  421.8 26.7 %collective-permute-done.22.refs_8_ = bf16[512,256]{1,0:T(8,128)(2,1)S(1)} collective-permute-done((bf16[512,256]{1,0:T(8,128)(2,1)S(1)}, bf16[512,256]{1,0:T(8,128)(2,1)S(1)}, u32[]{:S(2)}, u32[]{:S(2)}) %collective-permute-start.22) | collective-permute-done | bytes 262176 | tf_op jit(solution)/shard_map/ppermute | solution.py:470
  453.3 9.0 %collective-permute-done.21.refs_6_ = bf16[256,1024]{1,0:T(8,128)(2,1)} collective-permute-done((bf16[256,1024]{1,0:T(8,128)(2,1)}, bf16[256,1024]{1,0:T(8,128)(2,1)}, u32[]{:S(2)}, u32[]{:S(2)}) %collective-permute-start.21) | collective-permute-done | bytes 524320 | tf_op jit(solution)/shard_map/ppermute | solution.py:470
  462.3 30.9 %gated.1.h_ref = bf16[1536,1280]{1,0:T(8,128)(2,1)} custom-call(s32[3]{0:T(128)} %pad_add_fusion.3.place_ref, s32[1536,1]{1,0:T(8,128)} %broadcast_in_dim.44.adapter_ref, bf16[2048,256]{1,0:T(8,128)(2,1)} %ag_ref.1, bf16[2048,256]{1,0:T(8,128)(2,1)} %au_ref.1, bf16[768,2048]{1,0:T(8,128)(2,1)} %bitcast.37.refs_0_, ...), custom_call_target="tpu_custom_call" | custom-call | flops 1000 | bytes 1000 | tf_op jit(solution)/shard_map/gated/pallas_call | solution.py:360
  493.3 9.8 %project_down.3 = (bf16[768,1024]{1,0:T(8,128)(2,1)}, bf16[768,1024]{1,0:T(8,128)(2,1)}) custom-call(s32[3]{0:T(128)} %pad_add_fusion.4.at_ref, bf16[1536,1280]{1,0:T(8,128)(2,1)} %gated.1.h_ref, bf16[256,2048]{1,0:T(8,128)(2,1)} %b_ref.5, bf16[4096,256]{1,0:T(8,128)(2,1)} %all-gather.6.cloned.1.call-done.refs_0_, ...), custom_call_target="tpu_custom_call" | custom-call | flops 1000 | bytes 1000 | tf_op jit(solution)/shard_map/project_down/pallas_call | solution.py:421
  515.0 13.7 %collective-permute-done.23.refs_1_ = bf16[2048,256]{1,0:T(8,128)(2,1)S(1)} collective-permute-done((bf16[2048,256]{1,0:T(8,128)(2,1)S(1)}, bf16[2048,256]{1,0:T(8,128)(2,1)S(1)}, u32[]{:S(2)}, u32[]{:S(2)}) %collective-permute-start.23) | collective-permute-done | bytes 1048608 | tf_op jit(solution)/shard_map/ppermute | solution.py:470
  529.7 9.8 %project_down.2 = (bf16[768,1024]{1,0:T(8,128)(2,1)}, bf16[768,1024]{1,0:T(8,128)(2,1)}) custom-call(s32[3]{0:T(128)} %stack.155.at_ref, bf16[1536,1280]{1,0:T(8,128)(2,1)} %gated.1.h_ref, bf16[256,2048]{1,0:T(8,128)(2,1)} %b_ref.5, bf16[2048,256]{1,0:T(8,128)(2,1)} %bitcast.107, bf16[2048,256]{1,0:T(8,128)(2,1)} %copy-done.13), custom_call_target="tpu_custom_call" | custom-call | flops 1000 | bytes 1000 | tf_op jit(solution)/shard_map/project_down/pallas_call | solution.py:421
  553.5 16.3 %all-to-all-done.5 = bf16[4,192,1024]{2,1,0:T(8,128)(2,1)S(1)} async-done(((bf16[4,192,1024]{2,1,0:T(8,128)(2,1)}), bf16[4,192,1024]{2,1,0:T(8,128)(2,1)S(1)}, u32[]{:S(2)}, u32[]{:S(2)}) %all-to-all-start.5) | async-done | bytes 1572896 | tf_op jit(solution)/shard_map/all_to_all | solution.py:484
  575.6 9.5 %collective-permute-done.26.refs_2_ = bf16[192,1024]{1,0:T(8,128)(2,1)S(1)} collective-permute-done((bf16[192,1024]{1,0:T(8,128)(2,1)S(1)}, bf16[192,1024]{1,0:T(8,128)(2,1)S(1)}, u32[]{:S(2)}, u32[]{:S(2)}) %collective-permute-start.26) | collective-permute-done | bytes 393248 | tf_op jit(solution)/shard_map/ppermute | solution.py:470
  585.1 6.7 %collective-permute-done.31.refs_6_ = bf16[192,1024]{1,0:T(8,128)(2,1)S(1)} collective-permute-done((bf16[192,1024]{1,0:T(8,128)(2,1)S(1)}, bf16[192,1024]{1,0:T(8,128)(2,1)S(1)}, u32[]{:S(2)}, u32[]{:S(2)}) %collective-permute-start.31) | collective-permute-done | bytes 393248 | tf_op jit(solution)/shard_map/ppermute | solution.py:470
  (199 shorter events, 161.2 us)
Async XLA Ops:
  15.0 43.4 %collective-permute-start = (bf16[192,2048]{1,0:T(8,128)(2,1)}, bf16[192,2048]{1,0:T(8,128)(2,1)}, u32[]{:S(2)}, u32[]{:S(2)}) collective-permute-start(bf16[192,2048]{1,0:T(8,128)(2,1)} %constant_dynamic-slice_fusion.12), channel_id=1, source_target_pairs={{0,4},{1,5},{2,6},{3,7},{4,0},{5,1},{6,2},{7,3},{8,12},{9,13},{10,... | collective-permute-start | bytes 2359304 | tf_op jit(solution)/shard_map/ppermute | solution.py:470
  20.2 106.5 %collective-permute-start.5 = (bf16[256,768]{1,0:T(8,128)(2,1)S(1)}, bf16[256,768]{1,0:T(8,128)(2,1)}, u32[]{:S(2)}, u32[]{:S(2)}) collective-permute-start(bf16[256,768]{1,0:T(8,128)(2,1)S(1)} %copy.72.refs_4_), channel_id=1, source_target_pairs={{0,24},{1,25},{2,26},{3,27},{4,28},{5,29},{6,30},{7,31},{8,0},{9,1... | collective-permute-start | bytes 1179656 | tf_op jit(solution)/shard_map/ppermute | solution.py:470
  23.8 46.5 %collective-permute-start.7 = (bf16[256,768]{1,0:T(8,128)(2,1)S(1)}, bf16[256,768]{1,0:T(8,128)(2,1)}, u32[]{:S(2)}, u32[]{:S(2)}) collective-permute-start(bf16[256,768]{1,0:T(8,128)(2,1)S(1)} %copy.72.refs_4_), channel_id=1, source_target_pairs={{0,8},{1,9},{2,10},{3,11},{4,12},{5,13},{6,14},{7,15},{8,16},{9,17... | collective-permute-start | bytes 1179656 | tf_op jit(solution)/shard_map/ppermute | solution.py:470
  24.9 30.2 %collective-permute-start.4 = (bf16[256,768]{1,0:T(8,128)(2,1)}, bf16[256,768]{1,0:T(8,128)(2,1)}, u32[]{:S(2)}, u32[]{:S(2)}) collective-permute-start(bf16[256,768]{1,0:T(8,128)(2,1)} %copy.67), channel_id=1, source_target_pairs={{0,4},{1,5},{2,6},{3,7},{4,0},{5,1},{6,2},{7,3},{8,12},{9,13},{10,... | collective-permute-start | bytes 1179656 | tf_op jit(solution)/shard_map/ppermute | solution.py:470
  58.4 37.5 %collective-permute-start.2 = (bf16[192,2048]{1,0:T(8,128)(2,1)}, bf16[192,2048]{1,0:T(8,128)(2,1)}, u32[]{:S(2)}, u32[]{:S(2)}) collective-permute-start(bf16[192,2048]{1,0:T(8,128)(2,1)} %collective-permute-done.refs_0_), channel_id=1, source_target_pairs={{0,2},{1,3},{2,0},{3,1},{4,6},{5,7},{6,4},{7,5},{8,10},{9,11},{10,... | collective-permute-start | bytes 2359304 | tf_op jit(solution)/shard_map/ppermute | solution.py:470
  66.7 117.0 %all-to-all-start.3 = ((bf16[4,256,1024]{2,1,0:T(8,128)(2,1)}), bf16[4,256,1024]{2,1,0:T(8,128)(2,1)S(1)}, u32[]{:S(2)}, u32[]{:S(2)}) async-start(bf16[4,256,1024]{2,1,0:T(8,128)(2,1)} %copy.77), calls=%async_computation.3 | async-start | bytes 4194304 | tf_op jit(solution)/shard_map/all_to_all | solution.py:484
  70.3 34.3 %collective-permute-start.8 = (bf16[256,768]{1,0:T(8,128)(2,1)}, bf16[256,768]{1,0:T(8,128)(2,1)S(1)}, u32[]{:S(2)}, u32[]{:S(2)}) collective-permute-start(bf16[256,768]{1,0:T(8,128)(2,1)} %collective-permute-done.7.refs_10_), channel_id=1, source_target_pairs={{0,8},{1,9},{2,10},{3,11},{4,12},{5,13},{6,14},{7,15},{8,16},{9,17... | collective-permute-start | bytes 1179656 | tf_op jit(solution)/shard_map/ppermute | solution.py:470
  72.3 23.6 %collective-permute-start.11 = (bf16[256,256]{1,0:T(8,128)(2,1)}, bf16[256,256]{1,0:T(8,128)(2,1)S(1)}, u32[]{:S(2)}, u32[]{:S(2)}) collective-permute-start(bf16[256,256]{1,0:T(8,128)(2,1)} %get-tuple-element.20), channel_id=1, source_target_pairs={{0,4},{1,5},{2,6},{3,7},{4,0},{5,1},{6,2},{7,3},{8,12},{9,13},{10,... | collective-permute-start | bytes 393224 | tf_op jit(solution)/shard_map/ppermute | solution.py:470
  73.7 36.9 %collective-permute-start.9 = (bf16[256,768]{1,0:T(8,128)(2,1)}, bf16[256,768]{1,0:T(8,128)(2,1)S(1)}, u32[]{:S(2)}, u32[]{:S(2)}) collective-permute-start(bf16[256,768]{1,0:T(8,128)(2,1)} %collective-permute-done.6.refs_7_), channel_id=1, source_target_pairs={{0,24},{1,25},{2,26},{3,27},{4,28},{5,29},{6,30},{7,31},{8,0},{9,1... | collective-permute-start | bytes 1179656 | tf_op jit(solution)/shard_map/ppermute | solution.py:470
  95.9 41.8 %collective-permute-start.1 = (bf16[192,2048]{1,0:T(8,128)(2,1)}, bf16[192,2048]{1,0:T(8,128)(2,1)}, u32[]{:S(2)}, u32[]{:S(2)}) collective-permute-start(bf16[192,2048]{1,0:T(8,128)(2,1)} %collective-permute-done.refs_0_), channel_id=1, source_target_pairs={{0,1},{1,0},{2,3},{3,2},{4,5},{5,4},{6,7},{7,6},{8,9},{9,8},{10,11... | collective-permute-start | bytes 2359304 | tf_op jit(solution)/shard_map/ppermute | solution.py:470
  95.9 41.8 %collective-permute-start.3 = (bf16[192,2048]{1,0:T(8,128)(2,1)}, bf16[192,2048]{1,0:T(8,128)(2,1)}, u32[]{:S(2)}, u32[]{:S(2)}) collective-permute-start(bf16[192,2048]{1,0:T(8,128)(2,1)} %collective-permute-done.2.refs_2_), channel_id=1, source_target_pairs={{0,1},{1,0},{2,3},{3,2},{4,5},{5,4},{6,7},{7,6},{8,9},{9,8},{10,11... | collective-permute-start | bytes 2359304 | tf_op jit(solution)/shard_map/ppermute | solution.py:470
  125.9 40.8 %collective-permute-start.14 = (bf16[256,256]{1,0:T(8,128)(2,1)}, bf16[256,256]{1,0:T(8,128)(2,1)}, u32[]{:S(2)}, u32[]{:S(2)}) collective-permute-start(bf16[256,256]{1,0:T(8,128)(2,1)} %slice.80), channel_id=1, source_target_pairs={{0,8},{1,9},{2,10},{3,11},{4,12},{5,13},{6,14},{7,15},{8,16},{9,17... | collective-permute-start | bytes 393224 | tf_op jit(solution)/shard_map/ppermute | solution.py:470
  126.7 40.1 %collective-permute-start.15 = (bf16[256,256]{1,0:T(8,128)(2,1)}, bf16[256,256]{1,0:T(8,128)(2,1)}, u32[]{:S(2)}, u32[]{:S(2)}) collective-permute-start(bf16[256,256]{1,0:T(8,128)(2,1)} %slice.81), channel_id=1, source_target_pairs={{0,24},{1,25},{2,26},{3,27},{4,28},{5,29},{6,30},{7,31},{8,0},{9,1... | collective-permute-start | bytes 393224 | tf_op jit(solution)/shard_map/ppermute | solution.py:470
  183.6 24.4 %all-to-all-start = ((bf16[4,192,1024]{2,1,0:T(8,128)(2,1)}), bf16[4,192,1024]{2,1,0:T(8,128)(2,1)}, u32[]{:S(2)}, u32[]{:S(2)}) async-start(bf16[4,192,1024]{2,1,0:T(8,128)(2,1)} %bitcast.114), calls=%async_computation | async-start | bytes 3145728 | tf_op jit(solution)/shard_map/all_to_all | solution.py:484
  250.0 63.4 %all-to-all-start.2 = ((bf16[4,192,2048]{2,1,0:T(8,128)(2,1)}), bf16[4,192,2048]{2,1,0:T(8,128)(2,1)}, u32[]{:S(2)}, u32[]{:S(2)}) async-start(bf16[4,192,2048]{2,1,0:T(8,128)(2,1)} %bitcast.105), calls=%async_computation.2 | async-start | bytes 6291456 | tf_op jit(solution)/shard_map/all_to_all | solution.py:484
  254.7 103.7 %all-gather.4.cloned.1.call-start = ((), (), s32[]{:S(2)}) async-start(), calls=%async_computation.7 | async-start | bytes 6291456 | tf_op jit(solution)/shard_map/all_gather | solution.py:489
  255.4 160.0 %all-gather.6.cloned.1.call-start = ((), (), s32[]{:S(2)}) async-start(), calls=%async_computation.8 | async-start | bytes 3145728 | tf_op jit(solution)/shard_map/all_gather | solution.py:489
  313.3 149.0 %collective-permute-start.18 = (bf16[768,2048]{1,0:T(8,128)(2,1)}, bf16[768,2048]{1,0:T(8,128)(2,1)}, u32[]{:S(2)}, u32[]{:S(2)}) collective-permute-start(bf16[768,2048]{1,0:T(8,128)(2,1)} %bitcast.37.refs_0_), channel_id=1, source_target_pairs={{0,1},{1,0},{2,3},{3,2},{4,5},{5,4},{6,7},{7,6},{8,9},{9,8},{10,11... | collective-permute-start | bytes 9437192 | tf_op jit(solution)/shard_map/ppermute | solution.py:470
  313.3 149.0 %collective-permute-start.19 = (bf16[1024,1024]{1,0:T(8,128)(2,1)S(1)}, bf16[1024,1024]{1,0:T(8,128)(2,1)}, u32[]{:S(2)}, u32[]{:S(2)}) collective-permute-start(bf16[1024,1024]{1,0:T(8,128)(2,1)S(1)} %bitcast.110), channel_id=1, source_target_pairs={{0,2},{1,3},{2,0},{3,1},{4,6},{5,7},{6,4},{7,5},{8,10},{9,11},{10,... | collective-permute-start | bytes 6291464 | tf_op jit(solution)/shard_map/ppermute | solution.py:470
  361.5 100.9 %collective-permute-start.20 = (bf16[1024,1024]{1,0:T(8,128)(2,1)}, bf16[1024,1024]{1,0:T(8,128)(2,1)}, u32[]{:S(2)}, u32[]{:S(2)}) collective-permute-start(bf16[1024,1024]{1,0:T(8,128)(2,1)} %constant_dynamic-slice_fusion.4), channel_id=1, source_target_pairs={{0,2},{1,3},{2,0},{3,1},{4,6},{5,7},{6,4},{7,5},{8,10},{9,11},{10,... | collective-permute-start | bytes 6291464 | tf_op jit(solution)/shard_map/ppermute | solution.py:470
  417.8 75.5 %collective-permute-start.28 = (bf16[2048,256]{1,0:T(8,128)(2,1)}, bf16[2048,256]{1,0:T(8,128)(2,1)}, u32[]{:S(2)}, u32[]{:S(2)}) collective-permute-start(bf16[2048,256]{1,0:T(8,128)(2,1)} %constant_dynamic-slice_fusion), channel_id=1, source_target_pairs={{0,2},{1,3},{2,0},{3,1},{4,6},{5,7},{6,4},{7,5},{8,10},{9,11},{10,... | collective-permute-start | bytes 3145736 | tf_op jit(solution)/shard_map/ppermute | solution.py:470
  419.3 29.2 %collective-permute-start.22 = (bf16[512,256]{1,0:T(8,128)(2,1)S(1)}, bf16[512,256]{1,0:T(8,128)(2,1)S(1)}, u32[]{:S(2)}, u32[]{:S(2)}) collective-permute-start(bf16[512,256]{1,0:T(8,128)(2,1)S(1)} %constant_dynamic-slice_fusion.1.refs_7_), channel_id=1, source_target_pairs={{0,2},{1,3},{2,0},{3,1},{4,6},{5,7},{6,4},{7,5},{8,10},{9,11},{10,... | collective-permute-start | bytes 786440 | tf_op jit(solution)/shard_map/ppermute | solution.py:470
  503.2 25.6 %collective-permute-start.23 = (bf16[2048,256]{1,0:T(8,128)(2,1)S(1)}, bf16[2048,256]{1,0:T(8,128)(2,1)S(1)}, u32[]{:S(2)}, u32[]{:S(2)}) collective-permute-start(bf16[2048,256]{1,0:T(8,128)(2,1)S(1)} %bitcast.108), channel_id=1, source_target_pairs={{0,2},{1,3},{2,0},{3,1},{4,6},{5,7},{6,4},{7,5},{8,10},{9,11},{10,... | collective-permute-start | bytes 3145736 | tf_op jit(solution)/shard_map/ppermute | solution.py:470
  510.0 36.5 %all-to-all-start.6 = ((bf16[4,192,1024]{2,1,0:T(8,128)(2,1)}), bf16[4,192,1024]{2,1,0:T(8,128)(2,1)}, u32[]{:S(2)}, u32[]{:S(2)}) async-start(bf16[4,192,1024]{2,1,0:T(8,128)(2,1)} %bitcast.113), calls=%async_computation.6 | async-start | bytes 3145728 | tf_op jit(solution)/shard_map/all_to_all | solution.py:484
  (50 other events, 1110.4 us)
Sparse Core Ops, SparseCore 0:
  257.0 101.2 all-gather.3
  359.9 55.4 all-gather.5

commit v4 on v3

v4 whole, which is shorter than its diff:
```python
import math

import jax
import jax.numpy as jnp
from jax import lax
from jax.experimental import pallas as pl
from jax.experimental.pallas import tpu as pltpu
from jax.sharding import PartitionSpec as P

HD = 128
RANK = 16
AXES = ("req", "tp")
epsilon = 1e-05
rope_base = 10000.0
F32 = jnp.float32
BF16 = jnp.bfloat16
VM = pltpu.VMEM
PARAMS = pltpu.CompilerParams(vmem_limit_bytes=56 * 2**20)
COST = pl.CostEstimate(flops=1000, bytes_accessed=1000, transcendentals=0)


def dot(a, b):
    return jnp.dot(a, b, preferred_element_type=F32)


def layer_norm(values):
    row_mean = jnp.mean(values, axis=-1, keepdims=True)
    centred = values - row_mean
    spread = jnp.mean(centred * centred, axis=-1, keepdims=True)
    return (centred * lax.rsqrt(spread + epsilon)).astype(BF16)


def masked(inner, adapter_column):
    rank = lax.broadcasted_iota(jnp.int32, inner.shape, 1) // RANK
    return jnp.where(adapter_column == rank, inner, F32(0.0)).astype(BF16)


def whole(array):
    return pl.BlockSpec(array.shape, lambda *_: (0,) * array.ndim, pipeline_mode=pl.Buffered(1))


def mm(start, size):
    return pl.ds(pl.multiple_of(start * size, size), size)


def dma(source, target, semaphore):
    return pltpu.make_async_copy(source, target, semaphore)


def run_all(copies):
    for copy in copies:
        copy.start()
    for copy in copies:
        copy.wait()


SMEM_SPEC = pl.BlockSpec(memory_space=pltpu.SMEM)
VMEM_SPEC = pl.BlockSpec(memory_space=VM)
HBM_SPEC = pl.BlockSpec(memory_space=pl.ANY)


def split_heads(w_qkv, w_out, x):
    rows, _, columns = w_qkv.shape
    local = columns // 2
    width = w_out.shape[1]

    def kernel(x_ref, qkv_ref, out_ref, *outs):
        for which in range(2):
            at = mm(x_ref[0] ^ which, local)
            for i in range(3):
                outs[which][:, i * local : (i + 1) * local] = qkv_ref[:, i, at]
            outs[2 + which][...] = out_ref[at, :]

    return pl.pallas_call(
        kernel,
        in_specs=[SMEM_SPEC, VMEM_SPEC, VMEM_SPEC],
        out_specs=[VMEM_SPEC] * 4,
        out_shape=[jax.ShapeDtypeStruct((rows, 3 * local), BF16)] * 2
        + [jax.ShapeDtypeStruct((local, width), BF16)] * 2,
        compiler_params=PARAMS,
        cost_estimate=COST,
        name="split_heads",
    )(x, w_qkv, w_out)


def norm_rows(tokens, row, T):
    slots, width = tokens.shape
    piece = slots // T

    def kernel(row_ref, tok_ref, out, part):
        i = pl.program_id(0)
        normed = layer_norm(tok_ref[...].astype(F32))
        out[...] = normed

        @pl.when(i == row_ref[0])
        def _():
            part[...] = normed

    return pl.pallas_call(
        kernel,
        grid_spec=pltpu.PrefetchScalarGridSpec(
            num_scalar_prefetch=1,
            grid=(T,),
            in_specs=[pl.BlockSpec((piece, width), lambda i, r: (i, 0))],
            out_specs=[
                pl.BlockSpec((piece, width), lambda i, r: (i, 0)),
                pl.BlockSpec((piece, width), lambda i, r: (0, 0)),
            ],
        ),
        out_shape=[
            jax.ShapeDtypeStruct((slots, width), BF16),
            jax.ShapeDtypeStruct((piece, width), BF16),
        ],
        compiler_params=PARAMS,
        cost_estimate=COST,
        name="norm_rows",
    )(row, tokens)


def pack(gate, up, b):
    rows, columns = gate.shape
    quarter = columns // 4

    def spec(which):
        return pl.BlockSpec((rows, quarter), lambda i, o: (0, o[0] ^ (i * 2 + which)))

    def kernel(b_ref, g0, u0, g1, u1, keep, give):
        keep[0, :, :quarter], keep[0, :, quarter:] = g0[...], u0[...]
        give[0, :, :quarter], give[0, :, quarter:] = g1[...], u1[...]

    out = pl.BlockSpec((1, rows, 2 * quarter), lambda i, o: (i, 0, 0))
    return pl.pallas_call(
        kernel,
        grid_spec=pltpu.PrefetchScalarGridSpec(
            num_scalar_prefetch=1,
            grid=(2,),
            in_specs=[spec(0), spec(0), spec(1), spec(1)],
            out_specs=[out, out],
        ),
        out_shape=[jax.ShapeDtypeStruct((2, rows, 2 * quarter), BF16)] * 2,
        compiler_params=PARAMS,
        cost_estimate=COST,
        name="pack",
    )(b, gate, up, gate, up)


def join(own, came, x):
    rows, columns = own.shape[1:]
    spec = pl.BlockSpec((1, rows, columns), lambda i: (i, 0, 0))
    shape = jax.ShapeDtypeStruct((2 * rows, columns), BF16)

    def kernel(x_ref, own_ref, came_ref, near, give):
        @pl.when(pl.program_id(0) == 0)
        def _():
            near[mm(x_ref[0], rows), :] = own_ref[0]
            near[mm(1 - x_ref[0], rows), :] = came_ref[0]

        @pl.when(pl.program_id(0) == 1)
        def _():
            give[mm(x_ref[0], rows), :] = own_ref[0]
            give[mm(1 - x_ref[0], rows), :] = came_ref[0]

    return pl.pallas_call(
        kernel,
        grid=(2,),
        in_specs=[SMEM_SPEC, spec, spec],
        out_specs=[pl.BlockSpec((2 * rows, columns), lambda i: (0, 0))] * 2,
        out_shape=[shape, shape],
        compiler_params=PARAMS,
        cost_estimate=COST,
        name="join",
    )(x, own, came)


def tables(lengths, adapters, scalars, slots, T):
    count = lengths.shape[1]
    piece = slots // T
    half = HD // 2

    def kernel(len_ref, ad_ref, at_ref, column, line, two, cosine, sine, rows):
        def layout(index, slot, wants):
            end = jnp.int32(0)
            request, start = jnp.zeros(slot.shape, jnp.int32), jnp.zeros(slot.shape, jnp.int32)
            adapter = jnp.full(slot.shape, ad_ref[index, 0], jnp.int32)
            for k in range(count):
                end = end + len_ref[index, k]
                past = slot >= end
                request = request + past.astype(jnp.int32)
                if wants and k + 1 < count:
                    start = jnp.where(past, end, start)
                    adapter = jnp.where(past, ad_ref[index, k + 1], adapter)
            return request, slot - start, adapter

        lane = lax.broadcasted_iota(jnp.int32, (1, HD), 1)
        frequency = jnp.exp((lane % half).astype(F32) * F32(-math.log(rope_base) * 2.0 / HD))
        for i in range(2):
            index = at_ref[0] * 2 + i
            down = lax.broadcasted_iota(jnp.int32, (slots, 1), 0)
            request, position, adapter = layout(index, down, True)
            column[i] = request
            line[i] = layout(index, lax.broadcasted_iota(jnp.int32, (1, slots), 1), False)[0]
            here = slice(i * slots, (i + 1) * slots)
            two[here] = adapter
            angles = position.astype(F32) * frequency
            cosine[here] = jnp.cos(angles)
            sine[here] = jnp.where(lane < half, -jnp.sin(angles), jnp.sin(angles))
        for s in range(2):
            first = (at_ref[1] * 2 + (at_ref[2] ^ s)) * piece
            slot = first + lax.broadcasted_iota(jnp.int32, (piece, 1), 0)
            for b in range(4):
                to = (s * 4 + b) * piece
                rows[to : to + piece] = layout(at_ref[3] ^ b, slot, True)[2]

    table = jax.ShapeDtypeStruct((2 * slots, HD), F32)
    return pl.pallas_call(
        kernel,
        in_specs=[SMEM_SPEC] * 3,
        out_specs=[VMEM_SPEC] * 6,
        out_shape=[
            jax.ShapeDtypeStruct((2, slots, 1), jnp.int32),
            jax.ShapeDtypeStruct((2, 1, slots), jnp.int32),
            jax.ShapeDtypeStruct((2 * slots, 1), jnp.int32),
            table,
            table,
            jax.ShapeDtypeStruct((8 * piece, 1), jnp.int32),
        ],
        compiler_params=PARAMS,
        cost_estimate=COST,
        name="tables",
    )(lengths, adapters, scalars)


def finish(hidden_state, terms, at):
    piece, columns = terms[0].shape
    spec = pl.BlockSpec((piece, columns), lambda i, a: (0, 0))

    def kernel(at_ref, hidden_ref, *refs):
        total = hidden_ref[...]
        for ref in refs[:-1]:
            total = total + ref[...].astype(F32)
        refs[-1][...] = total.astype(BF16)

    return pl.pallas_call(
        kernel,
        grid_spec=pltpu.PrefetchScalarGridSpec(
            num_scalar_prefetch=1,
            grid=(1,),
            in_specs=[pl.BlockSpec((piece, columns), lambda i, a: (0, a[0]))] + [spec] * len(terms),
            out_specs=spec,
        ),
        out_shape=jax.ShapeDtypeStruct((piece, columns), BF16),
        compiler_params=PARAMS,
        cost_estimate=COST,
        name="finish",
    )(at, hidden_state, *terms)


def project_qkv(own, pieces, adapter, a, b, cosine, sine, weights, places):
    slots, width = own.shape
    total_rows, columns, rank = 2 * slots, b.shape[1], b.shape[0]
    piece, size, tile = pieces[0].shape[0], width // len(weights), columns // 3
    n_pieces, n_weights = len(pieces), len(weights)
    chunk = total_rows // 4
    column = adapter

    def kernel(at_ref, adapter_ref, a_ref, cos_ref, sin_ref, own_ref, b_ref, *refs):
        p_in, w_in, rest = refs[:n_pieces], refs[n_pieces : n_pieces + n_weights], refs[-7:]
        out, x, w, bb, low, x_sem, w_sem = rest

        def weight_copies(step, slot):
            to = pl.ds(step * tile, tile)
            for i in range(n_weights):
                yield dma(
                    w_in[i].at[:, to],
                    w.at[slot, mm(at_ref[1 + n_pieces + i], size), :],
                    w_sem.at[slot, i],
                )
            yield dma(b_ref.at[:, to], bb.at[slot], w_sem.at[slot, n_weights])

        x_copies = [dma(own_ref, x.at[mm(at_ref[0], slots), :], x_sem.at[n_pieces])]
        for i in range(n_pieces):
            x_copies.append(dma(p_in[i], x.at[mm(at_ref[1 + i], piece), :], x_sem.at[i]))
        for copy in x_copies:
            copy.start()
        for copy in weight_copies(0, 0):
            copy.start()
        for copy in x_copies:
            copy.wait()
        for step in range(3):
            slot = step % 2
            if step < 2:
                for copy in weight_copies(step + 1, 1 - slot):
                    copy.start()
            for copy in weight_copies(step, slot):
                copy.wait()

            @pl.loop(0, total_rows // chunk)
            def _(m):
                at = mm(m, chunk)
                xs = x[at, :]
                if step == 0:
                    low[at, :] = masked(dot(xs, a_ref[...]), adapter_ref[at, :])
                total = dot(xs, w[slot]) + dot(low[at, :], bb[slot])
                for h in range(tile // HD):
                    v = total[:, h * HD : (h + 1) * HD]
                    if step < 2:
                        v = v * cos_ref[at, :] + pltpu.roll(v, HD // 2, 1) * sin_ref[at, :]
                    start = step * tile + h * HD
                    out[at, start : start + HD] = v.astype(BF16)

    return pl.pallas_call(
        kernel,
        in_specs=[SMEM_SPEC] + [VMEM_SPEC] * 4 + [HBM_SPEC] * (2 + n_pieces + n_weights),
        out_specs=VMEM_SPEC,
        out_shape=jax.ShapeDtypeStruct((total_rows, columns), BF16),
        scratch_shapes=[
            VM((total_rows, width), BF16),
            VM((2, width, tile), BF16),
            VM((2, rank, tile), BF16),
            VM((total_rows, rank), BF16),
            pltpu.SemaphoreType.DMA((n_pieces + 1,)),
            pltpu.SemaphoreType.DMA((2, n_weights + 1)),
        ],
        compiler_params=PARAMS,
        cost_estimate=COST,
        name="project_qkv",
    )(places, column, a, cosine, sine, own, b, *pieces, *weights)


def attend(qkv, column, line):
    indices, slots = column.shape[:2]
    heads = qkv.shape[1] // 3 // HD
    rows = 256 if slots % 256 == 0 else slots

    def kernel(q, k, v, column_ref, line_ref, out):
        for at in range(0, slots, rows):
            seen = at + rows
            s = lax.dot_general(
                q[at:seen], k[:seen], (((1,), (1,)), ((), ())), preferred_element_type=F32
            )
            s = s * (1.0 / math.sqrt(HD))
            here = at + lax.broadcasted_iota(jnp.int32, s.shape, 0)
            there = lax.broadcasted_iota(jnp.int32, s.shape, 1)
            allowed = (column_ref[0, at:seen] == line_ref[0, :, :seen]) & (here >= there)
            s = jnp.where(allowed, s, F32(-1e30))
            e = jnp.exp(s - jnp.max(s, axis=1, keepdims=True))
            weights = (e * (1.0 / jnp.sum(e, axis=1, keepdims=True))).astype(BF16)
            out[at:seen] = dot(weights, v[:seen]).astype(BF16)

    return pl.pallas_call(
        kernel,
        grid=(indices, heads),
        in_specs=[
            pl.BlockSpec((slots, HD), lambda i, h: (i, h)),
            pl.BlockSpec((slots, HD), lambda i, h: (i, heads + h)),
            pl.BlockSpec((slots, HD), lambda i, h: (i, 2 * heads + h)),
            pl.BlockSpec((1, slots, 1), lambda i, h: (i, 0, 0)),
            pl.BlockSpec((1, 1, slots), lambda i, h: (i, 0, 0)),
        ],
        out_specs=pl.BlockSpec((slots, HD), lambda i, h: (i, h)),
        out_shape=jax.ShapeDtypeStruct((indices * slots, heads * HD), BF16),
        compiler_params=PARAMS,
        cost_estimate=COST,
        name="attend",
    )(qkv, qkv, qkv, column, line)


def project_out(attn, adapter, a, b, weights, order, scalars, T, came=None):
    total_rows, depth = attn.shape
    n, slots, piece, Y = len(weights), total_rows // 2, total_rows // 2 // T, T // 2
    flat = [p for w in weights for p in w]
    size = sum(p.shape[1] for p in flat) // n // 2
    half, columns = total_rows // 2, n * 2 * size
    extra = [] if came is None else [came]

    def kernel(order_ref, at_ref, attn_ref, adapter_ref, a_ref, b_ref, *refs):
        ws, outs, rows, low = refs[: len(flat)], refs[len(flat) + len(extra) : -2], *refs[-2:]
        x, y, c = at_ref[0], at_ref[1], at_ref[2]
        mine = a_ref[mm(x, depth), :]
        for i in range(2):
            for k in range(Y):
                here = mm((x ^ i) * T + lax.rem(y + Y - k, Y) * 2 + c, piece)
                to = (i * Y + k) * piece
                part = attn_ref[here, :]
                rows[to : to + piece] = part
                low[to : to + piece] = masked(dot(part, mine), adapter_ref[here, :])
        it = iter(ws)
        for k, w in enumerate(weights):
            blocks = []
            for p in w:
                ref = next(it)
                for start in range(0, p.shape[1], size):
                    blocks.append((ref, start))
            for i, (ref, start) in enumerate(blocks):
                there = mm(order_ref[2 * k + i], size)
                to = mm(k * 2 + (x ^ i), size)
                total = dot(rows[...], ref[:, start : start + size]) + dot(low[...], b_ref[:, there])
                if came is None:
                    outs[0][:, to] = total.astype(BF16)
                else:
                    total = (total + refs[len(flat)][:, to].astype(F32)).astype(BF16)
                    for p in range(2 * Y):
                        outs[p][:, to] = total[p * piece : (p + 1) * piece]

    shapes = [jax.ShapeDtypeStruct((half, columns), BF16)]
    if came is not None:
        shapes = [jax.ShapeDtypeStruct((piece, columns), BF16)] * (2 * Y)
    out = pl.pallas_call(
        kernel,
        in_specs=[SMEM_SPEC, SMEM_SPEC] + [VMEM_SPEC] * (4 + len(flat) + len(extra)),
        out_specs=[VMEM_SPEC] * len(shapes),
        out_shape=shapes,
        scratch_shapes=[VM((half, depth), BF16), VM((half, a.shape[1]), BF16)],
        compiler_params=PARAMS,
        cost_estimate=COST,
        name="project_out",
    )(order, scalars, attn, adapter, a, b, *flat, *extra)
    return out[0] if came is None else out


def residual_norm(tokens, row, order, chunks):
    width = tokens.shape[1]
    n = order.shape[0]
    piece, size, per = chunks[0][0].shape[0], width // n, n // len(chunks)
    flat = [term for chunk in chunks for term in chunk]

    def kernel(row_ref, order_ref, tok_ref, *refs):
        it, hidden, normed = iter(refs[:-2]), refs[-2], refs[-1]
        for c, chunk in enumerate(chunks):
            total = next(it)[...].astype(F32)
            for _ in chunk[1:]:
                total = total + next(it)[...].astype(F32)
            for place in range(per):
                to = mm(order_ref[c * per + place], size)
                more = total[:, place * size : (place + 1) * size]
                hidden[:, to] = tok_ref[:, to].astype(F32) + more
        normed[...] = layer_norm(hidden[...])

    return pl.pallas_call(
        kernel,
        grid_spec=pltpu.PrefetchScalarGridSpec(
            num_scalar_prefetch=2,
            grid=(1,),
            in_specs=[
                pl.BlockSpec((piece, width), lambda n, r, o: (r[0], 0)),
                *[pl.BlockSpec(p.shape, lambda n, r, o: (0, 0)) for p in flat],
            ],
            out_specs=[pl.BlockSpec((piece, width), lambda n, r, o: (0, 0))] * 2,
        ),
        out_shape=[
            jax.ShapeDtypeStruct((piece, width), F32),
            jax.ShapeDtypeStruct((piece, width), BF16),
        ],
        compiler_params=PARAMS,
        cost_estimate=COST,
        name="residual_norm",
    )(row, order, tokens, *flat)


def gated(rows, adapters, a_gate, a_up, sets, places):
    width = rows[0].shape[1]
    total_rows = sum(row.shape[0] for row in rows)
    units = sets[0][1].shape[1] // 2
    tile = min(256, units)
    tiles = units // tile
    rank = a_gate.shape[1]
    column = adapters
    flat = [w for s in sets for w in s[0]]
    first = [sum(len(s[0]) for s in sets[:k]) for k in range(len(sets) + 1)]
    bs = [s[1] for s in sets]
    downs = [s[2] for s in sets]
    n_rows, n_sets = len(rows), len(sets)
    most = max(len(s[0]) for s in sets)
    steps = n_sets * tiles
    chunk = total_rows // 4
    hidden_width = n_sets * units

    def kernel(place_ref, adapter_ref, ag_ref, au_ref, *refs):
        it = iter(refs)
        take = lambda k: [next(it) for _ in range(k)]
        x_in, w_in, b_in, d_in = take(n_rows), take(len(flat)), take(n_sets), take(n_sets)
        hidden, x, w, bb, lg, lu, ld, x_sem, w_sem, b_sem = take(10)

        def weight_copies(step, slot):
            s, t = divmod(step, tiles)
            for g in range(2):
                for i in range(first[s], first[s + 1]):
                    yield dma(
                        w_in[i].at[:, pl.ds(g * units + t * tile, tile)],
                        w.at[slot, g, mm(place_ref[i], flat[i].shape[0]), :],
                        w_sem.at[slot, g, i - first[s]],
                    )
                yield dma(
                    b_in[s].at[:, pl.ds(g * units + t * tile, tile)],
                    bb.at[slot, g],
                    b_sem.at[slot, g],
                )

        x_copies, start = [], 0
        for i in range(n_rows):
            x_copies.append(dma(x_in[i], x.at[pl.ds(start, rows[i].shape[0]), :], x_sem.at[i]))
            start += rows[i].shape[0]
        for copy in x_copies:
            copy.start()
        for copy in weight_copies(0, 0):
            copy.start()
        for copy in x_copies:
            copy.wait()
        for step in range(steps):
            slot = step % 2
            if step + 1 < steps:
                for copy in weight_copies(step + 1, 1 - slot):
                    copy.start()
            for copy in weight_copies(step, slot):
                copy.wait()
            s, t = divmod(step, tiles)

            @pl.loop(0, total_rows // chunk)
            def _(m):
                at = mm(m, chunk)
                xs = x[at, :]
                if step == 0:
                    lg[at, :] = masked(dot(xs, ag_ref[...]), adapter_ref[at, :])
                    lu[at, :] = masked(dot(xs, au_ref[...]), adapter_ref[at, :])
                gate = dot(xs, w[slot, 0]) + dot(lg[at, :], bb[slot, 0])
                up = dot(xs, w[slot, 1]) + dot(lu[at, :], bb[slot, 1])
                h = (gate / (1.0 + jnp.exp(-gate)) * up).astype(BF16)
                hidden[at, step * tile : (step + 1) * tile] = h
                more = dot(h, d_in[s][t * tile : (t + 1) * tile, :])
                if step > 0:
                    more = more + ld[at, :]
                if step < steps - 1:
                    ld[at, :] = more
                else:
                    hidden[at, hidden_width:] = masked(more, adapter_ref[at, :])

    return pl.pallas_call(
        kernel,
        in_specs=[SMEM_SPEC] + [VMEM_SPEC] * 3
        + [HBM_SPEC] * (n_rows + len(flat) + n_sets)
        + [VMEM_SPEC] * n_sets,
        out_specs=VMEM_SPEC,
        out_shape=jax.ShapeDtypeStruct((total_rows, hidden_width + rank), BF16),
        scratch_shapes=[
            VM((total_rows, width), BF16),
            VM((2, 2, width, tile), BF16),
            VM((2, 2, rank, tile), BF16),
            VM((total_rows, rank), BF16),
            VM((total_rows, rank), BF16),
            VM((total_rows, rank), F32),
            pltpu.SemaphoreType.DMA((n_rows,)),
            pltpu.SemaphoreType.DMA((2, 2, most)),
            pltpu.SemaphoreType.DMA((2, 2)),
        ],
        compiler_params=PARAMS,
        cost_estimate=COST,
        name="gated",
    )(places, column, a_gate, a_up, *rows, *flat, *bs, *downs)


def project_down(hidden, b, sets, units, at, which, came=None):
    half, depth = hidden.shape[0] // 2, hidden.shape[1]
    piece, rank = half // 4, b.shape[0]
    size = sets[0][0].shape[1]
    flat = [w for group in sets for w in group]
    n, n_sets, n_weights = 4, len(sets), len(flat)
    extra = [] if came is None else [came]

    def kernel(at_ref, h_ref, *refs):
        refs = list(refs)
        came_ref = refs.pop(0) if extra else None
        b_ref, w_in, outs, w, sems = refs[0], refs[1 : 1 + n_weights], refs[1 + n_weights : -2], *refs[-2:]
        copies = [
            dma(
                b_ref.at[:, mm(at_ref[0], n * size)],
                w.at[n_sets * units : n_sets * units + rank, :],
                sems.at[n_sets * n],
            )
        ]
        it = iter(w_in)
        for k, group in enumerate(sets):
            place = 0
            for array in group:
                ref = next(it)
                for i in range(array.shape[0] // units):
                    copies.append(
                        dma(
                            ref.at[pl.ds(i * units, units), :],
                            w.at[k * units : (k + 1) * units, place * size : (place + 1) * size],
                            sems.at[k * n + place],
                        )
                    )
                    place += 1
        run_all(copies)
        for m in range(2):
            here = slice(m * 2 * piece, (m + 1) * 2 * piece)
            total = dot(h_ref[here, :], w[...])
            if came is None:
                outs[0][here, :] = total.astype(BF16)
            else:
                total = (total + came_ref[here, :].astype(F32)).astype(BF16)
                outs[2 * m][...], outs[2 * m + 1][...] = total[:piece], total[piece:]

    shapes = [jax.ShapeDtypeStruct((half, n * size), BF16)]
    if came is not None:
        shapes = [jax.ShapeDtypeStruct((piece, n * size), BF16)] * 4
    out = pl.pallas_call(
        kernel,
        grid=(1,),
        in_specs=[SMEM_SPEC, pl.BlockSpec((half, depth), lambda i: (which, 0))]
        + [VMEM_SPEC] * len(extra)
        + [HBM_SPEC] * (1 + n_weights),
        out_specs=[VMEM_SPEC] * len(shapes),
        out_shape=shapes,
        scratch_shapes=[
            VM((depth, n * size), BF16),
            pltpu.SemaphoreType.DMA((n_sets * n + 1,)),
        ],
        compiler_params=PARAMS,
        cost_estimate=COST,
        name="project_down",
    )(at, hidden, *extra, b, *flat)
    return out[0] if came is None else out


def assemble(pieces, places, shape):
    rows, columns = pieces[0].shape

    def kernel(places_ref, *refs):
        out = refs[-1]
        for i in range(len(pieces)):
            to = mm(places_ref[2 * i], rows), mm(places_ref[2 * i + 1], columns)
            out[to] = refs[i][...]

    return pl.pallas_call(
        kernel,
        in_specs=[SMEM_SPEC] + [VMEM_SPEC] * len(pieces),
        out_specs=VMEM_SPEC,
        out_shape=jax.ShapeDtypeStruct(shape, BF16),
        compiler_params=PARAMS,
        cost_estimate=COST,
        name="assemble",
    )(places, *pieces)


@jax.tree_util.register_pytree_node_class
class Live:
    def __init__(self, **arrays):
        self.__dict__.update(arrays)

    def tree_flatten(self):
        names = tuple(sorted(self.__dict__))
        return [self.__dict__[name] for name in names], names

    @classmethod
    def tree_unflatten(cls, names, arrays):
        return cls(**dict(zip(names, arrays)))

    @property
    def pop(self):
        return Pop(self)

    @property
    def drop(self):
        return Drop(self)


class Pop:
    def __init__(self, live):
        self.__dict__.update(live=live)

    def __getattr__(self, name):
        return self.live.__dict__.pop(name)


class Drop(Pop):
    def __getattr__(self, name):
        self.live.__dict__.pop(name)
        return self


def make_body(R, T):
    Z, ZH, Y = R // 2, R // 4, T // 2

    def flat(z, x, y, c):
        return (z * 2 + x) * T + y * 2 + c

    def move(f):
        every = [(r // 2, r % 2, t // 2, t % 2) for r in range(R) for t in range(T)]
        return [(flat(*d), flat(*f(*d))) for d in every]

    def send(value, pairs):
        return lax.ppermute(value, AXES, pairs)

    to_core = move(lambda z, x, y, c: (z, x, y, 1 - c))
    to_x = move(lambda z, x, y, c: (z, 1 - x, y, c))
    z_up = move(lambda z, x, y, c: ((z + 1) % Z, x, y, c))
    z_down = move(lambda z, x, y, c: ((z - 1) % Z, x, y, c))
    from_y = {k: move(lambda z, x, y, c, k=k: (z, x, (y - k) % Y, c)) for k in range(1, Y)}
    same_xzl = [[zh * 4 + b for b in range(4)] for zh in range(ZH)]
    same_zh = [[zh * 4 + b for zh in range(ZH)] for b in range(4)]
    to_xy = {
        (i, k): move(lambda z, x, y, c, i=i, k=k: (z, x ^ i, (y - k) % Y, c))
        for i in (0, 1)
        for k in range(Y)
    }
    to_xzl = {
        (i, j): move(lambda z, x, y, c, i=i, j=j: (z ^ j, x ^ i, y, c))
        for j in (0, 1)
        for i in (0, 1)
    }

    from_zh = {
        k: move(lambda z, x, y, c, k=k: ((z - 2 * k) % Z, x, y, c)) for k in range(1, ZH)
    }
    to_zl = move(lambda z, x, y, c: (z ^ 1, x, y, c))

    def spread(value, axes, groups):
        return lax.all_to_all(value, axes, 0, 0, axis_index_groups=groups, tiled=True)

    def fence(live):
        return lax.optimization_barrier(live)

    def body(
        tokens, lengths, request_adapter, w_qkv, w_out, w_gate, w_up, w_down,
        a_qkv, b_qkv, a_out, b_out, a_gate, b_gate, a_up, b_up, a_down, b_down,
    ):
        r, t = lax.axis_index("req"), lax.axis_index("tp")
        z, x, y, c = r // 2, r % 2, t // 2, t % 2
        zh, zl = z // 2, z % 2
        slots, width = tokens.shape
        piece = slots // T
        block = width // R
        local = w_qkv.shape[2] // 2
        rank = a_qkv.shape[1]
        quarter = w_gate.shape[1] // 4
        span = width // ZH
        count = lengths.shape[1]
        far_y, far_zh, opposite = range(1, Y), range(1, ZH), Z // 2

        def cut(array, start, size, axis):
            return lax.dynamic_slice_in_dim(array, start, size, axis)

        def ints(values):
            return jnp.stack([jnp.asarray(v, jnp.int32) for v in values])

        L = Live(
            tokens=tokens, both=jnp.concatenate([lengths, request_adapter], axis=1), w_gate=w_gate,
            w_up=w_up, w_down=w_down, a_qkv=a_qkv, a_out=a_out, b_out=b_out, a_gate=a_gate,
            a_up=a_up, b_down=b_down, b_qkv=b_qkv, b_gate=b_gate, b_up=b_up, a_down=a_down,
        )
        keys = [(k, i) for k in range(Z) for i in (0, 1)]
        order = [((z + k) % Z) * 2 + (x ^ i) for k, i in keys]
        there = [(zh + h) % ZH for h in range(ZH)]
        at = [(1 - x) * T + ((y + k) % Y) * 2 + s for s in (c, 1 - c) for k in range(Y)]
        far_places = [h * 4 + (zl ^ j) * 2 + q for h in there[1:] for j in (0, 1) for q in (0, 1)]
        places = ([zh * 2 + zl, zh * 2 + 1 - zl] + far_places) * Y
        L.ints = Live(
            t=ints([t]), order=[ints(order[:Z]), ints(order[Z:])], qkv=ints([x, *at, *order]),
            xyc=[ints([x, y, c]), ints([x, y, 1 - c])],
            zyc=ints([zl, y, c, zl * 2 + x]), z=ints([(z + k) % Z for k in range(Z)]),
            gated=ints(places), span=[ints([h]) for h in there], b=ints([zl * 2 + x]),
        )
        mine = (zl * 2 + x) * quarter
        L.split = split_heads(w_qkv, w_out, ints([x]))
        L = fence(L)

        def ring_start(own):
            left = right = own
            got = {0: own}
            for k in range(1, opposite):
                left, right = send(left, z_up), send(right, z_down)
                got[Z - k], got[k] = left, right
            return got

        head, other_head, own_out, other_out = L.pop.split
        L.first = send(other_head, to_x)
        L.ring = [ring_start(head)]
        L.out = send(other_out, to_x)
        L.both = spread(jnp.concatenate([L.both] * 4, axis=0), "req", same_xzl)
        L.normed, L.mine = norm_rows(L.tokens, L.ints.t, T)
        L.b = jnp.concatenate(
            [cut(L.pop.b_gate, mine, quarter, 1), cut(L.pop.b_up, mine, quarter, 1)], axis=1
        )
        L.a_down = cut(L.a_down, mine, quarter, 0)
        L.b_heads = cut(L.pop.b_qkv, x * local, local, 2).reshape(rank, 3 * local)
        L.own_out = own_out
        L = fence(L)

        L.ring.append(ring_start(L.pop.first))
        L.quarter = send(L.pop.mine, to_x)
        L.b_far = [send(L.b, from_y[k]) for k in far_y]
        L.gu, L.gu_give = pack(L.pop.w_gate, L.pop.w_up, L.ints.b)
        L.out = jnp.concatenate([L.pop.own_out, L.out], axis=1)
        L = fence(L)

        L.ring[0][opposite] = send(L.ring[0][opposite + 1], z_up)
        L.ring[1][opposite] = send(L.ring[1][opposite - 1], z_down)
        L.quarters = [L.quarter] + [send(L.quarter, from_y[k]) for k in far_y]
        L.out = ring_start(L.out)
        L.gu_came = send(L.pop.gu_give, to_x)
        both = L.pop.both
        L.tables = tables(both[:, :count], both[:, count:], L.ints.zyc, slots, T)
        L = fence(L)
        L.quarters = L.quarters + [send(q, to_core) for q in L.quarters]
        L.for_out = [L.out[opposite + 1][:, :block], L.out[opposite - 1][:, block:]]
        L.near, L.give = join(L.pop.gu, L.pop.gu_came, L.ints.xyc[0])
        L = fence(L)

        one, two = L.pop.for_out
        L.far_out = [send(one, z_up), send(two, z_down)]
        L.far = send(L.pop.give, to_zl)
        L.y = [[send(L.near, from_y[k]) for k in far_y]]
        column, line, adapter, cosine, sine, adapters = L.tables
        L.joined = project_qkv(
            L.pop.normed, L.pop.quarters, adapter, L.pop.a_qkv, L.pop.b_heads, cosine,
            sine, [L.ring[i][k] for k, i in keys], L.ints.qkv,
        )
        L.pop.ring
        L = fence(L)

        def over_zh(w):
            return [send(w, from_zh[h]) for h in far_zh]

        rows = L.near.shape[0] // 2
        L.for_zh = [w[q * rows : (q + 1) * rows] for w in (L.near, L.far) for q in (0, 1)]
        L.y.append([send(L.far, from_y[k]) for k in far_y])
        L.zh = [over_zh(L.for_zh[0])]
        L.a_far = [send(L.a_down, from_y[k]) for k in far_y]
        column, line, adapter, cosine, sine, adapters = L.pop.tables
        L.attn = attend(L.pop.joined, column, line)
        blocks = [(L.out[k],) if k != opposite else tuple(L.far_out) for k in range(Z)]
        L.blocks = [blocks[:opposite], blocks[opposite:]]
        L.adapter, L.adapters = adapter, adapters
        L.pop.out, L.pop.far_out, L.pop.quarter
        L.down = spread(L.pop.w_down, "req", same_xzl)
        L = fence(L)

        def out_of(L, chunk, core, came=None):
            return project_out(
                L.attn, L.adapter, L.a_out, L.b_out, L.blocks[chunk],
                L.ints.order[chunk], L.ints.xyc[core], T, came,
            )

        L.zh += [over_zh(L.for_zh[1]), over_zh(L.for_zh[2])]
        came = [send(out_of(L, chunk, 1), to_core) for chunk in (0, 1)]
        L.sums = []
        for chunk in (0, 1):
            parts = out_of(L, chunk, 0, came[chunk])
            terms = [parts[0]]
            for i in (0, 1):
                for k in range(Y):
                    if i or k:
                        terms.append(send(parts[i * Y + k], to_xy[(i, k)]))
            L.sums.append(terms)
        L = fence(L)
        L.hidden_state, L.normed2 = residual_norm(
            L.pop.tokens, L.ints.t, L.ints.z, L.pop.sums
        )
        L.drop.attn.adapter.a_out.b_out.blocks
        split = L.down.shape[0] // 2
        L.for_down = [L.down[:split], L.down[split:]]
        L = fence(L)

        def relay(parts):
            return [[[send(w, from_y[k]) for w in part] for k in far_y] for part in parts]

        own = L.pop.normed2
        L.rows = [own, send(own, to_x), send(own, to_zl)]
        L.core = [send(own, to_core)]
        L.zh_y = relay(L.zh[:2])
        L.zh.append(over_zh(L.for_zh[3]))
        L.cut = [L.rows[1][: piece // 2], L.rows[2][piece // 2 :]]
        L = fence(L)
        one, two = L.pop.cut
        L.core += [send(row, to_core) for row in L.rows[1:]]
        L.rows += [send(one, to_zl), send(two, to_x)]
        L.zh_y += relay(L.zh[2:])
        L.down_zh = [over_zh(L.for_down[0])]
        L = fence(L)
        L.rows += L.pop.core + [send(row, to_core) for row in L.rows[3:]]
        L = fence(L)

        L.down_zh.append(over_zh(L.for_down[1]))
        L.down_y = [send(L.down, from_y[k]) for k in far_y]
        L.down_zh_y = relay(L.down_zh[:1])
        zh_blocks = [part[h] for h in range(ZH - 1) for part in L.zh]
        sets = [([L.near, L.far, *zh_blocks], L.b, L.a_down)]
        for k in range(Y - 1):
            relayed = [part[k][h] for h in range(ZH - 1) for part in L.zh_y]
            sets.append(([L.y[0][k], L.y[1][k], *relayed], L.b_far[k], L.a_far[k]))
        L.hidden = gated(
            L.rows, L.adapters, L.pop.a_gate, L.pop.a_up, sets, L.ints.gated
        )
        L.drop.near.far.for_zh.zh.b.a_down.zh_y.y.b_far.a_far.rows
        L = fence(L)

        L.down_zh_y += relay(L.down_zh[1:])
        down_sets = [[[L.down]] + [[w] for w in L.down_y]]
        for h in range(ZH - 1):
            far = [[part[k][h] for part in L.down_zh_y] for k in range(Y - 1)]
            down_sets.append([[part[h] for part in L.down_zh]] + far)

        def down_of(h, which, came=None):
            return project_down(
                L.hidden, L.b_down, down_sets[h], quarter, L.ints.span[h], which, came
            )

        came = [send(down_of(h, 1), to_core) for h in range(ZH)]
        pieces, places = [], []
        for h in range(ZH):
            parts = down_of(h, 0, came[h])
            terms = [parts[0]]
            terms += [send(parts[j * 2 + i], to_xzl[(i, j)]) for j in (0, 1) for i in (0, 1) if i or j]
            done = finish(L.hidden_state, terms, L.ints.span[h])
            for k in range(Y):
                there_y = done if k == 0 else send(done, from_y[k])
                for s, got in ((0, there_y), (1, send(there_y, to_core))):
                    pieces.append(got)
                    places += [((y + k) % Y) * 2 + (c ^ s), there[h]]
        return assemble(pieces, ints(places), tokens.shape)

    return body


def solution(mesh):
    in_specs = (
        P("req", None),
        P("req", None),
        P("req", None),
        P("req", None, "tp"),
        P("tp", "req"),
        P("req", "tp"),
        P("req", "tp"),
        P("tp", "req"),
        P(),
        P(None, None, "tp"),
        P("tp", None),
        P(),
        P(),
        P(None, "tp"),
        P(),
        P(None, "tp"),
        P("tp", None),
        P(),
    )
    return jax.shard_map(
        make_body(mesh.shape["req"], mesh.shape["tp"]),
        mesh=mesh, in_specs=in_specs, out_specs=P("req", None), check_vma=False,
    )
```

time: 606 us -> 434 us (0.72)
  waiting for transfers between devices: 326 us -> 189 us
  Pallas kernels: 96 us -> 142 us
  other arithmetic: 41 us -> 2.15 us
  blocking collectives: 23 us -> 0 us
  local copies, waits for them, and re-layouts: 40.5 us -> 22.6 us
  starting transfers between devices: 63.4 us -> 76.8 us
  between operations: 14 us -> 0.72 us
    all_to_all x7 -> x2, waiting for transfers between devices: 114 us -> 3.33 us  [spread(): lax.all_to_all(value, axes, 0, 0, axis_index_groups=groups, tiled=True)]
    all_gather x2 -> x0, waiting for transfers between devices: 97.5 us -> none  [gather_zh(): lax.all_gather(wait_for(value, after), 'req', axis=0, axis_index_groups=s...]
    ppermute x33 -> x66, waiting for transfers between devices: 114 us -> 185 us  [send(): return lax.ppermute(value, AXES, pairs)]
    pallas_call x2 -> x11, Pallas kernels: 19.6 us -> 54.2 us  [the longest x4 26.9 us: project_down(): pl.pallas_call(kernel, grid=(1,), in_specs=[SMEM_SPEC, pl.BlockSpec((half...]
    ppermute x33 -> x66, starting transfers between devices: 35.5 us -> 70.1 us  [send(): return lax.ppermute(value, AXES, pairs)]
    all_gather x1 -> x0, blocking collectives: 23 us -> none  [body(): lax.all_gather(both, 'req', axis=0, axis_index_groups=same_xzl, tiled=True)]
    convert_element_type x9 -> x0, other arithmetic: 21.9 us -> none  [the longest x4 10.4 us: body(): came = spread(pair.astype(BF16), 'req', same_xzl).astype(F32)]
    all_to_all x7 -> x2, starting transfers between devices: 27.6 us -> 6.69 us  [spread(): lax.all_to_all(value, axes, 0, 0, axis_index_groups=groups, tiled=True)]
  transfers between devices with their start and end apart: 42 -> 68, of which waited for: 20 -> 28; matrix products, arithmetic and copies ran while one was open for 11% -> 2% of each run, Pallas kernels for 14% -> 29%
where the time goes in v4:
time: 434 us; the launch traced here: 433 us
  waiting for transfers between devices  189 us (44%)
  Pallas kernels  142 us (33%)
  starting transfers between devices  76.8 us (18%)
  local copies, waits for them, and re-layouts  22.6 us (5%)
    ppermute x66, waiting for transfers between devices, send(): return lax.ppermute(value, AXES, pairs)  185 us
    ppermute x66, starting transfers between devices, send(): return lax.ppermute(value, AXES, pairs)  70.1 us
    pallas_call x1, Pallas kernels, gated(): pl.pallas_call(kernel, in_specs=[SMEM_SPEC] + [VMEM_SPEC] * 3 + [HBM_SPEC...  31.5 us
    pallas_call x4, Pallas kernels, project_down(): pl.pallas_call(kernel, grid=(1,), in_specs=[SMEM_SPEC, pl.BlockSpec((half...  26.9 us
    pallas_call x1, Pallas kernels, project_qkv(): pl.pallas_call(kernel, in_specs=[SMEM_SPEC] + [VMEM_SPEC] * 4 + [HBM_SPEC...  20.1 us
    pallas_call x4, Pallas kernels, project_out(): pl.pallas_call(kernel, in_specs=[SMEM_SPEC, SMEM_SPEC] + [VMEM_SPEC] * (4...  18.6 us
    unnamed x149, local copies, waits for them, and re-layouts  12.5 us
  transfers between devices with their start and end apart: 68, of which 28 were waited for; matrix products, arithmetic and copies ran while one was open for 2% of the time, Pallas kernels for 29%

profile of v4, /device:TPU:0, one launch (start us, length us, event | category | flops | bytes accessed | tf_op | source)
XLA Modules:
  0.0 432.7 jit_solution(4992489746423619246)
XLA Ops:
  40.5 7.6 %collective-permute-done.6.refs_7_ = bf16[256,768]{1,0:T(8,128)(2,1)S(1)} collective-permute-done((bf16[256,768]{1,0:T(8,128)(2,1)}, bf16[256,768]{1,0:T(8,128)(2,1)S(1)}, u32[]{:S(2)}, u32[]{:S(2)}) %collective-permute-start.6) | collective-permute-done | bytes 393248 | tf_op jit(solution)/shard_map/ppermute | solution.py:693
  48.1 6.0 %collective-permute-done.7.refs_11_ = bf16[256,768]{1,0:T(8,128)(2,1)S(1)} collective-permute-done((bf16[256,768]{1,0:T(8,128)(2,1)}, bf16[256,768]{1,0:T(8,128)(2,1)S(1)}, u32[]{:S(2)}, u32[]{:S(2)}) %collective-permute-start.7) | collective-permute-done | bytes 393248 | tf_op jit(solution)/shard_map/ppermute | solution.py:693
  61.1 5.8 %collective-permute-done.10.refs_2_ = bf16[256,512]{1,0:T(8,128)(2,1)S(1)} collective-permute-done((bf16[256,512]{1,0:T(8,128)(2,1)S(1)}, bf16[256,512]{1,0:T(8,128)(2,1)S(1)}, u32[]{:S(2)}, u32[]{:S(2)}) %collective-permute-start.10) | collective-permute-done | bytes 262176 | tf_op jit(solution)/shard_map/ppermute | solution.py:693
  68.1 7.8 %tables.1 = (s32[2,768,1]{2,1,0:T(8,128)}, s32[2,1,768]{2,1,0:T(1,128)}, s32[1536,1]{1,0:T(8,128)}, f32[1536,128]{1,0:T(8,128)}, f32[1536,128]{1,0:T(8,128)}, /*index=5*/s32[1536,1]{1,0:T(8,128)}) custom-call(s32[4,8]{1,0:T(4,128)} %get-tuple-element.936.len_ref, s32[4,8]{1,0:T(4,128)} %get-tuple-element.935.ad_ref, s32[4]{0:T(128)} %get-tuple-element.562.at_ref), custom_call_target="tpu_custom_call" | custom-call | flops 1000 | bytes 1000 | tf_op jit(solution)/shard_map/tables/pallas_call | solution.py:215
  75.9 10.0 %collective-permute-done.9.refs_1_ = bf16[256,512]{1,0:T(8,128)(2,1)S(1)} collective-permute-done((bf16[256,512]{1,0:T(8,128)(2,1)S(1)}, bf16[256,512]{1,0:T(8,128)(2,1)S(1)}, u32[]{:S(2)}, u32[]{:S(2)}) %collective-permute-start.9) | collective-permute-done | bytes 262176 | tf_op jit(solution)/shard_map/ppermute | solution.py:693
  98.0 20.1 %project_qkv.1.q.k.v = bf16[1536,768]{1,0:T(8,128)(2,1)} custom-call(s32[13]{0:T(128)} %stack.195.at_ref, s32[1536,1]{1,0:T(8,128)} %get-tuple-element.712.adapter_ref, bf16[2048,256]{1,0:T(8,128)(2,1)} %a_ref, f32[1536,128]{1,0:T(8,128)} %get-tuple-element.650.cos_ref, f32[1536,128]{1,0:T(8,128)} %get-tuple-element.651.sin_ref, ...), custom_call_target="tpu_custom_call" | custom-call | flops 1000 | bytes 1000 | tf_op jit(solution)/shard_map/project_qkv/pallas_call | solution.py:311
  131.3 8.4 %attend.1.attn_ref = bf16[1536,256]{1,0:T(8,128)(2,1)} custom-call(bf16[1536,768]{1,0:T(8,128)(2,1)} %project_qkv.1.q.k.v, bf16[1536,768]{1,0:T(8,128)(2,1)} %project_qkv.1.q.k.v, bf16[1536,768]{1,0:T(8,128)(2,1)} %project_qkv.1.q.k.v, s32[2,768,1]{2,1,0:T(8,128)} %get-tuple-element.682.column_ref, s32[2,1,768]{2,1,0:T(1,128)} %get-tuple-element.683.line_ref), custom_call_target="tpu_custom_call" | custom-call | flops 1000 | bytes 1000 | tf_op jit(solution)/shard_map/attend/pallas_call | solution.py:350
  140.8 14.6 %collective-permute-done.20.refs_25_ = bf16[512,256]{1,0:T(8,128)(2,1)S(1)} collective-permute-done((bf16[512,256]{1,0:T(8,128)(2,1)S(1)}, bf16[512,256]{1,0:T(8,128)(2,1)S(1)}, u32[]{:S(2)}, u32[]{:S(2)}) %collective-permute-start.20) | collective-permute-done | bytes 262176 | tf_op jit(solution)/shard_map/ppermute | solution.py:693
  182.9 20.5 %collective-permute-done.31.refs_13_ = bf16[256,1024]{1,0:T(8,128)(2,1)S(1)} collective-permute-done((bf16[256,1024]{1,0:T(8,128)(2,1)S(1)}, bf16[256,1024]{1,0:T(8,128)(2,1)S(1)}, u32[]{:S(2)}, u32[]{:S(2)}) %collective-permute-start.31) | collective-permute-done | bytes 524320 | tf_op jit(solution)/shard_map/ppermute | solution.py:693
  204.9 9.0 %collective-permute-done.32.refs_14_ = bf16[256,1024]{1,0:T(8,128)(2,1)S(1)} collective-permute-done((bf16[256,1024]{1,0:T(8,128)(2,1)S(1)}, bf16[256,1024]{1,0:T(8,128)(2,1)S(1)}, u32[]{:S(2)}, u32[]{:S(2)}) %collective-permute-start.32) | collective-permute-done | bytes 524320 | tf_op jit(solution)/shard_map/ppermute | solution.py:693
  216.9 9.2 %collective-permute-done.25.refs_2_ = bf16[192,1024]{1,0:T(8,128)(2,1)S(1)} collective-permute-done((bf16[192,1024]{1,0:T(8,128)(2,1)}, bf16[192,1024]{1,0:T(8,128)(2,1)S(1)}, u32[]{:S(2)}, u32[]{:S(2)}) %collective-permute-start.25) | collective-permute-done | bytes 393248 | tf_op jit(solution)/shard_map/ppermute | solution.py:693
  226.2 7.7 %collective-permute-done.26.refs_3_ = bf16[192,1024]{1,0:T(8,128)(2,1)S(1)} collective-permute-done((bf16[192,1024]{1,0:T(8,128)(2,1)}, bf16[192,1024]{1,0:T(8,128)(2,1)S(1)}, u32[]{:S(2)}, u32[]{:S(2)}) %collective-permute-start.26) | collective-permute-done | bytes 393248 | tf_op jit(solution)/shard_map/ppermute | solution.py:693
  246.9 11.3 %collective-permute-done.34.refs_1_ = bf16[192,2048]{1,0:T(8,128)(2,1)S(1)} collective-permute-done((bf16[192,2048]{1,0:T(8,128)(2,1)}, bf16[192,2048]{1,0:T(8,128)(2,1)S(1)}, u32[]{:S(2)}, u32[]{:S(2)}) %collective-permute-start.34) | collective-permute-done | bytes 786464 | tf_op jit(solution)/shard_map/ppermute | solution.py:693
  258.7 12.4 %collective-permute-done.35.refs_2_ = bf16[192,2048]{1,0:T(8,128)(2,1)S(1)} collective-permute-done((bf16[192,2048]{1,0:T(8,128)(2,1)}, bf16[192,2048]{1,0:T(8,128)(2,1)S(1)}, u32[]{:S(2)}, u32[]{:S(2)}) %collective-permute-start.35) | collective-permute-done | bytes 786464 | tf_op jit(solution)/shard_map/ppermute | solution.py:693
  277.9 8.3 %collective-permute-done.42.refs_3_ = bf16[96,2048]{1,0:T(8,128)(2,1)S(1)} collective-permute-done((bf16[96,2048]{1,0:T(8,128)(2,1)S(1)}, bf16[96,2048]{1,0:T(8,128)(2,1)S(1)}, u32[]{:S(2)}, u32[]{:S(2)}) %collective-permute-start.42) | collective-permute-done | bytes 393248 | tf_op jit(solution)/shard_map/ppermute | solution.py:693
  288.2 13.4 %collective-permute-done.41.refs_1_.refs_2_ = bf16[1024,256]{1,0:T(8,128)(2,1)S(1)} collective-permute-done((bf16[1024,256]{1,0:T(8,128)(2,1)S(1)}, bf16[1024,256]{1,0:T(8,128)(2,1)S(1)}, u32[]{:S(2)}, u32[]{:S(2)}) %collective-permute-start.41) | collective-permute-done | bytes 524320 | tf_op jit(solution)/shard_map/ppermute | solution.py:693
  311.4 31.5 %gated.1.h_ref = bf16[1536,1280]{1,0:T(8,128)(2,1)} custom-call(s32[12]{0:T(128)} %stack.179.place_ref, s32[1536,1]{1,0:T(8,128)} %get-tuple-element.874.adapter_ref, bf16[2048,256]{1,0:T(8,128)(2,1)} %ag_ref, bf16[2048,256]{1,0:T(8,128)(2,1)} %au_ref, bf16[192,2048]{1,0:T(8,128)(2,1)} %get-tuple-element.882.refs_0_, bf16[192,2048]{1,0:T(8,128)(2,1)} %copy-done.12, ...), custom_call_target="tpu_custom_call" | custom-call | flops 1000 | bytes 1000 | tf_op jit(solution)/shard_map/gated/pallas_call | solution.py:537
  346.4 6.7 %project_down.4 = bf16[768,1024]{1,0:T(8,128)(2,1)} custom-call(s32[1]{0:T(128)} %bitcast.1.at_ref, bf16[1536,1280]{1,0:T(8,128)(2,1)} %gated.1.h_ref, bf16[256,2048]{1,0:T(8,128)(2,1)} %refs_1_.1, bf16[2048,256]{1,0:T(8,128)(2,1)} %bitcast.42, bf16[2048,256]{1,0:T(8,128)(2,1)} %copy-done.3), custom_call_target="tpu_custom_call" | custom-call | flops 1000 | bytes 1000 | tf_op jit(solution)/shard_map/project_down/pallas_call | solution.py:607
  359.4 6.6 %project_down.6 = bf16[768,1024]{1,0:T(8,128)(2,1)} custom-call(s32[1]{0:T(128)} %bitcast.5.at_ref, bf16[1536,1280]{1,0:T(8,128)(2,1)} %gated.1.h_ref, bf16[256,2048]{1,0:T(8,128)(2,1)} %refs_1_.1, bf16[1024,256]{1,0:T(8,128)(2,1)} %copy-done.7, bf16[1024,256]{1,0:T(8,128)(2,1)} %copy-done.8, bf16[1024,256]{1,0:T(8,128)(2,1)} %copy-done.9, ...), custom_call_target="tpu_custom_call" | custom-call | flops 1000 | bytes 1000 | tf_op jit(solution)/shard_map/project_down/pallas_call | solution.py:607
  367.3 6.8 %project_down.5 = (bf16[192,1024]{1,0:T(8,128)(2,1)}, bf16[192,1024]{1,0:T(8,128)(2,1)}, bf16[192,1024]{1,0:T(8,128)(2,1)}, bf16[192,1024]{1,0:T(8,128)(2,1)}) custom-call(s32[1]{0:T(128)} %bitcast.1.at_ref, bf16[1536,1280]{1,0:T(8,128)(2,1)} %gated.1.h_ref, bf16[768,1024]{1,0:T(8,128)(2,1)} %copy-done.20, bf16[256,2048]{1,0:T(8,128)(2,1)} %refs_1_.1, ...), custom_call_target="tpu_custom_call" | custom-call | flops 1000 | bytes 1000 | tf_op jit(solution)/shard_map/project_down/pallas_call | solution.py:607
  378.8 6.8 %project_down.7 = (bf16[192,1024]{1,0:T(8,128)(2,1)}, bf16[192,1024]{1,0:T(8,128)(2,1)}, bf16[192,1024]{1,0:T(8,128)(2,1)}, bf16[192,1024]{1,0:T(8,128)(2,1)}) custom-call(s32[1]{0:T(128)} %bitcast.5.at_ref, bf16[1536,1280]{1,0:T(8,128)(2,1)} %gated.1.h_ref, bf16[768,1024]{1,0:T(8,128)(2,1)} %copy-done.19, bf16[256,2048]{1,0:T(8,128)(2,1)} %refs_1_.1, ...), custom_call_target="tpu_custom_call" | custom-call | flops 1000 | bytes 1000 | tf_op jit(solution)/shard_map/project_down/pallas_call | solution.py:607
  389.2 7.1 %collective-permute-done.54.refs_3_ = bf16[192,1024]{1,0:T(8,128)(2,1)S(1)} collective-permute-done((bf16[192,1024]{1,0:T(8,128)(2,1)}, bf16[192,1024]{1,0:T(8,128)(2,1)S(1)}, u32[]{:S(2)}, u32[]{:S(2)}) %collective-permute-start.54) | collective-permute-done | bytes 393248 | tf_op jit(solution)/shard_map/ppermute | solution.py:693
  404.6 7.8 %collective-permute-done.62.refs_3_ = bf16[192,1024]{1,0:T(8,128)(2,1)S(1)} collective-permute-done((bf16[192,1024]{1,0:T(8,128)(2,1)}, bf16[192,1024]{1,0:T(8,128)(2,1)S(1)}, u32[]{:S(2)}, u32[]{:S(2)}) %collective-permute-start.62) | collective-permute-done | bytes 393248 | tf_op jit(solution)/shard_map/ppermute | solution.py:693
  417.0 9.4 %collective-permute-done.64.refs_6_ = bf16[192,1024]{1,0:T(8,128)(2,1)S(1)} collective-permute-done((bf16[192,1024]{1,0:T(8,128)(2,1)}, bf16[192,1024]{1,0:T(8,128)(2,1)S(1)}, u32[]{:S(2)}, u32[]{:S(2)}) %collective-permute-start.64) | collective-permute-done | bytes 393248 | tf_op jit(solution)/shard_map/ppermute | solution.py:693
  (305 shorter events, 177.4 us)
Async XLA Ops:
  54.1 31.8 %collective-permute-start.8 = (bf16[2,256,1024]{2,1,0:T(8,128)(2,1)}, bf16[2,256,1024]{2,1,0:T(8,128)(2,1)S(1)}, u32[]{:S(2)}, u32[]{:S(2)}) collective-permute-start(bf16[2,256,1024]{2,1,0:T(8,128)(2,1)} %get-tuple-element.551), channel_id=1, source_target_pairs={{0,4},{1,5},{2,6},{3,7},{4,0},{5,1},{6,2},{7,3},{8,12},{9,13},{10,... | collective-permute-start | bytes 3145736 | tf_op jit(solution)/shard_map/ppermute | solution.py:693
  55.2 30.7 %collective-permute-start.11 = (bf16[192,2048]{1,0:T(8,128)(2,1)S(1)}, bf16[192,2048]{1,0:T(8,128)(2,1)S(1)}, u32[]{:S(2)}, u32[]{:S(2)}) collective-permute-start(bf16[192,2048]{1,0:T(8,128)(2,1)S(1)} %collective-permute-done.5.refs_0_), channel_id=1, source_target_pairs={{0,2},{1,3},{2,0},{3,1},{4,6},{5,7},{6,4},{7,5},{8,10},{9,11},{10,... | collective-permute-start | bytes 2359304 | tf_op jit(solution)/shard_map/ppermute | solution.py:693
  57.3 28.6 %collective-permute-start.12 = (bf16[256,768]{1,0:T(8,128)(2,1)}, bf16[256,768]{1,0:T(8,128)(2,1)S(1)}, u32[]{:S(2)}, u32[]{:S(2)}) collective-permute-start(bf16[256,768]{1,0:T(8,128)(2,1)} %collective-permute-done.3.refs_10_), channel_id=1, source_target_pairs={{0,8},{1,9},{2,10},{3,11},{4,12},{5,13},{6,14},{7,15},{8,16},{9,17... | collective-permute-start | bytes 1179656 | tf_op jit(solution)/shard_map/ppermute | solution.py:693
  58.5 27.4 %collective-permute-start.13 = (bf16[256,768]{1,0:T(8,128)(2,1)S(1)}, bf16[256,768]{1,0:T(8,128)(2,1)S(1)}, u32[]{:S(2)}, u32[]{:S(2)}) collective-permute-start(bf16[256,768]{1,0:T(8,128)(2,1)S(1)} %collective-permute-done.6.refs_7_), channel_id=1, source_target_pairs={{0,24},{1,25},{2,26},{3,27},{4,28},{5,29},{6,30},{7,31},{8,0},{9,1... | collective-permute-start | bytes 1179656 | tf_op jit(solution)/shard_map/ppermute | solution.py:693
  91.1 31.0 %collective-permute-start.16 = (bf16[512,1024]{1,0:T(8,128)(2,1)}, bf16[512,1024]{1,0:T(8,128)(2,1)S(1)}, u32[]{:S(2)}, u32[]{:S(2)}) collective-permute-start(bf16[512,1024]{1,0:T(8,128)(2,1)} %get-tuple-element.635), channel_id=1, source_target_pairs={{0,8},{1,9},{2,10},{3,11},{4,12},{5,13},{6,14},{7,15},{8,0},{9,1},... | collective-permute-start | bytes 3145736 | tf_op jit(solution)/shard_map/ppermute | solution.py:693
  91.7 30.3 %collective-permute-start.19 = (bf16[512,1024]{1,0:T(8,128)(2,1)}, bf16[512,1024]{1,0:T(8,128)(2,1)}, u32[]{:S(2)}, u32[]{:S(2)}) collective-permute-start(bf16[512,1024]{1,0:T(8,128)(2,1)} %get-tuple-element.892.refs_10_), channel_id=1, source_target_pairs={{0,2},{1,3},{2,0},{3,1},{4,6},{5,7},{6,4},{7,5},{8,10},{9,11},{10,... | collective-permute-start | bytes 3145736 | tf_op jit(solution)/shard_map/ppermute | solution.py:693
  93.2 28.5 %collective-permute-start.17 = (bf16[256,256]{1,0:T(8,128)(2,1)}, bf16[256,256]{1,0:T(8,128)(2,1)S(1)}, u32[]{:S(2)}, u32[]{:S(2)}) collective-permute-start(bf16[256,256]{1,0:T(8,128)(2,1)} %slice.38), channel_id=1, source_target_pairs={{0,8},{1,9},{2,10},{3,11},{4,12},{5,13},{6,14},{7,15},{8,16},{9,17... | collective-permute-start | bytes 393224 | tf_op jit(solution)/shard_map/ppermute | solution.py:693
  94.7 27.3 %collective-permute-start.18 = (bf16[256,256]{1,0:T(8,128)(2,1)S(1)}, bf16[256,256]{1,0:T(8,128)(2,1)S(1)}, u32[]{:S(2)}, u32[]{:S(2)}) collective-permute-start(bf16[256,256]{1,0:T(8,128)(2,1)S(1)} %slice.39), channel_id=1, source_target_pairs={{0,24},{1,25},{2,26},{3,27},{4,28},{5,29},{6,30},{7,31},{8,0},{9,1... | collective-permute-start | bytes 393224 | tf_op jit(solution)/shard_map/ppermute | solution.py:693
  122.7 32.7 %all-to-all-start.1 = ((bf16[4,512,256]{2,1,0:T(8,128)(2,1)}), bf16[4,512,256]{2,1,0:T(8,128)(2,1)S(1)}, u32[]{:S(2)}, u32[]{:S(2)}) async-start(bf16[4,512,256]{2,1,0:T(8,128)(2,1)} %bitcast.45), calls=%async_computation.1 | async-start | bytes 2097152 | tf_op jit(solution)/shard_map/all_to_all | solution.py:719
  126.2 29.2 %collective-permute-start.21 = (bf16[512,1024]{1,0:T(8,128)(2,1)S(1)}, bf16[512,1024]{1,0:T(8,128)(2,1)}, u32[]{:S(2)}, u32[]{:S(2)}) collective-permute-start(bf16[512,1024]{1,0:T(8,128)(2,1)S(1)} %collective-permute-done.16.refs_11_), channel_id=1, source_target_pairs={{0,2},{1,3},{2,0},{3,1},{4,6},{5,7},{6,4},{7,5},{8,10},{9,11},{10,... | collective-permute-start | bytes 3145736 | tf_op jit(solution)/shard_map/ppermute | solution.py:693
  128.7 26.7 %collective-permute-start.22 = (bf16[256,1024]{1,0:T(8,128)(2,1)S(1)}, bf16[256,1024]{1,0:T(8,128)(2,1)S(1)}, u32[]{:S(2)}, u32[]{:S(2)}) collective-permute-start(bf16[256,1024]{1,0:T(8,128)(2,1)S(1)} %get-tuple-element.934), channel_id=1, source_target_pairs={{0,16},{1,17},{2,18},{3,19},{4,20},{5,21},{6,22},{7,23},{8,24},{9,... | collective-permute-start | bytes 1572872 | tf_op jit(solution)/shard_map/ppermute | solution.py:693
  165.3 38.1 %collective-permute-start.31 = (bf16[256,1024]{1,0:T(8,128)(2,1)S(1)}, bf16[256,1024]{1,0:T(8,128)(2,1)S(1)}, u32[]{:S(2)}, u32[]{:S(2)}) collective-permute-start(bf16[256,1024]{1,0:T(8,128)(2,1)S(1)} %copy-done.43), channel_id=1, source_target_pairs={{0,16},{1,17},{2,18},{3,19},{4,20},{5,21},{6,22},{7,23},{8,24},{9,... | collective-permute-start | bytes 1572872 | tf_op jit(solution)/shard_map/ppermute | solution.py:693
  168.0 45.9 %collective-permute-start.32 = (bf16[256,1024]{1,0:T(8,128)(2,1)S(1)}, bf16[256,1024]{1,0:T(8,128)(2,1)S(1)}, u32[]{:S(2)}, u32[]{:S(2)}) collective-permute-start(bf16[256,1024]{1,0:T(8,128)(2,1)S(1)} %copy-done.44), channel_id=1, source_target_pairs={{0,16},{1,17},{2,18},{3,19},{4,20},{5,21},{6,22},{7,23},{8,24},{9,... | collective-permute-start | bytes 1572872 | tf_op jit(solution)/shard_map/ppermute | solution.py:693
  174.0 41.6 %collective-permute-start.28 = (bf16[192,1024]{1,0:T(8,128)(2,1)}, bf16[192,1024]{1,0:T(8,128)(2,1)S(1)}, u32[]{:S(2)}, u32[]{:S(2)}) collective-permute-start(bf16[192,1024]{1,0:T(8,128)(2,1)} %get-tuple-element.744), channel_id=1, source_target_pairs={{0,2},{1,3},{2,0},{3,1},{4,6},{5,7},{6,4},{7,5},{8,10},{9,11},{10,... | collective-permute-start | bytes 1179656 | tf_op jit(solution)/shard_map/ppermute | solution.py:693
  175.5 41.4 %collective-permute-start.29 = (bf16[192,1024]{1,0:T(8,128)(2,1)}, bf16[192,1024]{1,0:T(8,128)(2,1)S(1)}, u32[]{:S(2)}, u32[]{:S(2)}) collective-permute-start(bf16[192,1024]{1,0:T(8,128)(2,1)} %get-tuple-element.745), channel_id=1, source_target_pairs={{0,4},{1,5},{2,6},{3,7},{4,0},{5,1},{6,2},{7,3},{8,12},{9,13},{10,... | collective-permute-start | bytes 1179656 | tf_op jit(solution)/shard_map/ppermute | solution.py:693
  177.1 39.8 %collective-permute-start.30 = (bf16[192,1024]{1,0:T(8,128)(2,1)}, bf16[192,1024]{1,0:T(8,128)(2,1)S(1)}, u32[]{:S(2)}, u32[]{:S(2)}) collective-permute-start(bf16[192,1024]{1,0:T(8,128)(2,1)} %get-tuple-element.746), channel_id=1, source_target_pairs={{0,6},{1,7},{2,4},{3,5},{4,2},{5,3},{6,0},{7,1},{8,14},{9,15},{10,... | collective-permute-start | bytes 1179656 | tf_op jit(solution)/shard_map/ppermute | solution.py:693
  241.7 29.4 %collective-permute-start.35 = (bf16[192,2048]{1,0:T(8,128)(2,1)}, bf16[192,2048]{1,0:T(8,128)(2,1)S(1)}, u32[]{:S(2)}, u32[]{:S(2)}) collective-permute-start(bf16[192,2048]{1,0:T(8,128)(2,1)} %get-tuple-element.882.refs_0_), channel_id=1, source_target_pairs={{0,8},{1,9},{2,10},{3,11},{4,12},{5,13},{6,14},{7,15},{8,0},{9,1},... | collective-permute-start | bytes 2359304 | tf_op jit(solution)/shard_map/ppermute | solution.py:693
  243.0 28.7 %collective-permute-start.33 = (bf16[192,2048]{1,0:T(8,128)(2,1)}, bf16[192,2048]{1,0:T(8,128)(2,1)S(1)}, u32[]{:S(2)}, u32[]{:S(2)}) collective-permute-start(bf16[192,2048]{1,0:T(8,128)(2,1)} %get-tuple-element.882.refs_0_), channel_id=1, source_target_pairs={{0,1},{1,0},{2,3},{3,2},{4,5},{5,4},{6,7},{7,6},{8,9},{9,8},{10,11... | collective-permute-start | bytes 2359304 | tf_op jit(solution)/shard_map/ppermute | solution.py:693
  243.0 28.1 %collective-permute-start.36 = (bf16[256,1024]{1,0:T(8,128)(2,1)S(1)}, bf16[256,1024]{1,0:T(8,128)(2,1)S(1)}, u32[]{:S(2)}, u32[]{:S(2)}) collective-permute-start(bf16[256,1024]{1,0:T(8,128)(2,1)S(1)} %copy-done.42), channel_id=1, source_target_pairs={{0,16},{1,17},{2,18},{3,19},{4,20},{5,21},{6,22},{7,23},{8,24},{9,... | collective-permute-start | bytes 1572872 | tf_op jit(solution)/shard_map/ppermute | solution.py:693
  275.0 31.4 %collective-permute-start.39 = (bf16[192,2048]{1,0:T(8,128)(2,1)S(1)}, bf16[192,2048]{1,0:T(8,128)(2,1)S(1)}, u32[]{:S(2)}, u32[]{:S(2)}) collective-permute-start(bf16[192,2048]{1,0:T(8,128)(2,1)S(1)} %collective-permute-done.34.refs_1_), channel_id=1, source_target_pairs={{0,1},{1,0},{2,3},{3,2},{4,5},{5,4},{6,7},{7,6},{8,9},{9,8},{10,11... | collective-permute-start | bytes 2359304 | tf_op jit(solution)/shard_map/ppermute | solution.py:693
  275.0 31.4 %collective-permute-start.40 = (bf16[192,2048]{1,0:T(8,128)(2,1)S(1)}, bf16[192,2048]{1,0:T(8,128)(2,1)S(1)}, u32[]{:S(2)}, u32[]{:S(2)}) collective-permute-start(bf16[192,2048]{1,0:T(8,128)(2,1)S(1)} %collective-permute-done.35.refs_2_), channel_id=1, source_target_pairs={{0,1},{1,0},{2,3},{3,2},{4,5},{5,4},{6,7},{7,6},{8,9},{9,8},{10,11... | collective-permute-start | bytes 2359304 | tf_op jit(solution)/shard_map/ppermute | solution.py:693
  308.9 36.4 %collective-permute-start.48 = (bf16[2048,256]{1,0:T(8,128)(2,1)S(1)}, bf16[2048,256]{1,0:T(8,128)(2,1)S(1)}, u32[]{:S(2)}, u32[]{:S(2)}) collective-permute-start(bf16[2048,256]{1,0:T(8,128)(2,1)S(1)} %bitcast.41), channel_id=1, source_target_pairs={{0,2},{1,3},{2,0},{3,1},{4,6},{5,7},{6,4},{7,5},{8,10},{9,11},{10,... | collective-permute-start | bytes 3145736 | tf_op jit(solution)/shard_map/ppermute | solution.py:693
  309.5 33.4 %collective-permute-start.49 = (bf16[1024,256]{1,0:T(8,128)(2,1)}, bf16[1024,256]{1,0:T(8,128)(2,1)S(1)}, u32[]{:S(2)}, u32[]{:S(2)}) collective-permute-start(bf16[1024,256]{1,0:T(8,128)(2,1)} %get-tuple-element.878), channel_id=1, source_target_pairs={{0,16},{1,17},{2,18},{3,19},{4,20},{5,21},{6,22},{7,23},{8,24},{9,... | collective-permute-start | bytes 1572872 | tf_op jit(solution)/shard_map/ppermute | solution.py:693
  309.9 35.4 %collective-permute-start.50 = (bf16[1024,256]{1,0:T(8,128)(2,1)S(1)}, bf16[1024,256]{1,0:T(8,128)(2,1)S(1)}, u32[]{:S(2)}, u32[]{:S(2)}) collective-permute-start(bf16[1024,256]{1,0:T(8,128)(2,1)S(1)} %collective-permute-done.41.refs_1_.refs_2_), channel_id=1, source_target_pairs={{0,2},{1,3},{2,0},{3,1},{4,6},{5,7},{6,4},{7,5},{8,10},{9,11},{10,... | collective-permute-start | bytes 1572872 | tf_op jit(solution)/shard_map/ppermute | solution.py:693
  (118 other events, 1936.6 us)

commit v5 on v4

--- a/solution.py
+++ b/solution.py
@@ -47,40 +47,9 @@
     return pltpu.make_async_copy(source, target, semaphore)
 
 
-def run_all(copies):
-    for copy in copies:
-        copy.start()
-    for copy in copies:
-        copy.wait()
-
-
 SMEM_SPEC = pl.BlockSpec(memory_space=pltpu.SMEM)
 VMEM_SPEC = pl.BlockSpec(memory_space=VM)
 HBM_SPEC = pl.BlockSpec(memory_space=pl.ANY)
-
-
-def split_heads(w_qkv, w_out, x):
-    rows, _, columns = w_qkv.shape
-    local = columns // 2
-    width = w_out.shape[1]
-
-    def kernel(x_ref, qkv_ref, out_ref, *outs):
-        for which in range(2):
-            at = mm(x_ref[0] ^ which, local)
-            for i in range(3):
-                outs[which][:, i * local : (i + 1) * local] = qkv_ref[:, i, at]
-            outs[2 + which][...] = out_ref[at, :]
-
-    return pl.pallas_call(
-        kernel,
-        in_specs=[SMEM_SPEC, VMEM_SPEC, VMEM_SPEC],
-        out_specs=[VMEM_SPEC] * 4,
-        out_shape=[jax.ShapeDtypeStruct((rows, 3 * local), BF16)] * 2
-        + [jax.ShapeDtypeStruct((local, width), BF16)] * 2,
-        compiler_params=PARAMS,
-        cost_estimate=COST,
-        name="split_heads",
-    )(x, w_qkv, w_out)
 
 
 def norm_rows(tokens, row, T):
@@ -260,7 +229,7 @@
     total_rows, columns, rank = 2 * slots, b.shape[1], b.shape[0]
     piece, size, tile = pieces[0].shape[0], width // len(weights), columns // 3
     n_pieces, n_weights = len(pieces), len(weights)
-    chunk = total_rows // 4
+    chunk = total_rows // 2
     column = adapter
 
     def kernel(at_ref, adapter_ref, a_ref, cos_ref, sin_ref, own_ref, b_ref, *refs):
@@ -368,10 +337,11 @@
 def project_out(attn, adapter, a, b, weights, order, scalars, T, came=None):
     total_rows, depth = attn.shape
     n, slots, piece, Y = len(weights), total_rows // 2, total_rows // 2 // T, T // 2
+    extra = list(came or [])
     flat = [p for w in weights for p in w]
     size = sum(p.shape[1] for p in flat) // n // 2
     half, columns = total_rows // 2, n * 2 * size
-    extra = [] if came is None else [came]
+    per = n // max(1, len(extra))
 
     def kernel(order_ref, at_ref, attn_ref, adapter_ref, a_ref, b_ref, *refs):
         ws, outs, rows, low = refs[: len(flat)], refs[len(flat) + len(extra) : -2], *refs[-2:]
@@ -398,7 +368,8 @@
                 if came is None:
                     outs[0][:, to] = total.astype(BF16)
                 else:
-                    total = (total + refs[len(flat)][:, to].astype(F32)).astype(BF16)
+                    from_core = refs[len(flat) + k // per][:, mm(k % per * 2 + (x ^ i), size)]
+                    total = (total + from_core.astype(F32)).astype(BF16)
                     for p in range(2 * Y):
                         outs[p][:, to] = total[p * piece : (p + 1) * piece]
 
@@ -457,7 +428,7 @@
     )(row, order, tokens, *flat)
 
 
-def gated(rows, adapters, a_gate, a_up, sets, places):
+def gated(rows, adapters, a_gate, a_up, sets, places, unit):
     width = rows[0].shape[1]
     total_rows = sum(row.shape[0] for row in rows)
     units = sets[0][1].shape[1] // 2
@@ -472,7 +443,7 @@
     n_rows, n_sets = len(rows), len(sets)
     most = max(len(s[0]) for s in sets)
     steps = n_sets * tiles
-    chunk = total_rows // 4
+    chunk = total_rows // 2
     hidden_width = n_sets * units
 
     def kernel(place_ref, adapter_ref, ag_ref, au_ref, *refs):
@@ -487,7 +458,7 @@
                 for i in range(first[s], first[s + 1]):
                     yield dma(
                         w_in[i].at[:, pl.ds(g * units + t * tile, tile)],
-                        w.at[slot, g, mm(place_ref[i], flat[i].shape[0]), :],
+                        w.at[slot, g, pl.ds(pl.multiple_of(place_ref[i] * unit, unit), flat[i].shape[0]), :],
                         w_sem.at[slot, g, i - first[s]],
                     )
                 yield dma(
@@ -515,16 +486,15 @@
                 copy.wait()
             s, t = divmod(step, tiles)
 
-            @pl.loop(0, total_rows // chunk)
-            def _(m):
-                at = mm(m, chunk)
+            for m in range(total_rows // chunk):
+                at = slice(m * chunk, (m + 1) * chunk)
                 xs = x[at, :]
                 if step == 0:
                     lg[at, :] = masked(dot(xs, ag_ref[...]), adapter_ref[at, :])
                     lu[at, :] = masked(dot(xs, au_ref[...]), adapter_ref[at, :])
                 gate = dot(xs, w[slot, 0]) + dot(lg[at, :], bb[slot, 0])
                 up = dot(xs, w[slot, 1]) + dot(lu[at, :], bb[slot, 1])
-                h = (gate / (1.0 + jnp.exp(-gate)) * up).astype(BF16)
+                h = (0.5 * gate * (1.0 + jnp.tanh(0.5 * gate)) * up).astype(BF16)
                 hidden[at, step * tile : (step + 1) * tile] = h
                 more = dot(h, d_in[s][t * tile : (t + 1) * tile, :])
                 if step > 0:
@@ -566,16 +536,25 @@
     n, n_sets, n_weights = 4, len(sets), len(flat)
     extra = [] if came is None else [came]
 
-    def kernel(at_ref, h_ref, *refs):
+    def kernel(at_ref, h_in, *refs):
         refs = list(refs)
         came_ref = refs.pop(0) if extra else None
-        b_ref, w_in, outs, w, sems = refs[0], refs[1 : 1 + n_weights], refs[1 + n_weights : -2], *refs[-2:]
+        b_ref, w_in, outs = refs[0], refs[1 : 1 + n_weights], refs[1 + n_weights : -4]
+        w, h_ref, sems, h_sems = refs[-4:]
         copies = [
             dma(
                 b_ref.at[:, mm(at_ref[0], n * size)],
                 w.at[n_sets * units : n_sets * units + rank, :],
                 sems.at[n_sets * n],
             )
+        ]
+        h_copies = [
+            dma(
+                h_in.at[pl.ds(which * half + m * 2 * piece, 2 * piece), :],
+                h_ref.at[pl.ds(m * 2 * piece, 2 * piece), :],
+                h_sems.at[m],
+            )
+            for m in range(2)
         ]
         it = iter(w_in)
         for k, group in enumerate(sets):
@@ -586,13 +565,17 @@
                     copies.append(
                         dma(
                             ref.at[pl.ds(i * units, units), :],
-                            w.at[k * units : (k + 1) * units, place * size : (place + 1) * size],
+                            w.at[k * units : (k + 1) * units, mm(at_ref[1] ^ place, size)],
                             sems.at[k * n + place],
                         )
                     )
                     place += 1
-        run_all(copies)
+        for copy in copies + h_copies:
+            copy.start()
+        for copy in copies:
+            copy.wait()
         for m in range(2):
+            h_copies[m].wait()
             here = slice(m * 2 * piece, (m + 1) * 2 * piece)
             total = dot(h_ref[here, :], w[...])
             if came is None:
@@ -606,15 +589,16 @@
         shapes = [jax.ShapeDtypeStruct((piece, n * size), BF16)] * 4
     out = pl.pallas_call(
         kernel,
-        grid=(1,),
-        in_specs=[SMEM_SPEC, pl.BlockSpec((half, depth), lambda i: (which, 0))]
+        in_specs=[SMEM_SPEC, HBM_SPEC]
         + [VMEM_SPEC] * len(extra)
         + [HBM_SPEC] * (1 + n_weights),
         out_specs=[VMEM_SPEC] * len(shapes),
         out_shape=shapes,
         scratch_shapes=[
             VM((depth, n * size), BF16),
+            VM((half, depth), BF16),
             pltpu.SemaphoreType.DMA((n_sets * n + 1,)),
+            pltpu.SemaphoreType.DMA((2,)),
         ],
         compiler_params=PARAMS,
         cost_estimate=COST,
@@ -746,24 +730,30 @@
 
         L = Live(
             tokens=tokens, both=jnp.concatenate([lengths, request_adapter], axis=1), w_gate=w_gate,
-            w_up=w_up, w_down=w_down, a_qkv=a_qkv, a_out=a_out, b_out=b_out, a_gate=a_gate,
+            w_up=w_up, a_qkv=a_qkv, a_out=a_out, b_out=b_out, a_gate=a_gate,
             a_up=a_up, b_down=b_down, b_qkv=b_qkv, b_gate=b_gate, b_up=b_up, a_down=a_down,
         )
         keys = [(k, i) for k in range(Z) for i in (0, 1)]
         order = [((z + k) % Z) * 2 + (x ^ i) for k, i in keys]
         there = [(zh + h) % ZH for h in range(ZH)]
         at = [(1 - x) * T + ((y + k) % Y) * 2 + s for s in (c, 1 - c) for k in range(Y)]
-        far_places = [h * 4 + (zl ^ j) * 2 + q for h in there[1:] for j in (0, 1) for q in (0, 1)]
-        places = ([zh * 2 + zl, zh * 2 + 1 - zl] + far_places) * Y
+        far_places = []
+        for h in there[1:]:
+            first, other = (h * 2 + zl) * 4, (h * 2 + 1 - zl) * 4
+            far_places += [first, first + 2, other, other + 1]
+        places = ([(zh * 2 + zl) * 4, (zh * 2 + 1 - zl) * 4] + far_places) * Y
         L.ints = Live(
-            t=ints([t]), order=[ints(order[:Z]), ints(order[Z:])], qkv=ints([x, *at, *order]),
+            t=ints([t]), order=[ints(order[:Z]), ints(order[Z:]), ints(order)], qkv=ints([x, *at, *order]),
             xyc=[ints([x, y, c]), ints([x, y, 1 - c])],
             zyc=ints([zl, y, c, zl * 2 + x]), z=ints([(z + k) % Z for k in range(Z)]),
-            gated=ints(places), span=[ints([h]) for h in there], b=ints([zl * 2 + x]),
+            gated=ints(places), span=[ints([h]) for h in there],
+            down=[ints([h, zl * 2 + x]) for h in there], b=ints([zl * 2 + x]),
         )
         mine = (zl * 2 + x) * quarter
-        L.split = split_heads(w_qkv, w_out, ints([x]))
-        L = fence(L)
+
+        def heads_of(w, which):
+            return cut(w, which * local, local, 2).reshape(w.shape[0], 3 * local)
+
 
         def ring_start(own):
             left = right = own
@@ -773,10 +763,9 @@
                 got[Z - k], got[k] = left, right
             return got
 
-        head, other_head, own_out, other_out = L.pop.split
-        L.first = send(other_head, to_x)
-        L.ring = [ring_start(head)]
-        L.out = send(other_out, to_x)
+        L.first = send(heads_of(w_qkv, 1 - x), to_x)
+        L.ring = [ring_start(heads_of(w_qkv, x))]
+        L.out = send(cut(w_out, (1 - x) * local, local, 0), to_x)
         L.both = spread(jnp.concatenate([L.both] * 4, axis=0), "req", same_xzl)
         L.normed, L.mine = norm_rows(L.tokens, L.ints.t, T)
         L.b = jnp.concatenate(
@@ -784,12 +773,16 @@
         )
         L.a_down = cut(L.a_down, mine, quarter, 0)
         L.b_heads = cut(L.pop.b_qkv, x * local, local, 2).reshape(rank, 3 * local)
-        L.own_out = own_out
+        L.own_out = cut(w_out, x * local, local, 0)
+        me = zl * 2 + x
+        L.down_keep = [cut(w_down, (me ^ b) * quarter, quarter, 0) for b in (0, 2)]
+        L.down_give = jnp.concatenate([cut(w_down, (me ^ b) * quarter, quarter, 0) for b in (1, 3)], 0)
         L = fence(L)
 
         L.ring.append(ring_start(L.pop.first))
         L.quarter = send(L.pop.mine, to_x)
         L.b_far = [send(L.b, from_y[k]) for k in far_y]
+        L.a_far = [send(L.a_down, from_y[k]) for k in far_y]
         L.gu, L.gu_give = pack(L.pop.w_gate, L.pop.w_up, L.ints.b)
         L.out = jnp.concatenate([L.pop.own_out, L.out], axis=1)
         L = fence(L)
@@ -811,6 +804,7 @@
         L.far_out = [send(one, z_up), send(two, z_down)]
         L.far = send(L.pop.give, to_zl)
         L.y = [[send(L.near, from_y[k]) for k in far_y]]
+        L.down_came = send(L.pop.down_give, to_x)
         column, line, adapter, cosine, sine, adapters = L.tables
         L.joined = project_qkv(
             L.pop.normed, L.pop.quarters, adapter, L.pop.a_qkv, L.pop.b_heads, cosine,
@@ -822,88 +816,94 @@
         def over_zh(w):
             return [send(w, from_zh[h]) for h in far_zh]
 
+        def relay(arrays):
+            return [[send(w, from_y[k]) for w in arrays] for k in far_y]
+
+        def out_of(chunk, core, came=None):
+            return project_out(
+                attn, adapter, L.a_out, L.b_out, blocks[chunk], L.ints.order[chunk],
+                L.ints.xyc[core], T, came,
+            )
+
         rows = L.near.shape[0] // 2
-        L.for_zh = [w[q * rows : (q + 1) * rows] for w in (L.near, L.far) for q in (0, 1)]
+        L.near_parts = [L.near[:rows], L.near[rows:]]
         L.y.append([send(L.far, from_y[k]) for k in far_y])
-        L.zh = [over_zh(L.for_zh[0])]
-        L.a_far = [send(L.a_down, from_y[k]) for k in far_y]
+        keep, down_came = L.pop.down_keep, L.pop.down_came
+        L.down_near = jnp.concatenate([keep[0], down_came[:quarter]], axis=0)
+        L.down_far = send(jnp.concatenate([keep[1], down_came[quarter:]], axis=0), to_zl)
+        L.zh0 = over_zh(L.near_parts[0])
         column, line, adapter, cosine, sine, adapters = L.pop.tables
-        L.attn = attend(L.pop.joined, column, line)
+        attn = attend(L.pop.joined, column, line)
         blocks = [(L.out[k],) if k != opposite else tuple(L.far_out) for k in range(Z)]
-        L.blocks = [blocks[:opposite], blocks[opposite:]]
-        L.adapter, L.adapters = adapter, adapters
-        L.pop.out, L.pop.far_out, L.pop.quarter
-        L.down = spread(L.pop.w_down, "req", same_xzl)
-        L = fence(L)
-
-        def out_of(L, chunk, core, came=None):
-            return project_out(
-                L.attn, L.adapter, L.a_out, L.b_out, L.blocks[chunk],
-                L.ints.order[chunk], L.ints.xyc[core], T, came,
-            )
-
-        L.zh += [over_zh(L.for_zh[1]), over_zh(L.for_zh[2])]
-        came = [send(out_of(L, chunk, 1), to_core) for chunk in (0, 1)]
-        L.sums = []
-        for chunk in (0, 1):
-            parts = out_of(L, chunk, 0, came[chunk])
-            terms = [parts[0]]
-            for i in (0, 1):
-                for k in range(Y):
-                    if i or k:
-                        terms.append(send(parts[i * Y + k], to_xy[(i, k)]))
-            L.sums.append(terms)
+        blocks = [blocks[:opposite], blocks[opposite:], blocks]
+        L.gives = [out_of(chunk, 1) for chunk in (0, 1)]
+        L.attn, L.adapter, L.adapters, L.blocks = attn, adapter, adapters, blocks
+        L.drop.out.far_out.quarter
+        L = fence(L)
+        part = rows_unit = rows // 2
+        L.far_parts = [L.far[:part], L.far[part:]]
+        L.zh2 = over_zh(L.far_parts[0])
+        L.relay0 = relay(L.zh0)
+        attn, adapter, blocks = L.pop.attn, L.pop.adapter, L.pop.blocks
+        L.parts = out_of(2, 0, [send(give, to_core) for give in L.pop.gives])
+        L.drop.a_out.b_out
+        L = fence(L)
+
+        parts = L.pop.parts
+        terms = [parts[0]]
+        for i in (0, 1):
+            for k in range(Y):
+                if i or k:
+                    terms.append(send(parts[i * Y + k], to_xy[(i, k)]))
+        L.zh3 = over_zh(L.far_parts[1])
+        L.terms = terms
         L = fence(L)
         L.hidden_state, L.normed2 = residual_norm(
-            L.pop.tokens, L.ints.t, L.ints.z, L.pop.sums
+            L.pop.tokens, L.ints.t, L.ints.z, [L.pop.terms]
         )
-        L.drop.attn.adapter.a_out.b_out.blocks
-        split = L.down.shape[0] // 2
-        L.for_down = [L.down[:split], L.down[split:]]
-        L = fence(L)
-
-        def relay(parts):
-            return [[[send(w, from_y[k]) for w in part] for k in far_y] for part in parts]
+        L.for_down = [L.pop.down_near, L.pop.down_far]
+        L = fence(L)
 
         own = L.pop.normed2
         L.rows = [own, send(own, to_x), send(own, to_zl)]
-        L.core = [send(own, to_core)]
-        L.zh_y = relay(L.zh[:2])
-        L.zh.append(over_zh(L.for_zh[3]))
+        L.relay3 = relay(L.zh3)
+        L.zh1 = over_zh(L.near_parts[1])
+        L.down_y = [[send(L.for_down[0], from_y[k]) for k in far_y]]
         L.cut = [L.rows[1][: piece // 2], L.rows[2][piece // 2 :]]
         L = fence(L)
         one, two = L.pop.cut
-        L.core += [send(row, to_core) for row in L.rows[1:]]
         L.rows += [send(one, to_zl), send(two, to_x)]
-        L.zh_y += relay(L.zh[2:])
+        L.relay1, L.relay2 = relay(L.zh1), relay(L.zh2)
         L.down_zh = [over_zh(L.for_down[0])]
         L = fence(L)
-        L.rows += L.pop.core + [send(row, to_core) for row in L.rows[3:]]
+        L.rows += [send(row, to_core) for row in L.rows]
         L = fence(L)
 
         L.down_zh.append(over_zh(L.for_down[1]))
-        L.down_y = [send(L.down, from_y[k]) for k in far_y]
-        L.down_zh_y = relay(L.down_zh[:1])
-        zh_blocks = [part[h] for h in range(ZH - 1) for part in L.zh]
+        L.down_y.append([send(L.for_down[1], from_y[k]) for k in far_y])
+        L.down_zh_y = [relay(L.down_zh[0])]
+        zh_blocks = [part[h] for h in range(ZH - 1) for part in (L.zh0, L.zh1, L.zh2, L.zh3)]
         sets = [([L.near, L.far, *zh_blocks], L.b, L.a_down)]
         for k in range(Y - 1):
-            relayed = [part[k][h] for h in range(ZH - 1) for part in L.zh_y]
+            relayed = [part[k][h] for h in range(ZH - 1) for part in (L.relay0, L.relay1, L.relay2, L.relay3)]
             sets.append(([L.y[0][k], L.y[1][k], *relayed], L.b_far[k], L.a_far[k]))
         L.hidden = gated(
-            L.rows, L.adapters, L.pop.a_gate, L.pop.a_up, sets, L.ints.gated
+            L.rows, L.adapters, L.pop.a_gate, L.pop.a_up, sets, L.ints.gated,
+            rows_unit,
         )
-        L.drop.near.far.for_zh.zh.b.a_down.zh_y.y.b_far.a_far.rows
-        L = fence(L)
-
-        L.down_zh_y += relay(L.down_zh[1:])
-        down_sets = [[[L.down]] + [[w] for w in L.down_y]]
+        L.drop.near.far.near_parts.far_parts.zh0.zh1.zh2.zh3.relay0.relay1.relay2.relay3
+        L.drop.b.a_down.y.b_far.a_far.rows
+        L = fence(L)
+
+        L.down_zh_y.append(relay(L.down_zh[1]))
+        down_sets = [[L.for_down] + [[part[k] for part in L.down_y] for k in range(Y - 1)]]
         for h in range(ZH - 1):
             far = [[part[k][h] for part in L.down_zh_y] for k in range(Y - 1)]
             down_sets.append([[part[h] for part in L.down_zh]] + far)
 
         def down_of(h, which, came=None):
             return project_down(
-                L.hidden, L.b_down, down_sets[h], quarter, L.ints.span[h], which, came
+                L.hidden, L.b_down, down_sets[h], quarter, L.ints.down[h], which, came
             )
 
         came = [send(down_of(h, 1), to_core) for h in range(ZH)]

time: 434 us -> 408 us (0.940); the launches traced: 433 us -> 401 us
  waiting for transfers between devices: 189 us -> 157 us
  Pallas kernels: 142 us -> 137 us
    ppermute x66, waiting for transfers between devices: 185 us -> 157 us  [send(): return lax.ppermute(value, AXES, pairs)]
    pallas_call x1, Pallas kernels: 31.5 us -> 36.3 us  [gated(): pl.pallas_call(kernel, in_specs=[SMEM_SPEC] + [VMEM_SPEC] * 3 + [HBM_SPEC...]
    pallas_call x5 -> x4, Pallas kernels: 30.2 us -> 26.1 us  [project_down(): pl.pallas_call(kernel, in_specs=[SMEM_SPEC, HBM_SPEC] + [VMEM_SPEC] * len...]
    pallas_call x4 -> x3, Pallas kernels: 18.6 us -> 15.5 us  [project_out(): pl.pallas_call(kernel, in_specs=[SMEM_SPEC, SMEM_SPEC] + [VMEM_SPEC] * (4...]
  transfers between devices with their start and end apart: 68 -> 67, of which waited for: 28 -> 28; matrix products, arithmetic and copies ran while one was open for 2% -> 5% of each run, Pallas kernels for 29% -> 32%
where the time goes in v5:
time: 408 us; the launch traced here: 401 us
  waiting for transfers between devices  157 us (38%)
  Pallas kernels  137 us (34%)
  starting transfers between devices  73.8 us (18%)
  local copies, waits for them, and re-layouts  26.3 us (6%)
  other arithmetic  4.47 us (1%)
    ppermute x66, waiting for transfers between devices, send(): return lax.ppermute(value, AXES, pairs)  157 us
    ppermute x66, starting transfers between devices, send(): return lax.ppermute(value, AXES, pairs)  70.6 us
    pallas_call x1, Pallas kernels, gated(): pl.pallas_call(kernel, in_specs=[SMEM_SPEC] + [VMEM_SPEC] * 3 + [HBM_SPEC...  36.3 us
    pallas_call x4, Pallas kernels, project_down(): pl.pallas_call(kernel, in_specs=[SMEM_SPEC, HBM_SPEC] + [VMEM_SPEC] * len...  26.1 us
    pallas_call x1, Pallas kernels, project_qkv(): pl.pallas_call(kernel, in_specs=[SMEM_SPEC] + [VMEM_SPEC] * 4 + [HBM_SPEC...  18.6 us
    pallas_call x3, Pallas kernels, project_out(): pl.pallas_call(kernel, in_specs=[SMEM_SPEC, SMEM_SPEC] + [VMEM_SPEC] * (4...  15.5 us
    unnamed x149, local copies, waits for them, and re-layouts  9.46 us
    pallas_call x1, Pallas kernels, attend(): pl.pallas_call(kernel, grid=(indices, heads), in_specs=[pl.BlockSpec((slo...  8.42 us
  transfers between devices with their start and end apart: 67, of which 28 were waited for; matrix products, arithmetic and copies ran while one was open for 5% of the time, Pallas kernels for 32%

profile of v5, /device:TPU:0, one launch (start us, length us, event | category | flops | bytes accessed | tf_op | source)
XLA Modules:
  0.0 400.6 jit_solution(518631040499278229)
XLA Ops:
  2.5 5.0 %collective-permute-start.2 = (bf16[256,768]{1,0:T(8,128)(2,1)}, bf16[256,768]{1,0:T(8,128)(2,1)}, u32[]{:S(2)}, u32[]{:S(2)}) collective-permute-start(bf16[256,768]{1,0:T(8,128)(2,1)} %copy.34), channel_id=1, source_target_pairs={{0,24},{1,25},{2,26},{3,27},{4,28},{5,29},{6,30},{7,31},{8,0},{9,1... | collective-permute-start | bytes 1179656 | tf_op jit(solution)/shard_map/ppermute | solution.py:677
  21.6 5.3 %norm_rows.1 = (bf16[768,2048]{1,0:T(8,128)(2,1)}, bf16[192,2048]{1,0:T(8,128)(2,1)}) custom-call(s32[1]{0:T(128)} %bitcast.30.row_ref, bf16[768,2048]{1,0:T(8,128)(2,1)} %tok_ref.2), custom_call_target="tpu_custom_call" | custom-call | flops 1000 | bytes 1000 | tf_op jit(solution)/shard_map/norm_rows/pallas_call | solution.py:68
  41.0 8.0 %collective-permute-done.4.refs_25_ = bf16[512,256]{1,0:T(8,128)(2,1)S(1)} collective-permute-done((bf16[512,256]{1,0:T(8,128)(2,1)S(1)}, bf16[512,256]{1,0:T(8,128)(2,1)S(1)}, u32[]{:S(2)}, u32[]{:S(2)}) %collective-permute-start.4) | collective-permute-done | bytes 262176 | tf_op jit(solution)/shard_map/ppermute | solution.py:677
  60.1 11.5 %collective-permute-done.10.refs_1_ = bf16[256,512]{1,0:T(8,128)(2,1)S(1)} collective-permute-done((bf16[256,512]{1,0:T(8,128)(2,1)S(1)}, bf16[256,512]{1,0:T(8,128)(2,1)S(1)}, u32[]{:S(2)}, u32[]{:S(2)}) %collective-permute-start.10) | collective-permute-done | bytes 262176 | tf_op jit(solution)/shard_map/ppermute | solution.py:677
  73.9 7.8 %tables.1 = (s32[2,768,1]{2,1,0:T(8,128)}, s32[2,1,768]{2,1,0:T(1,128)}, s32[1536,1]{1,0:T(8,128)}, f32[1536,128]{1,0:T(8,128)}, f32[1536,128]{1,0:T(8,128)}, /*index=5*/s32[1536,1]{1,0:T(8,128)}) custom-call(s32[4,8]{1,0:T(4,128)} %get-tuple-element.1006.len_ref, s32[4,8]{1,0:T(4,128)} %get-tuple-element.1005.ad_ref, s32[4]{0:T(128)} %get-tuple-element.571.at_ref), custom_call_target="tpu_custom_call" | custom-call | flops 1000 | bytes 1000 | tf_op jit(solution)/shard_map/tables/pallas_call | solution.py:184
  99.8 18.6 %project_qkv.1.q.k.v = bf16[1536,768]{1,0:T(8,128)(2,1)} custom-call(s32[13]{0:T(128)} %stack.218.at_ref, s32[1536,1]{1,0:T(8,128)} %get-tuple-element.756.adapter_ref, bf16[2048,256]{1,0:T(8,128)(2,1)} %a_ref, f32[1536,128]{1,0:T(8,128)} %get-tuple-element.671.cos_ref, f32[1536,128]{1,0:T(8,128)} %get-tuple-element.672.sin_ref, ...), custom_call_target="tpu_custom_call" | custom-call | flops 1000 | bytes 1000 | tf_op jit(solution)/shard_map/project_qkv/pallas_call | solution.py:280
  128.3 8.4 %attend.1.attn_ref = bf16[1536,256]{1,0:T(8,128)(2,1)} custom-call(bf16[1536,768]{1,0:T(8,128)(2,1)} %project_qkv.1.q.k.v, bf16[1536,768]{1,0:T(8,128)(2,1)} %project_qkv.1.q.k.v, bf16[1536,768]{1,0:T(8,128)(2,1)} %project_qkv.1.q.k.v, s32[2,768,1]{2,1,0:T(8,128)} %get-tuple-element.703.column_ref, s32[2,1,768]{2,1,0:T(1,128)} %get-tuple-element.704.line_ref), custom_call_target="tpu_custom_call" | custom-call | flops 1000 | bytes 1000 | tf_op jit(solution)/shard_map/attend/pallas_call | solution.py:319
  141.0 4.4 %project_out.4 = bf16[768,1024]{1,0:T(8,128)(2,1)} custom-call(s32[4]{0:T(128)} %get-tuple-element.720.order_ref, s32[3]{0:T(128)} %get-tuple-element.719.at_ref, bf16[1536,256]{1,0:T(8,128)(2,1)} %attend.1.attn_ref, s32[1536,1]{1,0:T(8,128)} %get-tuple-element.756.adapter_ref, bf16[512,256]{1,0:T(8,128)(2,1)} %a_ref.3, bf16[256,2048]{1,0:T(8,128)(2,1)} %b_ref.2, ...), custom_call_target="tpu_custom_call" | custom-call | flops 1000 | bytes 1000 | tf_op jit(solution)/shard_map/project_out/pallas_call | solution.py:379
  156.3 6.7 %project_out.5 = (bf16[192,2048]{1,0:T(8,128)(2,1)}, bf16[192,2048]{1,0:T(8,128)(2,1)}, bf16[192,2048]{1,0:T(8,128)(2,1)}, bf16[192,2048]{1,0:T(8,128)(2,1)}) custom-call(s32[8]{0:T(128)} %stack.212.order_ref, s32[3]{0:T(128)} %get-tuple-element.751.x_ref.at_ref, bf16[1536,256]{1,0:T(8,128)(2,1)} %attend.1.attn_ref, ...), custom_call_target="tpu_custom_call" | custom-call | flops 1000 | bytes 1000 | tf_op jit(solution)/shard_map/project_out/pallas_call | solution.py:379
  169.3 16.3 %collective-permute-done.29.refs_1_ = bf16[192,2048]{1,0:T(8,128)(2,1)S(1)} collective-permute-done((bf16[192,2048]{1,0:T(8,128)(2,1)}, bf16[192,2048]{1,0:T(8,128)(2,1)S(1)}, u32[]{:S(2)}, u32[]{:S(2)}) %collective-permute-start.29) | collective-permute-done | bytes 786464 | tf_op jit(solution)/shard_map/ppermute | solution.py:677
  187.9 15.7 %collective-permute-done.31.refs_3_ = bf16[192,2048]{1,0:T(8,128)(2,1)S(1)} collective-permute-done((bf16[192,2048]{1,0:T(8,128)(2,1)}, bf16[192,2048]{1,0:T(8,128)(2,1)S(1)}, u32[]{:S(2)}, u32[]{:S(2)}) %collective-permute-start.31) | collective-permute-done | bytes 786464 | tf_op jit(solution)/shard_map/ppermute | solution.py:677
  205.0 5.0 %residual_norm.1 = (f32[192,2048]{1,0:T(8,128)}, bf16[192,2048]{1,0:T(8,128)(2,1)}) custom-call(s32[1]{0:T(128)} %bitcast.30.row_ref, s32[4]{0:T(128)} %get-tuple-element.817.order_ref, bf16[768,2048]{1,0:T(8,128)(2,1)} %tok_ref.2, bf16[192,2048]{1,0:T(8,128)(2,1)} %get-tuple-element.819.refs_0_, bf16[192,2048]{1,0:T(8,128)(2,1)} %copy-done.36, ...), custom_call_target="tpu_custom_call" | custom-call | flops 1000 | bytes 1000 | tf_op jit(solution)/shard_map/residual_norm/pallas_call | solution.py:410
  216.3 13.4 %collective-permute-done.33.refs_1_ = bf16[192,2048]{1,0:T(8,128)(2,1)S(1)} collective-permute-done((bf16[192,2048]{1,0:T(8,128)(2,1)}, bf16[192,2048]{1,0:T(8,128)(2,1)S(1)}, u32[]{:S(2)}, u32[]{:S(2)}) %collective-permute-start.33) | collective-permute-done | bytes 786464 | tf_op jit(solution)/shard_map/ppermute | solution.py:677
  229.7 12.2 %collective-permute-done.34.refs_2_ = bf16[192,2048]{1,0:T(8,128)(2,1)S(1)} collective-permute-done((bf16[192,2048]{1,0:T(8,128)(2,1)}, bf16[192,2048]{1,0:T(8,128)(2,1)S(1)}, u32[]{:S(2)}, u32[]{:S(2)}) %collective-permute-start.34) | collective-permute-done | bytes 786464 | tf_op jit(solution)/shard_map/ppermute | solution.py:677
  247.8 14.4 %collective-permute-done.40.refs_20_ = bf16[128,1024]{1,0:T(8,128)(2,1)S(1)} collective-permute-done((bf16[128,1024]{1,0:T(8,128)(2,1)S(1)}, bf16[128,1024]{1,0:T(8,128)(2,1)S(1)}, u32[]{:S(2)}, u32[]{:S(2)}) %collective-permute-start.40) | collective-permute-done | bytes 262176 | tf_op jit(solution)/shard_map/ppermute | solution.py:677
  275.6 36.3 %gated.1.h_in = bf16[1536,1280]{1,0:T(8,128)(2,1)} custom-call(s32[12]{0:T(128)} %stack.201.place_ref, s32[1536,1]{1,0:T(8,128)} %get-tuple-element.931.adapter_ref, bf16[2048,256]{1,0:T(8,128)(2,1)} %ag_ref, bf16[2048,256]{1,0:T(8,128)(2,1)} %au_ref, bf16[192,2048]{1,0:T(8,128)(2,1)} %get-tuple-element.940.refs_0_, bf16[192,2048]{1,0:T(8,128)(2,1)} %copy-done.12, ...), custom_call_target="tpu_custom_call" | custom-call | flops 1000 | bytes 1000 | tf_op jit(solution)/shard_map/gated/pallas_call | solution.py:507
  313.4 6.3 %project_down.4 = bf16[768,1024]{1,0:T(8,128)(2,1)} custom-call(s32[2]{0:T(128)} %get-tuple-element.973.at_ref, bf16[1536,1280]{1,0:T(8,128)(2,1)} %gated.1.h_in, bf16[256,2048]{1,0:T(8,128)(2,1)} %refs_1_.1, bf16[1024,256]{1,0:T(8,128)(2,1)} %copy-done, bf16[1024,256]{1,0:T(8,128)(2,1)} %copy-done.4, bf16[1024,256]{1,0:T(8,128)(2,1)} %copy-done.5, ...), custom_call_target="tpu_custom_call" | custom-call | flops 1000 | bytes 1000 | tf_op jit(solution)/shard_map/project_down/pallas_call | solution.py:590
  319.8 5.6 %collective-permute-done.58.refs_4_.refs_5_ = bf16[1024,256]{1,0:T(8,128)(2,1)S(1)} collective-permute-done((bf16[1024,256]{1,0:T(8,128)(2,1)S(1)}, bf16[1024,256]{1,0:T(8,128)(2,1)S(1)}, u32[]{:S(2)}, u32[]{:S(2)}) %collective-permute-start.58) | collective-permute-done | bytes 524320 | tf_op jit(solution)/shard_map/ppermute | solution.py:677
  326.3 6.4 %project_down.6 = bf16[768,1024]{1,0:T(8,128)(2,1)} custom-call(s32[2]{0:T(128)} %get-tuple-element.985.at_ref, bf16[1536,1280]{1,0:T(8,128)(2,1)} %gated.1.h_in, bf16[256,2048]{1,0:T(8,128)(2,1)} %refs_1_.1, bf16[1024,256]{1,0:T(8,128)(2,1)} %copy-done.6, bf16[1024,256]{1,0:T(8,128)(2,1)} %copy-done.7, bf16[1024,256]{1,0:T(8,128)(2,1)} %copy-done.8, ...), custom_call_target="tpu_custom_call" | custom-call | flops 1000 | bytes 1000 | tf_op jit(solution)/shard_map/project_down/pallas_call | solution.py:590
  334.0 6.6 %project_down.5 = (bf16[192,1024]{1,0:T(8,128)(2,1)}, bf16[192,1024]{1,0:T(8,128)(2,1)}, bf16[192,1024]{1,0:T(8,128)(2,1)}, bf16[192,1024]{1,0:T(8,128)(2,1)}) custom-call(s32[2]{0:T(128)} %get-tuple-element.973.at_ref, bf16[1536,1280]{1,0:T(8,128)(2,1)} %gated.1.h_in, bf16[768,1024]{1,0:T(8,128)(2,1)} %copy-done.20, bf16[256,2048]{1,0:T(8,128)(2,1)} %refs_1_.1, ...), custom_call_target="tpu_custom_call" | custom-call | flops 1000 | bytes 1000 | tf_op jit(solution)/shard_map/project_down/pallas_call | solution.py:590
  346.0 6.7 %project_down.7 = (bf16[192,1024]{1,0:T(8,128)(2,1)}, bf16[192,1024]{1,0:T(8,128)(2,1)}, bf16[192,1024]{1,0:T(8,128)(2,1)}, bf16[192,1024]{1,0:T(8,128)(2,1)}) custom-call(s32[2]{0:T(128)} %get-tuple-element.985.at_ref, bf16[1536,1280]{1,0:T(8,128)(2,1)} %gated.1.h_in, bf16[768,1024]{1,0:T(8,128)(2,1)} %copy-done.18, bf16[256,2048]{1,0:T(8,128)(2,1)} %refs_1_.1, ...), custom_call_target="tpu_custom_call" | custom-call | flops 1000 | bytes 1000 | tf_op jit(solution)/shard_map/project_down/pallas_call | solution.py:590
  356.3 7.0 %collective-permute-done.54.refs_3_ = bf16[192,1024]{1,0:T(8,128)(2,1)S(1)} collective-permute-done((bf16[192,1024]{1,0:T(8,128)(2,1)}, bf16[192,1024]{1,0:T(8,128)(2,1)S(1)}, u32[]{:S(2)}, u32[]{:S(2)}) %collective-permute-start.54) | collective-permute-done | bytes 393248 | tf_op jit(solution)/shard_map/ppermute | solution.py:677
  371.7 8.1 %collective-permute-done.62.refs_3_ = bf16[192,1024]{1,0:T(8,128)(2,1)S(1)} collective-permute-done((bf16[192,1024]{1,0:T(8,128)(2,1)}, bf16[192,1024]{1,0:T(8,128)(2,1)S(1)}, u32[]{:S(2)}, u32[]{:S(2)}) %collective-permute-start.62) | collective-permute-done | bytes 393248 | tf_op jit(solution)/shard_map/ppermute | solution.py:677
  385.2 9.0 %collective-permute-done.64.refs_6_ = bf16[192,1024]{1,0:T(8,128)(2,1)S(1)} collective-permute-done((bf16[192,1024]{1,0:T(8,128)(2,1)}, bf16[192,1024]{1,0:T(8,128)(2,1)S(1)}, u32[]{:S(2)}, u32[]{:S(2)}) %collective-permute-start.64) | collective-permute-done | bytes 393248 | tf_op jit(solution)/shard_map/ppermute | solution.py:677
  (309 shorter events, 154.4 us)
Async XLA Ops:
  2.5 26.8 %collective-permute-start.2 = (bf16[256,768]{1,0:T(8,128)(2,1)}, bf16[256,768]{1,0:T(8,128)(2,1)}, u32[]{:S(2)}, u32[]{:S(2)}) collective-permute-start(bf16[256,768]{1,0:T(8,128)(2,1)} %copy.34), channel_id=1, source_target_pairs={{0,24},{1,25},{2,26},{3,27},{4,28},{5,29},{6,30},{7,31},{8,0},{9,1... | collective-permute-start | bytes 1179656 | tf_op jit(solution)/shard_map/ppermute | solution.py:677
  29.3 23.4 %collective-permute-start.6 = (bf16[192,2048]{1,0:T(8,128)(2,1)}, bf16[192,2048]{1,0:T(8,128)(2,1)S(1)}, u32[]{:S(2)}, u32[]{:S(2)}) collective-permute-start(bf16[192,2048]{1,0:T(8,128)(2,1)} %get-tuple-element.536), channel_id=1, source_target_pairs={{0,4},{1,5},{2,6},{3,7},{4,0},{5,1},{6,2},{7,3},{8,12},{9,13},{10,... | collective-permute-start | bytes 2359304 | tf_op jit(solution)/shard_map/ppermute | solution.py:677
  53.7 29.8 %collective-permute-start.9 = (bf16[2,256,1024]{2,1,0:T(8,128)(2,1)}, bf16[2,256,1024]{2,1,0:T(8,128)(2,1)S(1)}, u32[]{:S(2)}, u32[]{:S(2)}) collective-permute-start(bf16[2,256,1024]{2,1,0:T(8,128)(2,1)} %get-tuple-element.557), channel_id=1, source_target_pairs={{0,4},{1,5},{2,6},{3,7},{4,0},{5,1},{6,2},{7,3},{8,12},{9,13},{10,... | collective-permute-start | bytes 3145736 | tf_op jit(solution)/shard_map/ppermute | solution.py:677
  54.1 29.4 %collective-permute-start.12 = (bf16[192,2048]{1,0:T(8,128)(2,1)S(1)}, bf16[192,2048]{1,0:T(8,128)(2,1)S(1)}, u32[]{:S(2)}, u32[]{:S(2)}) collective-permute-start(bf16[192,2048]{1,0:T(8,128)(2,1)S(1)} %collective-permute-done.6.refs_0_), channel_id=1, source_target_pairs={{0,2},{1,3},{2,0},{3,1},{4,6},{5,7},{6,4},{7,5},{8,10},{9,11},{10,... | collective-permute-start | bytes 2359304 | tf_op jit(solution)/shard_map/ppermute | solution.py:677
  56.3 27.2 %collective-permute-start.13 = (bf16[256,768]{1,0:T(8,128)(2,1)}, bf16[256,768]{1,0:T(8,128)(2,1)S(1)}, u32[]{:S(2)}, u32[]{:S(2)}) collective-permute-start(bf16[256,768]{1,0:T(8,128)(2,1)} %collective-permute-done.3.refs_10_), channel_id=1, source_target_pairs={{0,8},{1,9},{2,10},{3,11},{4,12},{5,13},{6,14},{7,15},{8,16},{9,17... | collective-permute-start | bytes 1179656 | tf_op jit(solution)/shard_map/ppermute | solution.py:677
  56.6 26.9 %collective-permute-start.14 = (bf16[256,768]{1,0:T(8,128)(2,1)S(1)}, bf16[256,768]{1,0:T(8,128)(2,1)S(1)}, u32[]{:S(2)}, u32[]{:S(2)}) collective-permute-start(bf16[256,768]{1,0:T(8,128)(2,1)S(1)} %collective-permute-done.7.refs_7_), channel_id=1, source_target_pairs={{0,24},{1,25},{2,26},{3,27},{4,28},{5,29},{6,30},{7,31},{8,0},{9,1... | collective-permute-start | bytes 1179656 | tf_op jit(solution)/shard_map/ppermute | solution.py:677
  89.1 31.0 %collective-permute-start.18 = (bf16[512,1024]{1,0:T(8,128)(2,1)}, bf16[512,1024]{1,0:T(8,128)(2,1)S(1)}, u32[]{:S(2)}, u32[]{:S(2)}) collective-permute-start(bf16[512,1024]{1,0:T(8,128)(2,1)} %get-tuple-element.653), channel_id=1, source_target_pairs={{0,8},{1,9},{2,10},{3,11},{4,12},{5,13},{6,14},{7,15},{8,0},{9,1},... | collective-permute-start | bytes 3145736 | tf_op jit(solution)/shard_map/ppermute | solution.py:677
  90.6 30.4 %collective-permute-start.21 = (bf16[512,1024]{1,0:T(8,128)(2,1)}, bf16[512,1024]{1,0:T(8,128)(2,1)}, u32[]{:S(2)}, u32[]{:S(2)}) collective-permute-start(bf16[512,1024]{1,0:T(8,128)(2,1)} %get-tuple-element.950.refs_10_), channel_id=1, source_target_pairs={{0,2},{1,3},{2,0},{3,1},{4,6},{5,7},{6,4},{7,5},{8,10},{9,11},{10,... | collective-permute-start | bytes 3145736 | tf_op jit(solution)/shard_map/ppermute | solution.py:677
  92.1 28.0 %collective-permute-start.17 = (bf16[1024,256]{1,0:T(8,128)(2,1)}, bf16[1024,256]{1,0:T(8,128)(2,1)S(1)}, u32[]{:S(2)}, u32[]{:S(2)}) collective-permute-start(bf16[1024,256]{1,0:T(8,128)(2,1)} %pad_maximum_fusion.1), channel_id=1, source_target_pairs={{0,4},{1,5},{2,6},{3,7},{4,0},{5,1},{6,2},{7,3},{8,12},{9,13},{10,... | collective-permute-start | bytes 1572872 | tf_op jit(solution)/shard_map/ppermute | solution.py:677
  93.9 24.8 %collective-permute-start.19 = (bf16[256,256]{1,0:T(8,128)(2,1)}, bf16[256,256]{1,0:T(8,128)(2,1)S(1)}, u32[]{:S(2)}, u32[]{:S(2)}) collective-permute-start(bf16[256,256]{1,0:T(8,128)(2,1)} %slice.38), channel_id=1, source_target_pairs={{0,8},{1,9},{2,10},{3,11},{4,12},{5,13},{6,14},{7,15},{8,16},{9,17... | collective-permute-start | bytes 393224 | tf_op jit(solution)/shard_map/ppermute | solution.py:677
  94.6 25.5 %collective-permute-start.20 = (bf16[256,256]{1,0:T(8,128)(2,1)}, bf16[256,256]{1,0:T(8,128)(2,1)}, u32[]{:S(2)}, u32[]{:S(2)}) collective-permute-start(bf16[256,256]{1,0:T(8,128)(2,1)} %slice.39), channel_id=1, source_target_pairs={{0,24},{1,25},{2,26},{3,27},{4,28},{5,29},{6,30},{7,31},{8,0},{9,1... | collective-permute-start | bytes 393224 | tf_op jit(solution)/shard_map/ppermute | solution.py:677
  120.9 29.2 %collective-permute-start.23 = (bf16[512,1024]{1,0:T(8,128)(2,1)S(1)}, bf16[512,1024]{1,0:T(8,128)(2,1)S(1)}, u32[]{:S(2)}, u32[]{:S(2)}) collective-permute-start(bf16[512,1024]{1,0:T(8,128)(2,1)S(1)} %collective-permute-done.18.refs_11_), channel_id=1, source_target_pairs={{0,2},{1,3},{2,0},{3,1},{4,6},{5,7},{6,4},{7,5},{8,10},{9,11},{10,... | collective-permute-start | bytes 3145736 | tf_op jit(solution)/shard_map/ppermute | solution.py:677
  124.6 25.6 %collective-permute-start.24 = (bf16[256,1024]{1,0:T(8,128)(2,1)S(1)}, bf16[256,1024]{1,0:T(8,128)(2,1)S(1)}, u32[]{:S(2)}, u32[]{:S(2)}) collective-permute-start(bf16[256,1024]{1,0:T(8,128)(2,1)S(1)} %get-tuple-element.994), channel_id=1, source_target_pairs={{0,16},{1,17},{2,18},{3,19},{4,20},{5,21},{6,22},{7,23},{8,24},{9,... | collective-permute-start | bytes 1572872 | tf_op jit(solution)/shard_map/ppermute | solution.py:677
  169.0 34.6 %collective-permute-start.31 = (bf16[192,2048]{1,0:T(8,128)(2,1)}, bf16[192,2048]{1,0:T(8,128)(2,1)S(1)}, u32[]{:S(2)}, u32[]{:S(2)}) collective-permute-start(bf16[192,2048]{1,0:T(8,128)(2,1)} %get-tuple-element.799), channel_id=1, source_target_pairs={{0,6},{1,7},{2,4},{3,5},{4,2},{5,3},{6,0},{7,1},{8,14},{9,15},{10,... | collective-permute-start | bytes 2359304 | tf_op jit(solution)/shard_map/ppermute | solution.py:677
  169.3 35.6 %collective-permute-start.32 = (bf16[384,1024]{1,0:T(8,128)(2,1)S(1)}, bf16[384,1024]{1,0:T(8,128)(2,1)S(1)}, u32[]{:S(2)}, u32[]{:S(2)}) collective-permute-start(bf16[384,1024]{1,0:T(8,128)(2,1)S(1)} %copy-done.35), channel_id=1, source_target_pairs={{0,16},{1,17},{2,18},{3,19},{4,20},{5,21},{6,22},{7,23},{8,24},{9,... | collective-permute-start | bytes 2359304 | tf_op jit(solution)/shard_map/ppermute | solution.py:677
  211.3 30.6 %collective-permute-start.34 = (bf16[192,2048]{1,0:T(8,128)(2,1)}, bf16[192,2048]{1,0:T(8,128)(2,1)S(1)}, u32[]{:S(2)}, u32[]{:S(2)}) collective-permute-start(bf16[192,2048]{1,0:T(8,128)(2,1)} %get-tuple-element.940.refs_0_), channel_id=1, source_target_pairs={{0,8},{1,9},{2,10},{3,11},{4,12},{5,13},{6,14},{7,15},{8,0},{9,1},... | collective-permute-start | bytes 2359304 | tf_op jit(solution)/shard_map/ppermute | solution.py:677
  211.3 30.7 %collective-permute-start.36 = (bf16[384,1024]{1,0:T(8,128)(2,1)S(1)}, bf16[384,1024]{1,0:T(8,128)(2,1)S(1)}, u32[]{:S(2)}, u32[]{:S(2)}) collective-permute-start(bf16[384,1024]{1,0:T(8,128)(2,1)S(1)} %collective-permute-done.32.refs_15_), channel_id=1, source_target_pairs={{0,2},{1,3},{2,0},{3,1},{4,6},{5,7},{6,4},{7,5},{8,10},{9,11},{10,... | collective-permute-start | bytes 2359304 | tf_op jit(solution)/shard_map/ppermute | solution.py:677
  212.7 29.3 %collective-permute-start.35 = (bf16[1024,256]{1,0:T(8,128)(2,1)S(1)}, bf16[1024,256]{1,0:T(8,128)(2,1)S(1)}, u32[]{:S(2)}, u32[]{:S(2)}) collective-permute-start(bf16[1024,256]{1,0:T(8,128)(2,1)S(1)} %pad_maximum_fusion.3.refs_1_.refs_2_), channel_id=1, source_target_pairs={{0,2},{1,3},{2,0},{3,1},{4,6},{5,7},{6,4},{7,5},{8,10},{9,11},{10,... | collective-permute-start | bytes 1572872 | tf_op jit(solution)/shard_map/ppermute | solution.py:677
  213.3 28.6 %collective-permute-start.37 = (bf16[256,1024]{1,0:T(8,128)(2,1)S(1)}, bf16[256,1024]{1,0:T(8,128)(2,1)S(1)}, u32[]{:S(2)}, u32[]{:S(2)}) collective-permute-start(bf16[256,1024]{1,0:T(8,128)(2,1)S(1)} %copy-done.45), channel_id=1, source_target_pairs={{0,16},{1,17},{2,18},{3,19},{4,20},{5,21},{6,22},{7,23},{8,24},{9,... | collective-permute-start | bytes 1572872 | tf_op jit(solution)/shard_map/ppermute | solution.py:677
  242.0 24.9 %collective-permute-start.38 = (bf16[1024,256]{1,0:T(8,128)(2,1)S(1)}, bf16[1024,256]{1,0:T(8,128)(2,1)S(1)}, u32[]{:S(2)}, u32[]{:S(2)}) collective-permute-start(bf16[1024,256]{1,0:T(8,128)(2,1)S(1)} %pad_maximum_fusion.3.refs_1_.refs_2_), channel_id=1, source_target_pairs={{0,16},{1,17},{2,18},{3,19},{4,20},{5,21},{6,22},{7,23},{8,24},{9,... | collective-permute-start | bytes 1572872 | tf_op jit(solution)/shard_map/ppermute | solution.py:677
  273.4 38.5 %collective-permute-start.48 = (bf16[1024,256]{1,0:T(8,128)(2,1)S(1)}, bf16[1024,256]{1,0:T(8,128)(2,1)S(1)}, u32[]{:S(2)}, u32[]{:S(2)}) collective-permute-start(bf16[1024,256]{1,0:T(8,128)(2,1)S(1)} %collective-permute-done.22.refs_2_.refs_3_), channel_id=1, source_target_pairs={{0,2},{1,3},{2,0},{3,1},{4,6},{5,7},{6,4},{7,5},{8,10},{9,11},{10,... | collective-permute-start | bytes 1572872 | tf_op jit(solution)/shard_map/ppermute | solution.py:677
  274.8 37.2 %collective-permute-start.49 = (bf16[1024,256]{1,0:T(8,128)(2,1)S(1)}, bf16[1024,256]{1,0:T(8,128)(2,1)S(1)}, u32[]{:S(2)}, u32[]{:S(2)}) collective-permute-start(bf16[1024,256]{1,0:T(8,128)(2,1)S(1)} %collective-permute-done.22.refs_2_.refs_3_), channel_id=1, source_target_pairs={{0,16},{1,17},{2,18},{3,19},{4,20},{5,21},{6,22},{7,23},{8,24},{9,... | collective-permute-start | bytes 1572872 | tf_op jit(solution)/shard_map/ppermute | solution.py:677
  274.8 37.1 %collective-permute-start.50 = (bf16[1024,256]{1,0:T(8,128)(2,1)S(1)}, bf16[1024,256]{1,0:T(8,128)(2,1)S(1)}, u32[]{:S(2)}, u32[]{:S(2)}) collective-permute-start(bf16[1024,256]{1,0:T(8,128)(2,1)S(1)} %collective-permute-done.38.refs_1_.refs_2_), channel_id=1, source_target_pairs={{0,2},{1,3},{2,0},{3,1},{4,6},{5,7},{6,4},{7,5},{8,10},{9,11},{10,... | collective-permute-start | bytes 1572872 | tf_op jit(solution)/shard_map/ppermute | solution.py:677
  355.5 24.3 %collective-permute-start.62 = (bf16[192,1024]{1,0:T(8,128)(2,1)}, bf16[192,1024]{1,0:T(8,128)(2,1)S(1)}, u32[]{:S(2)}, u32[]{:S(2)}) collective-permute-start(bf16[192,1024]{1,0:T(8,128)(2,1)} %get-tuple-element.992), channel_id=1, source_target_pairs={{0,12},{1,13},{2,14},{3,15},{4,8},{5,9},{6,10},{7,11},{8,4},{9,5},... | collective-permute-start | bytes 1179656 | tf_op jit(solution)/shard_map/ppermute | solution.py:677
  (116 other events, 1882.9 us)
